TPU v7x, 512 devices: a whole 4x8x8 slice. The times are simulated.
512 devices in a mesh: cuts: 16 (over z_lo, y), space: 32 (over x, z_hi, core).
Axes of the slice: x: 4, y: 8, z: 8 (z_hi: 4, z_lo: 2; z = z_hi * 2 + z_lo), core: 2. Of those that a mesh axis runs over, the one named last changes fastest.
Arguments:
- starts: float32 [16, 3, 128, 64, 128], P('cuts', None, 'space'), may hold values from -3 to 3
Outputs:
- new_starts: float32 [16, 3, 128, 64, 128], P('cuts', None, 'space')
All inputs are finite; a program needn't handle non-finite values.
Results may differ from a plain program's by a relative error of at most 0.0001.
Values sent between devices are 32-bit elements; how exact they have to be, the bound alone decides.
No kernel may reach another device: no remote copies, remote signals or barrier semaphores. Data moves between devices by JAX's collectives and lax.ppermute only.
A program may use at most 64 MiB of HBM per device.

v0:
```python
import jax
import jax.numpy as jnp
from jax import lax
from jax.sharding import Mesh
from jax.sharding import PartitionSpec as P

FSTEPS = 16
CSTEPS = 2
CUTS = ("cuts_0", "cuts_1")


fine_rate = 0.08
fine_advect = 0.04
coarse_rate = 0.16
coarse_advect = 0.16


def padded_2(cells, sides, width):
    for axis, dim in sides:
        count = lax.axis_size(axis)
        ends = count - 1
        head = lax.slice_in_dim(cells, 0, width, axis=dim)
        tail = lax.slice_in_dim(cells, cells.shape[dim] - width, cells.shape[dim], axis=dim)
        cells = jnp.concatenate(
            [
                lax.ppermute(tail, axis, [(i, (i + 1) % count) for i in range(ends)]),
                cells,
                lax.ppermute(head, axis, [((i + 1) % count, i) for i in range(ends)]),
            ],
            axis=dim,
        )
    return cells


def passed_along(shard, axis, by):
    length = lax.axis_size(axis)
    pairs = [(i, i + by) for i in range(length) if 0 <= i + by < length]
    return lax.ppermute(shard, axis, pairs)


def sent_to_all(shard, axis):
    copies = jnp.broadcast_to(shard, (lax.axis_size(axis), *shard.shape))
    return lax.all_to_all(copies, axis, split_axis=0, concat_axis=0, tiled=True)


def joined_along(tiles, dim):
    shape = list(tiles.shape[1:])
    shape[dim] *= tiles.shape[0]
    return jnp.moveaxis(tiles, 0, dim).reshape(shape)


def gathered_copies(shard, axis, dim):
    tiles = sent_to_all(shard, axis)
    return joined_along(tiles, dim)


def broadcast_by_axis(shard, axes, root):
    shard = jnp.where(lax.axis_index(axes) == root, shard, jnp.zeros_like(shard))
    for axis in axes:
        shard = lax.psum(shard, axis)
    return shard


def advance(extended, rate, advect):
    padded = jnp.pad(extended, ((0, 0), (0, 0), (1, 1), (1, 1)))
    centre = padded[:, 1:-1, 1:-1, 1:-1]
    x_plus = padded[:, 2:, 1:-1, 1:-1]
    x_minus = padded[:, :-2, 1:-1, 1:-1]
    y_plus = padded[:, 1:-1, 2:, 1:-1]
    y_minus = padded[:, 1:-1, :-2, 1:-1]
    z_plus = padded[:, 1:-1, 1:-1, 2:]
    z_minus = padded[:, 1:-1, 1:-1, :-2]
    laplace = x_plus + x_minus + (y_plus + y_minus) + (z_plus + z_minus) - 6.0 * centre
    convect = (
        centre[0:1] * (x_plus - x_minus)
        + centre[1:2] * (y_plus - y_minus)
        + centre[2:3] * (z_plus - z_minus)
    )
    return centre + rate * laplace - advect * convect


def restrict(field):
    blocks = field.reshape(
        field.shape[0], field.shape[1] // 2, 2, field.shape[2] // 2, 2, field.shape[3] // 2, 2
    )
    return jnp.sum(blocks, axis=(2, 4, 6)) * 0.125


def prolong(field):
    return jnp.repeat(jnp.repeat(jnp.repeat(field, 2, axis=1), 2, axis=2), 2, axis=3)


def double_fine(index, field):
    width = field.shape[1]
    extended = padded_2(field, (("space", 1),), 2)
    first = advance(extended, fine_rate, fine_advect)
    global_rows = lax.axis_index("space") * width - 1 + jnp.arange(width + 2, dtype=jnp.int32)
    inside = (global_rows >= 0) & (global_rows < width * lax.axis_size("space"))
    first = jnp.where(inside[None, :, None, None], first, 0.0)
    return advance(first, fine_rate, fine_advect)


def fine_run(field):
    return lax.fori_loop(0, FSTEPS // 2, double_fine, field)


def coarse_single(index, field):
    extended = padded_2(field, (("space", 1),), 1)
    return advance(extended, coarse_rate, coarse_advect)


def coarse_run(field):
    return lax.fori_loop(0, CSTEPS, coarse_single, field)


def shards(starts):
    initial = starts[0]
    ends = fine_run(initial)
    coarse_start = restrict(initial)
    old_coarse = coarse_run(coarse_start)
    change = ends - prolong(old_coarse)
    previous = passed_along(change, CUTS, 1)
    previous_coarse = restrict(previous)
    position = lax.axis_index(CUTS)
    groups = lax.axis_size(CUTS)
    gathered = gathered_copies(previous_coarse[None], CUTS, 0)
    first_state = broadcast_by_axis(coarse_start, CUTS, 0)

    def local_turn(index, carry):
        current, stored = carry
        advanced = coarse_run(current)
        current = advanced + lax.dynamic_index_in_dim(gathered, index + 1, 0, keepdims=False)
        stored = jnp.where(position == index + 1, advanced, stored)
        return (current, stored)

    unused, stored = lax.fori_loop(
        0, groups - 1, local_turn, (first_state, jnp.zeros_like(coarse_start))
    )
    corrected = jnp.where(position == 0, initial, prolong(stored) + previous)
    return corrected[None]


def solution(mesh):
    torus = Mesh(mesh.devices.reshape(2, 8, mesh.shape["space"]), ("cuts_0", "cuts_1", "space"))
    placed = (P(CUTS, None, "space", None, None),)
    return jax.shard_map(
        shards,
        mesh=torus,
        in_specs=placed,
        out_specs=P(CUTS, None, "space", None, None),
        check_vma=False,
    )
```

profile of v0, /device:TPU:2, one launch (start us, length us, event | category | flops | bytes accessed | tf_op | source)
XLA Modules:
  0.0 620.3 jit_solution(11844629904105889778)
XLA Ops:
  0.0 27.2 %reshape_squeeze.3 = f32[3,2,2,32,2,64,2]{6,5,4,3,2,1,0:T(8,128)} reshape(f32[1,3,4,64,128]{4,3,2,1,0:T(8,128)} %param.9) | data formatting | bytes 786432 | tf_op jit(solution)/shard_map/reshape;squeeze | solution.py:83
  27.2 9.4 %reduce_sum.18 = f32[3,2,32,64]{3,2,1,0:T(8,128)S(1)} reduce(f32[3,2,2,32,2,64,2]{6,5,4,3,2,1,0:T(8,128)} %reshape_squeeze.3, f32[]{:T(128)} %constant.108.clone.1), dimensions={2,4,6}, to_apply=%region_0.1 | reduce | flops 86016 | bytes 442372 | tf_op jit(solution)/shard_map/reduce_sum | solution.py:86
  36.7 29.9 %while.71 = (s32[]{:T(128)}, f32[3,2,32,64]{3,2,1,0:T(8,128)S(1)}, s32[]{:T(128)}) while((s32[]{:T(128)}, f32[3,2,32,64]{3,2,1,0:T(8,128)S(1)}, s32[]{:T(128)}) %tuple.132), condition=%wide.region_6.7_spmd, body=%wide.region_5.6_spmd.sunk | while | flops 661970 | bytes 1090877 | solution.py:113
  36.7 10.3 %collective-permute-start.2 = (f32[3,1,32,64]{3,2,1,0:T(8,128)S(1)}, f32[3,1,32,64]{3,2,1,0:T(8,128)S(1)}, u32[]{:S(2)}, u32[]{:S(2)}) collective-permute-start(f32[3,1,32,64]{3,2,1,0:T(8,128)S(1)} %get-tuple-element.364), channel_id=1, source_target_pairs={{1,0},{2,1},{3,2},{4,3},{5,4},{6,5},{7,6},{8,7},{9,8},{10,9},{11,1... | collective-permute-start | bytes 73736 | tf_op jit(solution)/shard_map/while/body/eval_jaxpr/ppermute | solution.py:28
  67.8 108.3 %while.70 = (s32[]{:T(128)}, f32[3,4,64,128]{3,2,1,0:T(8,128)S(1)}, s32[]{:T(128)}, u32[]{:T(128)}, s32[]{:T(128)}, /*index=5*/s32[]{:T(128)}) while((s32[]{:T(128)}, f32[3,4,64,128]{3,2,1,0:T(8,128)S(1)}, s32[]{:T(128)}, u32[]{:T(128)}, s32[]{:T(128)}, /*index=5*/s32[]{:T(128)}) %tuple.129), condition=%wide.region_4.5_spmd, body=%wide.region_3.4_spmd.sunk | while | flops 4816926 | bytes 13370059 | solution.py:104
  99.4 6.8 %collective-permute-start.1 = (f32[3,2,64,128]{3,2,1,0:T(8,128)S(1)}, f32[3,2,64,128]{3,2,1,0:T(8,128)S(1)}, u32[]{:S(2)}, u32[]{:S(2)}) collective-permute-start(f32[3,2,64,128]{3,2,1,0:T(8,128)S(1)} %get-tuple-element.351), channel_id=1, source_target_pairs={{1,0},{2,1},{3,2},{4,3},{5,4},{6,5},{7,6},{8,7},{9,8},{10,9},{11,1... | collective-permute-start | bytes 589832 | tf_op jit(solution)/shard_map/while/body/eval_jaxpr/ppermute | solution.py:28
  112.8 6.8 %collective-permute-start.1 = (f32[3,2,64,128]{3,2,1,0:T(8,128)S(1)}, f32[3,2,64,128]{3,2,1,0:T(8,128)S(1)}, u32[]{:S(2)}, u32[]{:S(2)}) collective-permute-start(f32[3,2,64,128]{3,2,1,0:T(8,128)S(1)} %get-tuple-element.351), channel_id=1, source_target_pairs={{1,0},{2,1},{3,2},{4,3},{5,4},{6,5},{7,6},{8,7},{9,8},{10,9},{11,1... | collective-permute-start | bytes 589832 | tf_op jit(solution)/shard_map/while/body/eval_jaxpr/ppermute | solution.py:28
  125.9 6.8 %collective-permute-start.1 = (f32[3,2,64,128]{3,2,1,0:T(8,128)S(1)}, f32[3,2,64,128]{3,2,1,0:T(8,128)S(1)}, u32[]{:S(2)}, u32[]{:S(2)}) collective-permute-start(f32[3,2,64,128]{3,2,1,0:T(8,128)S(1)} %get-tuple-element.351), channel_id=1, source_target_pairs={{1,0},{2,1},{3,2},{4,3},{5,4},{6,5},{7,6},{8,7},{9,8},{10,9},{11,1... | collective-permute-start | bytes 589832 | tf_op jit(solution)/shard_map/while/body/eval_jaxpr/ppermute | solution.py:28
  139.0 6.8 %collective-permute-start.1 = (f32[3,2,64,128]{3,2,1,0:T(8,128)S(1)}, f32[3,2,64,128]{3,2,1,0:T(8,128)S(1)}, u32[]{:S(2)}, u32[]{:S(2)}) collective-permute-start(f32[3,2,64,128]{3,2,1,0:T(8,128)S(1)} %get-tuple-element.351), channel_id=1, source_target_pairs={{1,0},{2,1},{3,2},{4,3},{5,4},{6,5},{7,6},{8,7},{9,8},{10,9},{11,1... | collective-permute-start | bytes 589832 | tf_op jit(solution)/shard_map/while/body/eval_jaxpr/ppermute | solution.py:28
  152.0 6.8 %collective-permute-start.1 = (f32[3,2,64,128]{3,2,1,0:T(8,128)S(1)}, f32[3,2,64,128]{3,2,1,0:T(8,128)S(1)}, u32[]{:S(2)}, u32[]{:S(2)}) collective-permute-start(f32[3,2,64,128]{3,2,1,0:T(8,128)S(1)} %get-tuple-element.351), channel_id=1, source_target_pairs={{1,0},{2,1},{3,2},{4,3},{5,4},{6,5},{7,6},{8,7},{9,8},{10,9},{11,1... | collective-permute-start | bytes 589832 | tf_op jit(solution)/shard_map/while/body/eval_jaxpr/ppermute | solution.py:28
  165.0 6.8 %collective-permute-start.1 = (f32[3,2,64,128]{3,2,1,0:T(8,128)S(1)}, f32[3,2,64,128]{3,2,1,0:T(8,128)S(1)}, u32[]{:S(2)}, u32[]{:S(2)}) collective-permute-start(f32[3,2,64,128]{3,2,1,0:T(8,128)S(1)} %get-tuple-element.351), channel_id=1, source_target_pairs={{1,0},{2,1},{3,2},{4,3},{5,4},{6,5},{7,6},{8,7},{9,8},{10,9},{11,1... | collective-permute-start | bytes 589832 | tf_op jit(solution)/shard_map/while/body/eval_jaxpr/ppermute | solution.py:28
  184.8 26.5 %reshape.34 = f32[3,2,2,32,2,64,2]{6,5,4,3,2,1,0:T(8,128)} reshape(f32[3,4,64,128]{3,2,1,0:T(8,128)S(1)} %collective-permute-done.6) | data formatting | bytes 786432 | tf_op jit(solution)/shard_map/reshape | solution.py:83
  211.3 9.4 %reduce_sum.19 = f32[3,2,32,64]{3,2,1,0:T(8,128)S(1)} reduce(f32[3,2,2,32,2,64,2]{6,5,4,3,2,1,0:T(8,128)} %reshape.34, f32[]{:T(128)} %constant.108.clone.1), dimensions={2,4,6}, to_apply=%region_7.8 | reduce | flops 86016 | bytes 442372 | tf_op jit(solution)/shard_map/reduce_sum | solution.py:86
  222.8 9.3 %all-to-all-start = ((f32[16,1,12288]{2,1,0:T(1,128)}), f32[16,1,12288]{2,1,0:T(1,128)S(1)}, u32[]{:S(2)}, u32[]{:S(2)}) async-start(f32[16,1,12288]{2,1,0:T(1,128)} %reshape.39), calls=%async_computation | async-start | bytes 1572864 | tf_op jit(solution)/shard_map/all_to_all | solution.py:43
  232.4 11.6 %psum.14 = f32[3,2,32,64]{3,2,1,0:T(8,128)S(1)} all-reduce(f32[3,2,32,64]{3,2,1,0:T(8,128)S(1)} %get-tuple-element.253), channel_id=1, replica_groups=mesh['cuts_0'=2,'cuts_1'=8,'space'=32] {'cuts_0'}, use_global_device_ids=true, to_apply=%region_1.2 | all-reduce | flops 12288 | bytes 98304 | tf_op jit(solution)/shard_map/psum | solution.py:60
  244.1 30.5 %psum.15 = f32[3,2,32,64]{3,2,1,0:T(8,128)S(1)} all-reduce(f32[3,2,32,64]{3,2,1,0:T(8,128)S(1)} %psum.14), channel_id=1, replica_groups=mesh['cuts_0'=2,'cuts_1'=8,'space'=32] {'cuts_1'}, use_global_device_ids=true, to_apply=%region_2.3 | all-reduce | flops 12288 | bytes 98304 | tf_op jit(solution)/shard_map/psum | solution.py:60
  280.6 337.4 %while.73 = (s32[]{:T(128)}, f32[3,2,32,64]{3,2,1,0:T(8,128)S(1)}, f32[3,2,32,64]{3,2,1,0:T(8,128)S(1)}, f32[16,3,2,32,64]{4,3,2,1,0:T(8,128)}, s32[]{:T(128)}, ...) while((s32[]{:T(128)}, f32[3,2,32,64]{3,2,1,0:T(8,128)S(1)}, f32[3,2,32,64]{3,2,1,0:T(8,128)S(1)}, ...), condition=%wide.region_11.12_spmd.clone, body=%wide.region_8.11_spmd.clone.sunk | while | flops 698841 | bytes 1336828 | solution.py:136
  280.6 21.4 %while.74 = (s32[]{:T(128)}, f32[3,2,32,64]{3,2,1,0:T(8,128)S(1)}, s32[]{:T(128)}) while((s32[]{:T(128)}, f32[3,2,32,64]{3,2,1,0:T(8,128)S(1)}, s32[]{:T(128)}) %tuple.126), condition=%wide.region_10.10_spmd, body=%wide.region_9.9_spmd.sunk | while | flops 661970 | bytes 1090877 | solution.py:113
  303.0 21.4 %while.74 = (s32[]{:T(128)}, f32[3,2,32,64]{3,2,1,0:T(8,128)S(1)}, s32[]{:T(128)}) while((s32[]{:T(128)}, f32[3,2,32,64]{3,2,1,0:T(8,128)S(1)}, s32[]{:T(128)}) %tuple.126), condition=%wide.region_10.10_spmd, body=%wide.region_9.9_spmd.sunk | while | flops 661970 | bytes 1090877 | solution.py:113
  325.3 21.4 %while.74 = (s32[]{:T(128)}, f32[3,2,32,64]{3,2,1,0:T(8,128)S(1)}, s32[]{:T(128)}) while((s32[]{:T(128)}, f32[3,2,32,64]{3,2,1,0:T(8,128)S(1)}, s32[]{:T(128)}) %tuple.126), condition=%wide.region_10.10_spmd, body=%wide.region_9.9_spmd.sunk | while | flops 661970 | bytes 1090877 | solution.py:113
  347.7 21.9 %while.74 = (s32[]{:T(128)}, f32[3,2,32,64]{3,2,1,0:T(8,128)S(1)}, s32[]{:T(128)}) while((s32[]{:T(128)}, f32[3,2,32,64]{3,2,1,0:T(8,128)S(1)}, s32[]{:T(128)}) %tuple.126), condition=%wide.region_10.10_spmd, body=%wide.region_9.9_spmd.sunk | while | flops 661970 | bytes 1090877 | solution.py:113
  370.6 21.8 %while.74 = (s32[]{:T(128)}, f32[3,2,32,64]{3,2,1,0:T(8,128)S(1)}, s32[]{:T(128)}) while((s32[]{:T(128)}, f32[3,2,32,64]{3,2,1,0:T(8,128)S(1)}, s32[]{:T(128)}) %tuple.126), condition=%wide.region_10.10_spmd, body=%wide.region_9.9_spmd.sunk | while | flops 661970 | bytes 1090877 | solution.py:113
  393.4 21.4 %while.74 = (s32[]{:T(128)}, f32[3,2,32,64]{3,2,1,0:T(8,128)S(1)}, s32[]{:T(128)}) while((s32[]{:T(128)}, f32[3,2,32,64]{3,2,1,0:T(8,128)S(1)}, s32[]{:T(128)}) %tuple.126), condition=%wide.region_10.10_spmd, body=%wide.region_9.9_spmd.sunk | while | flops 661970 | bytes 1090877 | solution.py:113
  415.7 21.4 %while.74 = (s32[]{:T(128)}, f32[3,2,32,64]{3,2,1,0:T(8,128)S(1)}, s32[]{:T(128)}) while((s32[]{:T(128)}, f32[3,2,32,64]{3,2,1,0:T(8,128)S(1)}, s32[]{:T(128)}) %tuple.126), condition=%wide.region_10.10_spmd, body=%wide.region_9.9_spmd.sunk | while | flops 661970 | bytes 1090877 | solution.py:113
  438.1 21.4 %while.74 = (s32[]{:T(128)}, f32[3,2,32,64]{3,2,1,0:T(8,128)S(1)}, s32[]{:T(128)}) while((s32[]{:T(128)}, f32[3,2,32,64]{3,2,1,0:T(8,128)S(1)}, s32[]{:T(128)}) %tuple.126), condition=%wide.region_10.10_spmd, body=%wide.region_9.9_spmd.sunk | while | flops 661970 | bytes 1090877 | solution.py:113
  460.5 21.4 %while.74 = (s32[]{:T(128)}, f32[3,2,32,64]{3,2,1,0:T(8,128)S(1)}, s32[]{:T(128)}) while((s32[]{:T(128)}, f32[3,2,32,64]{3,2,1,0:T(8,128)S(1)}, s32[]{:T(128)}) %tuple.126), condition=%wide.region_10.10_spmd, body=%wide.region_9.9_spmd.sunk | while | flops 661970 | bytes 1090877 | solution.py:113
  482.9 21.9 %while.74 = (s32[]{:T(128)}, f32[3,2,32,64]{3,2,1,0:T(8,128)S(1)}, s32[]{:T(128)}) while((s32[]{:T(128)}, f32[3,2,32,64]{3,2,1,0:T(8,128)S(1)}, s32[]{:T(128)}) %tuple.126), condition=%wide.region_10.10_spmd, body=%wide.region_9.9_spmd.sunk | while | flops 661970 | bytes 1090877 | solution.py:113
  505.8 21.8 %while.74 = (s32[]{:T(128)}, f32[3,2,32,64]{3,2,1,0:T(8,128)S(1)}, s32[]{:T(128)}) while((s32[]{:T(128)}, f32[3,2,32,64]{3,2,1,0:T(8,128)S(1)}, s32[]{:T(128)}) %tuple.126), condition=%wide.region_10.10_spmd, body=%wide.region_9.9_spmd.sunk | while | flops 661970 | bytes 1090877 | solution.py:113
  528.5 21.4 %while.74 = (s32[]{:T(128)}, f32[3,2,32,64]{3,2,1,0:T(8,128)S(1)}, s32[]{:T(128)}) while((s32[]{:T(128)}, f32[3,2,32,64]{3,2,1,0:T(8,128)S(1)}, s32[]{:T(128)}) %tuple.126), condition=%wide.region_10.10_spmd, body=%wide.region_9.9_spmd.sunk | while | flops 661970 | bytes 1090877 | solution.py:113
  550.9 21.4 %while.74 = (s32[]{:T(128)}, f32[3,2,32,64]{3,2,1,0:T(8,128)S(1)}, s32[]{:T(128)}) while((s32[]{:T(128)}, f32[3,2,32,64]{3,2,1,0:T(8,128)S(1)}, s32[]{:T(128)}) %tuple.126), condition=%wide.region_10.10_spmd, body=%wide.region_9.9_spmd.sunk | while | flops 661970 | bytes 1090877 | solution.py:113
  573.3 21.4 %while.74 = (s32[]{:T(128)}, f32[3,2,32,64]{3,2,1,0:T(8,128)S(1)}, s32[]{:T(128)}) while((s32[]{:T(128)}, f32[3,2,32,64]{3,2,1,0:T(8,128)S(1)}, s32[]{:T(128)}) %tuple.126), condition=%wide.region_10.10_spmd, body=%wide.region_9.9_spmd.sunk | while | flops 661970 | bytes 1090877 | solution.py:113
  595.6 21.4 %while.74 = (s32[]{:T(128)}, f32[3,2,32,64]{3,2,1,0:T(8,128)S(1)}, s32[]{:T(128)}) while((s32[]{:T(128)}, f32[3,2,32,64]{3,2,1,0:T(8,128)S(1)}, s32[]{:T(128)}) %tuple.126), condition=%wide.region_10.10_spmd, body=%wide.region_9.9_spmd.sunk | while | flops 661970 | bytes 1090877 | solution.py:113
  (430 shorter events, 441.0 us)
Async XLA Ops:
  36.7 12.3 %collective-permute-start.2 = (f32[3,1,32,64]{3,2,1,0:T(8,128)S(1)}, f32[3,1,32,64]{3,2,1,0:T(8,128)S(1)}, u32[]{:S(2)}, u32[]{:S(2)}) collective-permute-start(f32[3,1,32,64]{3,2,1,0:T(8,128)S(1)} %get-tuple-element.364), channel_id=1, source_target_pairs={{1,0},{2,1},{3,2},{4,3},{5,4},{6,5},{7,6},{8,7},{9,8},{10,9},{11,1... | collective-permute-start | bytes 73736 | tf_op jit(solution)/shard_map/while/body/eval_jaxpr/ppermute | solution.py:28
  47.1 8.5 %collective-permute-start.3 = (f32[3,1,32,64]{3,2,1,0:T(8,128)S(1)}, f32[3,1,32,64]{3,2,1,0:T(8,128)S(1)}, u32[]{:S(2)}, u32[]{:S(2)}) collective-permute-start(f32[3,1,32,64]{3,2,1,0:T(8,128)S(1)} %get-tuple-element.365), channel_id=1, source_target_pairs={{0,1},{1,2},{2,3},{3,4},{4,5},{5,6},{6,7},{7,8},{8,9},{9,10},{10,1... | collective-permute-start | bytes 73736 | tf_op jit(solution)/shard_map/while/body/eval_jaxpr/ppermute | solution.py:26
  67.8 10.1 %collective-permute-start = (f32[3,2,64,128]{3,2,1,0:T(8,128)S(1)}, f32[3,2,64,128]{3,2,1,0:T(8,128)S(1)}, u32[]{:S(2)}, u32[]{:S(2)}) collective-permute-start(f32[3,2,64,128]{3,2,1,0:T(8,128)S(1)} %get-tuple-element.347), channel_id=1, source_target_pairs={{0,1},{1,2},{2,3},{3,4},{4,5},{5,6},{6,7},{7,8},{8,9},{9,10},{10,1... | collective-permute-start | bytes 589832 | tf_op jit(solution)/shard_map/while/body/eval_jaxpr/ppermute | solution.py:26
  69.8 12.0 %collective-permute-start.1 = (f32[3,2,64,128]{3,2,1,0:T(8,128)S(1)}, f32[3,2,64,128]{3,2,1,0:T(8,128)S(1)}, u32[]{:S(2)}, u32[]{:S(2)}) collective-permute-start(f32[3,2,64,128]{3,2,1,0:T(8,128)S(1)} %get-tuple-element.351), channel_id=1, source_target_pairs={{1,0},{2,1},{3,2},{4,3},{5,4},{6,5},{7,6},{8,7},{9,8},{10,9},{11,1... | collective-permute-start | bytes 589832 | tf_op jit(solution)/shard_map/while/body/eval_jaxpr/ppermute | solution.py:28
  82.8 10.2 %collective-permute-start = (f32[3,2,64,128]{3,2,1,0:T(8,128)S(1)}, f32[3,2,64,128]{3,2,1,0:T(8,128)S(1)}, u32[]{:S(2)}, u32[]{:S(2)}) collective-permute-start(f32[3,2,64,128]{3,2,1,0:T(8,128)S(1)} %get-tuple-element.347), channel_id=1, source_target_pairs={{0,1},{1,2},{2,3},{3,4},{4,5},{5,6},{6,7},{7,8},{8,9},{9,10},{10,1... | collective-permute-start | bytes 589832 | tf_op jit(solution)/shard_map/while/body/eval_jaxpr/ppermute | solution.py:26
  84.8 11.6 %collective-permute-start.1 = (f32[3,2,64,128]{3,2,1,0:T(8,128)S(1)}, f32[3,2,64,128]{3,2,1,0:T(8,128)S(1)}, u32[]{:S(2)}, u32[]{:S(2)}) collective-permute-start(f32[3,2,64,128]{3,2,1,0:T(8,128)S(1)} %get-tuple-element.351), channel_id=1, source_target_pairs={{1,0},{2,1},{3,2},{4,3},{5,4},{6,5},{7,6},{8,7},{9,8},{10,9},{11,1... | collective-permute-start | bytes 589832 | tf_op jit(solution)/shard_map/while/body/eval_jaxpr/ppermute | solution.py:28
  97.5 10.2 %collective-permute-start = (f32[3,2,64,128]{3,2,1,0:T(8,128)S(1)}, f32[3,2,64,128]{3,2,1,0:T(8,128)S(1)}, u32[]{:S(2)}, u32[]{:S(2)}) collective-permute-start(f32[3,2,64,128]{3,2,1,0:T(8,128)S(1)} %get-tuple-element.347), channel_id=1, source_target_pairs={{0,1},{1,2},{2,3},{3,4},{4,5},{5,6},{6,7},{7,8},{8,9},{9,10},{10,1... | collective-permute-start | bytes 589832 | tf_op jit(solution)/shard_map/while/body/eval_jaxpr/ppermute | solution.py:26
  99.4 10.4 %collective-permute-start.1 = (f32[3,2,64,128]{3,2,1,0:T(8,128)S(1)}, f32[3,2,64,128]{3,2,1,0:T(8,128)S(1)}, u32[]{:S(2)}, u32[]{:S(2)}) collective-permute-start(f32[3,2,64,128]{3,2,1,0:T(8,128)S(1)} %get-tuple-element.351), channel_id=1, source_target_pairs={{1,0},{2,1},{3,2},{4,3},{5,4},{6,5},{7,6},{8,7},{9,8},{10,9},{11,1... | collective-permute-start | bytes 589832 | tf_op jit(solution)/shard_map/while/body/eval_jaxpr/ppermute | solution.py:28
  110.9 10.2 %collective-permute-start = (f32[3,2,64,128]{3,2,1,0:T(8,128)S(1)}, f32[3,2,64,128]{3,2,1,0:T(8,128)S(1)}, u32[]{:S(2)}, u32[]{:S(2)}) collective-permute-start(f32[3,2,64,128]{3,2,1,0:T(8,128)S(1)} %get-tuple-element.347), channel_id=1, source_target_pairs={{0,1},{1,2},{2,3},{3,4},{4,5},{5,6},{6,7},{7,8},{8,9},{9,10},{10,1... | collective-permute-start | bytes 589832 | tf_op jit(solution)/shard_map/while/body/eval_jaxpr/ppermute | solution.py:26
  112.8 10.0 %collective-permute-start.1 = (f32[3,2,64,128]{3,2,1,0:T(8,128)S(1)}, f32[3,2,64,128]{3,2,1,0:T(8,128)S(1)}, u32[]{:S(2)}, u32[]{:S(2)}) collective-permute-start(f32[3,2,64,128]{3,2,1,0:T(8,128)S(1)} %get-tuple-element.351), channel_id=1, source_target_pairs={{1,0},{2,1},{3,2},{4,3},{5,4},{6,5},{7,6},{8,7},{9,8},{10,9},{11,1... | collective-permute-start | bytes 589832 | tf_op jit(solution)/shard_map/while/body/eval_jaxpr/ppermute | solution.py:28
  124.0 10.2 %collective-permute-start = (f32[3,2,64,128]{3,2,1,0:T(8,128)S(1)}, f32[3,2,64,128]{3,2,1,0:T(8,128)S(1)}, u32[]{:S(2)}, u32[]{:S(2)}) collective-permute-start(f32[3,2,64,128]{3,2,1,0:T(8,128)S(1)} %get-tuple-element.347), channel_id=1, source_target_pairs={{0,1},{1,2},{2,3},{3,4},{4,5},{5,6},{6,7},{7,8},{8,9},{9,10},{10,1... | collective-permute-start | bytes 589832 | tf_op jit(solution)/shard_map/while/body/eval_jaxpr/ppermute | solution.py:26
  125.9 10.0 %collective-permute-start.1 = (f32[3,2,64,128]{3,2,1,0:T(8,128)S(1)}, f32[3,2,64,128]{3,2,1,0:T(8,128)S(1)}, u32[]{:S(2)}, u32[]{:S(2)}) collective-permute-start(f32[3,2,64,128]{3,2,1,0:T(8,128)S(1)} %get-tuple-element.351), channel_id=1, source_target_pairs={{1,0},{2,1},{3,2},{4,3},{5,4},{6,5},{7,6},{8,7},{9,8},{10,9},{11,1... | collective-permute-start | bytes 589832 | tf_op jit(solution)/shard_map/while/body/eval_jaxpr/ppermute | solution.py:28
  137.0 10.2 %collective-permute-start = (f32[3,2,64,128]{3,2,1,0:T(8,128)S(1)}, f32[3,2,64,128]{3,2,1,0:T(8,128)S(1)}, u32[]{:S(2)}, u32[]{:S(2)}) collective-permute-start(f32[3,2,64,128]{3,2,1,0:T(8,128)S(1)} %get-tuple-element.347), channel_id=1, source_target_pairs={{0,1},{1,2},{2,3},{3,4},{4,5},{5,6},{6,7},{7,8},{8,9},{9,10},{10,1... | collective-permute-start | bytes 589832 | tf_op jit(solution)/shard_map/while/body/eval_jaxpr/ppermute | solution.py:26
  139.0 10.0 %collective-permute-start.1 = (f32[3,2,64,128]{3,2,1,0:T(8,128)S(1)}, f32[3,2,64,128]{3,2,1,0:T(8,128)S(1)}, u32[]{:S(2)}, u32[]{:S(2)}) collective-permute-start(f32[3,2,64,128]{3,2,1,0:T(8,128)S(1)} %get-tuple-element.351), channel_id=1, source_target_pairs={{1,0},{2,1},{3,2},{4,3},{5,4},{6,5},{7,6},{8,7},{9,8},{10,9},{11,1... | collective-permute-start | bytes 589832 | tf_op jit(solution)/shard_map/while/body/eval_jaxpr/ppermute | solution.py:28
  150.1 10.2 %collective-permute-start = (f32[3,2,64,128]{3,2,1,0:T(8,128)S(1)}, f32[3,2,64,128]{3,2,1,0:T(8,128)S(1)}, u32[]{:S(2)}, u32[]{:S(2)}) collective-permute-start(f32[3,2,64,128]{3,2,1,0:T(8,128)S(1)} %get-tuple-element.347), channel_id=1, source_target_pairs={{0,1},{1,2},{2,3},{3,4},{4,5},{5,6},{6,7},{7,8},{8,9},{9,10},{10,1... | collective-permute-start | bytes 589832 | tf_op jit(solution)/shard_map/while/body/eval_jaxpr/ppermute | solution.py:26
  152.0 10.0 %collective-permute-start.1 = (f32[3,2,64,128]{3,2,1,0:T(8,128)S(1)}, f32[3,2,64,128]{3,2,1,0:T(8,128)S(1)}, u32[]{:S(2)}, u32[]{:S(2)}) collective-permute-start(f32[3,2,64,128]{3,2,1,0:T(8,128)S(1)} %get-tuple-element.351), channel_id=1, source_target_pairs={{1,0},{2,1},{3,2},{4,3},{5,4},{6,5},{7,6},{8,7},{9,8},{10,9},{11,1... | collective-permute-start | bytes 589832 | tf_op jit(solution)/shard_map/while/body/eval_jaxpr/ppermute | solution.py:28
  163.1 10.2 %collective-permute-start = (f32[3,2,64,128]{3,2,1,0:T(8,128)S(1)}, f32[3,2,64,128]{3,2,1,0:T(8,128)S(1)}, u32[]{:S(2)}, u32[]{:S(2)}) collective-permute-start(f32[3,2,64,128]{3,2,1,0:T(8,128)S(1)} %get-tuple-element.347), channel_id=1, source_target_pairs={{0,1},{1,2},{2,3},{3,4},{4,5},{5,6},{6,7},{7,8},{8,9},{9,10},{10,1... | collective-permute-start | bytes 589832 | tf_op jit(solution)/shard_map/while/body/eval_jaxpr/ppermute | solution.py:26
  165.0 10.0 %collective-permute-start.1 = (f32[3,2,64,128]{3,2,1,0:T(8,128)S(1)}, f32[3,2,64,128]{3,2,1,0:T(8,128)S(1)}, u32[]{:S(2)}, u32[]{:S(2)}) collective-permute-start(f32[3,2,64,128]{3,2,1,0:T(8,128)S(1)} %get-tuple-element.351), channel_id=1, source_target_pairs={{1,0},{2,1},{3,2},{4,3},{5,4},{6,5},{7,6},{8,7},{9,8},{10,9},{11,1... | collective-permute-start | bytes 589832 | tf_op jit(solution)/shard_map/while/body/eval_jaxpr/ppermute | solution.py:28
  176.2 8.7 %collective-permute-start.6 = (f32[3,4,64,128]{3,2,1,0:T(8,128)S(1)}, f32[3,4,64,128]{3,2,1,0:T(8,128)S(1)}, u32[]{:S(2)}, u32[]{:S(2)}) collective-permute-start(f32[3,4,64,128]{3,2,1,0:T(8,128)S(1)} %sub.66), channel_id=1, source_target_pairs={{0,32},{32,64},{64,96},{96,128},{128,160},{160,192},{192,224},{224... | collective-permute-start | bytes 1179656 | tf_op jit(solution)/shard_map/ppermute | solution.py:38
  222.8 53.0 %all-to-all-start = ((f32[16,1,12288]{2,1,0:T(1,128)}), f32[16,1,12288]{2,1,0:T(1,128)S(1)}, u32[]{:S(2)}, u32[]{:S(2)}) async-start(f32[16,1,12288]{2,1,0:T(1,128)} %reshape.39), calls=%async_computation | async-start | bytes 1572864 | tf_op jit(solution)/shard_map/all_to_all | solution.py:43
  327.3 8.4 %collective-permute-start.5 = (f32[3,1,32,64]{3,2,1,0:T(8,128)S(1)}, f32[3,1,32,64]{3,2,1,0:T(8,128)S(1)}, u32[]{:S(2)}, u32[]{:S(2)}) collective-permute-start(f32[3,1,32,64]{3,2,1,0:T(8,128)S(1)} %get-tuple-element.381), channel_id=1, source_target_pairs={{0,1},{1,2},{2,3},{3,4},{4,5},{5,6},{6,7},{7,8},{8,9},{9,10},{10,1... | collective-permute-start | bytes 73736 | tf_op jit(solution)/shard_map/while/body/eval_jaxpr/while/body/eval_jaxpr/ppermute | solution.py:26
  338.0 8.4 %collective-permute-start.5 = (f32[3,1,32,64]{3,2,1,0:T(8,128)S(1)}, f32[3,1,32,64]{3,2,1,0:T(8,128)S(1)}, u32[]{:S(2)}, u32[]{:S(2)}) collective-permute-start(f32[3,1,32,64]{3,2,1,0:T(8,128)S(1)} %get-tuple-element.381), channel_id=1, source_target_pairs={{0,1},{1,2},{2,3},{3,4},{4,5},{5,6},{6,7},{7,8},{8,9},{9,10},{10,1... | collective-permute-start | bytes 73736 | tf_op jit(solution)/shard_map/while/body/eval_jaxpr/while/body/eval_jaxpr/ppermute | solution.py:26
  349.7 8.9 %collective-permute-start.5 = (f32[3,1,32,64]{3,2,1,0:T(8,128)S(1)}, f32[3,1,32,64]{3,2,1,0:T(8,128)S(1)}, u32[]{:S(2)}, u32[]{:S(2)}) collective-permute-start(f32[3,1,32,64]{3,2,1,0:T(8,128)S(1)} %get-tuple-element.381), channel_id=1, source_target_pairs={{0,1},{1,2},{2,3},{3,4},{4,5},{5,6},{6,7},{7,8},{8,9},{9,10},{10,1... | collective-permute-start | bytes 73736 | tf_op jit(solution)/shard_map/while/body/eval_jaxpr/while/body/eval_jaxpr/ppermute | solution.py:26
  360.9 8.4 %collective-permute-start.5 = (f32[3,1,32,64]{3,2,1,0:T(8,128)S(1)}, f32[3,1,32,64]{3,2,1,0:T(8,128)S(1)}, u32[]{:S(2)}, u32[]{:S(2)}) collective-permute-start(f32[3,1,32,64]{3,2,1,0:T(8,128)S(1)} %get-tuple-element.381), channel_id=1, source_target_pairs={{0,1},{1,2},{2,3},{3,4},{4,5},{5,6},{6,7},{7,8},{8,9},{9,10},{10,1... | collective-permute-start | bytes 73736 | tf_op jit(solution)/shard_map/while/body/eval_jaxpr/while/body/eval_jaxpr/ppermute | solution.py:26
  372.5 8.8 %collective-permute-start.5 = (f32[3,1,32,64]{3,2,1,0:T(8,128)S(1)}, f32[3,1,32,64]{3,2,1,0:T(8,128)S(1)}, u32[]{:S(2)}, u32[]{:S(2)}) collective-permute-start(f32[3,1,32,64]{3,2,1,0:T(8,128)S(1)} %get-tuple-element.381), channel_id=1, source_target_pairs={{0,1},{1,2},{2,3},{3,4},{4,5},{5,6},{6,7},{7,8},{8,9},{9,10},{10,1... | collective-permute-start | bytes 73736 | tf_op jit(solution)/shard_map/while/body/eval_jaxpr/while/body/eval_jaxpr/ppermute | solution.py:26
  383.6 8.4 %collective-permute-start.5 = (f32[3,1,32,64]{3,2,1,0:T(8,128)S(1)}, f32[3,1,32,64]{3,2,1,0:T(8,128)S(1)}, u32[]{:S(2)}, u32[]{:S(2)}) collective-permute-start(f32[3,1,32,64]{3,2,1,0:T(8,128)S(1)} %get-tuple-element.381), channel_id=1, source_target_pairs={{0,1},{1,2},{2,3},{3,4},{4,5},{5,6},{6,7},{7,8},{8,9},{9,10},{10,1... | collective-permute-start | bytes 73736 | tf_op jit(solution)/shard_map/while/body/eval_jaxpr/while/body/eval_jaxpr/ppermute | solution.py:26
  406.0 8.4 %collective-permute-start.5 = (f32[3,1,32,64]{3,2,1,0:T(8,128)S(1)}, f32[3,1,32,64]{3,2,1,0:T(8,128)S(1)}, u32[]{:S(2)}, u32[]{:S(2)}) collective-permute-start(f32[3,1,32,64]{3,2,1,0:T(8,128)S(1)} %get-tuple-element.381), channel_id=1, source_target_pairs={{0,1},{1,2},{2,3},{3,4},{4,5},{5,6},{6,7},{7,8},{8,9},{9,10},{10,1... | collective-permute-start | bytes 73736 | tf_op jit(solution)/shard_map/while/body/eval_jaxpr/while/body/eval_jaxpr/ppermute | solution.py:26
  428.4 8.4 %collective-permute-start.5 = (f32[3,1,32,64]{3,2,1,0:T(8,128)S(1)}, f32[3,1,32,64]{3,2,1,0:T(8,128)S(1)}, u32[]{:S(2)}, u32[]{:S(2)}) collective-permute-start(f32[3,1,32,64]{3,2,1,0:T(8,128)S(1)} %get-tuple-element.381), channel_id=1, source_target_pairs={{0,1},{1,2},{2,3},{3,4},{4,5},{5,6},{6,7},{7,8},{8,9},{9,10},{10,1... | collective-permute-start | bytes 73736 | tf_op jit(solution)/shard_map/while/body/eval_jaxpr/while/body/eval_jaxpr/ppermute | solution.py:26
  450.8 8.4 %collective-permute-start.5 = (f32[3,1,32,64]{3,2,1,0:T(8,128)S(1)}, f32[3,1,32,64]{3,2,1,0:T(8,128)S(1)}, u32[]{:S(2)}, u32[]{:S(2)}) collective-permute-start(f32[3,1,32,64]{3,2,1,0:T(8,128)S(1)} %get-tuple-element.381), channel_id=1, source_target_pairs={{0,1},{1,2},{2,3},{3,4},{4,5},{5,6},{6,7},{7,8},{8,9},{9,10},{10,1... | collective-permute-start | bytes 73736 | tf_op jit(solution)/shard_map/while/body/eval_jaxpr/while/body/eval_jaxpr/ppermute | solution.py:26
  473.1 8.4 %collective-permute-start.5 = (f32[3,1,32,64]{3,2,1,0:T(8,128)S(1)}, f32[3,1,32,64]{3,2,1,0:T(8,128)S(1)}, u32[]{:S(2)}, u32[]{:S(2)}) collective-permute-start(f32[3,1,32,64]{3,2,1,0:T(8,128)S(1)} %get-tuple-element.381), channel_id=1, source_target_pairs={{0,1},{1,2},{2,3},{3,4},{4,5},{5,6},{6,7},{7,8},{8,9},{9,10},{10,1... | collective-permute-start | bytes 73736 | tf_op jit(solution)/shard_map/while/body/eval_jaxpr/while/body/eval_jaxpr/ppermute | solution.py:26
  495.5 8.9 %collective-permute-start.5 = (f32[3,1,32,64]{3,2,1,0:T(8,128)S(1)}, f32[3,1,32,64]{3,2,1,0:T(8,128)S(1)}, u32[]{:S(2)}, u32[]{:S(2)}) collective-permute-start(f32[3,1,32,64]{3,2,1,0:T(8,128)S(1)} %get-tuple-element.381), channel_id=1, source_target_pairs={{0,1},{1,2},{2,3},{3,4},{4,5},{5,6},{6,7},{7,8},{8,9},{9,10},{10,1... | collective-permute-start | bytes 73736 | tf_op jit(solution)/shard_map/while/body/eval_jaxpr/while/body/eval_jaxpr/ppermute | solution.py:26
  518.4 8.8 %collective-permute-start.5 = (f32[3,1,32,64]{3,2,1,0:T(8,128)S(1)}, f32[3,1,32,64]{3,2,1,0:T(8,128)S(1)}, u32[]{:S(2)}, u32[]{:S(2)}) collective-permute-start(f32[3,1,32,64]{3,2,1,0:T(8,128)S(1)} %get-tuple-element.381), channel_id=1, source_target_pairs={{0,1},{1,2},{2,3},{3,4},{4,5},{5,6},{6,7},{7,8},{8,9},{9,10},{10,1... | collective-permute-start | bytes 73736 | tf_op jit(solution)/shard_map/while/body/eval_jaxpr/while/body/eval_jaxpr/ppermute | solution.py:26
  (52 other events, 297.3 us)
where the time goes:
time: 623 us; the launch traced here: 620 us
  starting transfers between devices  229 us (37%)
  waiting for transfers between devices  227 us (36%)
  local copies, waits for them, and re-layouts  65.9 us (11%)
  other arithmetic  52.5 us (8%)
  blocking collectives  42.2 us (7%)
    ppermute x40, waiting for transfers between devices, padded_2(): lax.ppermute(tail, axis, [(i, (i + 1) % count) for i in range(ends)])  205 us
    ppermute x40, starting transfers between devices, padded_2(): lax.ppermute(head, axis, [((i + 1) % count, i) for i in range(ends)])  124 us
    ppermute x40, starting transfers between devices, padded_2(): lax.ppermute(tail, axis, [(i, (i + 1) % count) for i in range(ends)])  91.9 us
    psum x2, blocking collectives, broadcast_by_axis(): shard = lax.psum(shard, axis)  42.2 us
    another operation x1, local copies, waits for them, and re-layouts, restrict(): field.reshape(field.shape[0], field.shape[1] // 2, 2, field.shape[2] // 2...  27.2 us
    reshape x1, local copies, waits for them, and re-layouts, restrict(): field.reshape(field.shape[0], field.shape[1] // 2, 2, field.shape[2] // 2...  26.5 us
    reduce_sum x2, other arithmetic, restrict(): return jnp.sum(blocks, axis=(2, 4, 6)) * 0.125  18.9 us
    ppermute x40, waiting for transfers between devices, padded_2(): lax.ppermute(head, axis, [((i + 1) % count, i) for i in range(ends)])  16.7 us
  transfers between devices with their start and end apart: 82, of which 49 were waited for; matrix products, arithmetic and copies ran while one was open for 0% of the time, Pallas kernels for 0%

commit v1 on v0

v1 whole, which is shorter than its diff:
```python
import functools

import jax
import jax.numpy as jnp
from jax import lax
from jax.experimental import pallas as pl
from jax.experimental.pallas import tpu as pltpu
from jax.sharding import PartitionSpec as P

FSTEPS = 16
HALO = 4
ROUNDS = FSTEPS // HALO
NY = 64
NZ = 128
CY = NY // 4
GROUPS = 16
SLABS = 32
AXES = ("cuts", "space")
PAIRS = [[2 * k, 2 * k + 1] for k in range(SLABS // 2)]

fine_rate = 0.08
fine_advect = 0.04
coarse_rate = 0.16
coarse_advect = 0.16

VMEM = pl.BlockSpec(memory_space=pltpu.VMEM)
SMEM = pl.BlockSpec(memory_space=pltpu.SMEM)
PARAMS = pltpu.CompilerParams(vmem_limit_bytes=32 * 1024 * 1024)
f32 = jnp.float32


def one_plane(src, dst, i, o, rows, rate, advect, factor, top, bottom, left, right):
    for j in range(rows // 8):
        at = 8 + 8 * j
        mid = pl.ds(at, 8)
        v = [src[c, i, mid, :] for c in range(3)]
        av = [advect * v[c] for c in range(3)]
        xp, xm = rate - av[0], rate + av[0]
        yp, ym = rate - av[1], rate + av[1]
        zp = jnp.where(right, 0.0, rate - av[2])
        zm = jnp.where(left, 0.0, rate + av[2])
        for c in range(3):
            new = v[c] * (1.0 - 6.0 * rate)
            new += xp * src[c, i + 1, mid, :] + xm * src[c, i - 1, mid, :]
            new += yp * src[c, i, pl.ds(at + 1, 8), :] + ym * src[c, i, pl.ds(at - 1, 8), :]
            new += zp * pltpu.roll(v[c], 127, 1) + zm * pltpu.roll(v[c], 1, 1)
            dst[c, o, mid, :] = new * factor


def lanes(shape=(8, 128)):
    return lax.broadcasted_iota(jnp.int32, shape, 1)


def guards(dst, c, o, low):
    last = pltpu.roll(dst[c, o, pl.ds(CY, 8), :], 64, 1)
    first = pltpu.roll(dst[c, o, pl.ds(8, 8), :], 64, 1)
    dst[c, o, 7:8, :] = jnp.where(low, 0.0, last)[7:8, :]
    dst[c, o, CY + 8 : CY + 9, :] = jnp.where(low, first, 0.0)[0:1, :]


def coarse_step(src, dst, begin, end, limits):
    lane = lanes()
    left = (lane & 63) == 0
    right = (lane & 63) == 63
    low = lane < 64
    for i in range(begin, end):
        factor = limits(i)
        one_plane(src, dst, i, i, CY, coarse_rate, coarse_advect, factor, None, None, left, right)
        for c in range(3):
            guards(dst, c, i, low)


def fill_guards(dst, begin, end):
    low = lanes() < 64
    for i in range(begin, end):
        for c in range(3):
            guards(dst, c, i, low)


def pairs_to_one(scale):
    rows = lax.broadcasted_iota(jnp.int32, (256, 128), 0)
    columns = lax.broadcasted_iota(jnp.int32, (256, 128), 1)
    return jnp.where((rows >> 1) == columns, f32(scale), f32(0.0))


def one_to_pairs():
    rows = lax.broadcasted_iota(jnp.int32, (128, 256), 0)
    columns = lax.broadcasted_iota(jnp.int32, (128, 256), 1)
    return jnp.where(rows == (columns >> 1), f32(1.0), f32(0.0))


def dot(a, b):
    return jnp.dot(a, b, precision=lax.Precision.HIGHEST, preferred_element_type=f32)


def restricted(planes):
    def rows(c, p):
        total = (planes(c, 2 * p, 0) + planes(c, 2 * p, 1)) + (planes(c, 2 * p + 1, 0) + planes(c, 2 * p + 1, 1))
        return jnp.concatenate([total[:CY], total[CY:]], axis=1)

    return rows


def fine_kernel(last, flags, left_ref, mid_ref, right_ref, *rest):
    if last:
        oc_ref, out_ref, q_ref, a, b, sums = rest
    else:
        out_ref, a, b = rest
    lane = lanes()
    left = lane == 0
    right = lane == 127
    zero = jnp.zeros((8, 128), f32)
    for c in range(3):

        def clear(i, carry):
            for buffer in (a, b):
                buffer[c, i, 0:8, :] = zero
                buffer[c, i, NY + 8 : NY + 16, :] = zero
            return carry

        lax.fori_loop(0, 3 * HALO, clear, 0)
        for at, ref in ((0, left_ref), (HALO, mid_ref), (2 * HALO, right_ref)):
            for i in range(HALO):
                a[c, at + i, 8 : NY + 8, :] = ref[c, i]
    has_left = flags[0].astype(f32)
    has_right = flags[1].astype(f32)
    src, dst = a, b
    for step in range(1, HALO + 1):

        def plane(i, carry):
            factor = jnp.where(i < HALO, has_left, jnp.where(i >= 2 * HALO, has_right, 1.0))
            one_plane(src, dst, i, i, NY, fine_rate, fine_advect, factor, None, None, left, right)
            return carry

        lax.fori_loop(step, 3 * HALO - step, plane, 0)
        src, dst = dst, src
    for c in range(3):
        for i in range(HALO):
            out_ref[c, i] = src[c, HALO + i, 8 : NY + 8, :]
    if last:
        rows = restricted(lambda c, p, start: src[c, HALO + p, pl.ds(8 + start, 32, stride=2), :])
        for c in range(3):
            for p in range(2):
                sums[pl.ds((c * 2 + p) * CY, CY), :] = rows(c, p)
        ended = dot(sums[...], pairs_to_one(0.125))
        keep = jnp.where(flags[2] == 0, 0.0, 1.0)
        for c in range(3):
            for p in range(2):
                at = (c * 2 + p) * CY
                q_ref[c, p] = ended[at : at + CY] - keep * oc_ref[c, p]


def fine_round(flags, left, mid, right, oc=None):
    last = oc is not None
    shape = jax.ShapeDtypeStruct(mid.shape, f32)
    buffer = pltpu.VMEM((3, 3 * HALO, NY + 16, NZ), f32)
    coarse = jax.ShapeDtypeStruct((3, 2, CY, NZ), f32)
    return pl.pallas_call(
        functools.partial(fine_kernel, last),
        out_shape=(shape, coarse) if last else shape,
        in_specs=[SMEM] + [VMEM] * (4 if last else 3),
        out_specs=(VMEM, VMEM) if last else VMEM,
        scratch_shapes=[buffer, buffer] + ([pltpu.VMEM((6 * CY, 256), f32)] if last else []),
        compiler_params=PARAMS,
        cost_estimate=pl.CostEstimate(flops=40_000_000, bytes_accessed=2_000_000, transcendentals=0),
        name="fine_last" if last else "fine_steps",
    )(flags, left, mid, right, *([oc] if last else []))


def first_coarse_kernel(flags, left_ref, mid_ref, right_ref, out_ref, a, b, sums):
    for c in range(3):
        for part, ref in enumerate((left_ref, mid_ref, right_ref)):
            rows = restricted(lambda c, p, start: ref[c, p, pl.ds(start, 32, stride=2), :])
            for p in range(2):
                sums[pl.ds((c * 6 + part * 2 + p) * CY, CY), :] = rows(c, p)
    averaged = dot(sums[...], pairs_to_one(0.125))
    for c in range(3):
        for i in range(6):
            at = (c * 6 + i) * CY
            a[c, i, 8 : CY + 8, :] = averaged[at : at + CY]
    fill_guards(a, 0, 6)
    has_left = flags[0].astype(f32)
    has_right = flags[1].astype(f32)
    limits = lambda i: has_left if i < 2 else has_right if i >= 4 else f32(1.0)
    coarse_step(a, b, 1, 5, limits)
    coarse_step(b, a, 2, 4, limits)
    for c in range(3):
        for i in range(2):
            out_ref[c, i] = a[c, 2 + i, 8 : CY + 8, :]


def first_coarse(flags, left, mid, right):
    buffer = pltpu.VMEM((3, 6, CY + 16, NZ), f32)
    return pl.pallas_call(
        first_coarse_kernel,
        out_shape=jax.ShapeDtypeStruct((3, 2, CY, NZ), f32),
        in_specs=[SMEM, VMEM, VMEM, VMEM],
        out_specs=VMEM,
        scratch_shapes=[buffer, buffer, pltpu.VMEM((18 * CY, 256), f32)],
        compiler_params=PARAMS,
        cost_estimate=pl.CostEstimate(flops=4_000_000, bytes_accessed=1_300_000, transcendentals=0),
        name="first_coarse",
    )(flags, left, mid, right)


def change_kernel(ends_ref, oc_ref, out_ref):
    expand = one_to_pairs()
    for c in range(3):
        for p in range(2):
            wide = dot(oc_ref[c, p], expand)
            tall = jnp.concatenate([wide[:, :NZ], wide[:, NZ:]], axis=0)
            for i in (2 * p, 2 * p + 1):
                for start in (0, 1):
                    at = pl.ds(start, 32, stride=2)
                    out_ref[c, i, at, :] = ends_ref[c, i, at, :] - tall


def fine_change(ends, oc):
    return pl.pallas_call(
        change_kernel,
        out_shape=jax.ShapeDtypeStruct(ends.shape, f32),
        in_specs=[VMEM, VMEM],
        out_specs=VMEM,
        compiler_params=PARAMS,
        cost_estimate=pl.CostEstimate(flops=1_000_000, bytes_accessed=900_000, transcendentals=0),
        name="fine_change",
    )(ends, oc)


def sweep_kernel(turn, flags, got_ref, before_ref, d_left, d_mid, d_right, d_own, even_ref, odd_ref, s_ref, even_out, odd_out, a, b):
    for c in range(3):
        for core in range(2):
            for i in range(4):
                a[c, 8 * core + i, 8 : CY + 8, :] = got_ref[core, c, i]
            for i in range(2):
                a[c, 4 + 2 * core + i, 8 : CY + 8, :] = before_ref[core, c, i]
    fill_guards(a, 0, 12)
    has_left = flags[3].astype(f32)
    has_right = flags[4].astype(f32)
    core = flags[5]
    mine = flags[2] == 2 * turn
    limits = lambda i: has_left if i < 4 else has_right if i >= 8 else f32(1.0)
    coarse_step(a, b, 1, 11, limits)
    coarse_step(b, a, 2, 10, limits)
    for c in range(3):
        for i in range(2):
            first = jnp.where(core == 0, a[c, 4 + i, 8 : CY + 8, :], a[c, 6 + i, 8 : CY + 8, :])
            even_out[c, i] = jnp.where(mine, first, even_ref[c, i])
        for i, part in enumerate([d_left.at[c, 0], d_left.at[c, 1]] + [d_mid.at[c, k] for k in range(4)] + [d_right.at[c, 0], d_right.at[c, 1]]):
            a[c, 2 + i, 8 : CY + 8, :] += part[...]
    fill_guards(a, 2, 10)
    coarse_step(a, b, 3, 9, limits)
    coarse_step(b, a, 4, 8, limits)
    for c in range(3):
        for i in range(4):
            s_ref[c, i] = a[c, 4 + i, 8 : CY + 8, :] + d_own[c, i]
        for i in range(2):
            second = jnp.where(core == 0, a[c, 4 + i, 8 : CY + 8, :], a[c, 6 + i, 8 : CY + 8, :])
            odd_out[c, i] = jnp.where(mine, second, odd_ref[c, i])


def sweep(turn, flags, *arrays):
    buffer = pltpu.VMEM((3, 12, CY + 16, NZ), f32)
    two = jax.ShapeDtypeStruct((3, 2, CY, NZ), f32)
    four = jax.ShapeDtypeStruct((3, 4, CY, NZ), f32)
    return pl.pallas_call(
        functools.partial(sweep_kernel, turn),
        out_shape=(four, two, two),
        in_specs=[SMEM] + [VMEM] * len(arrays),
        out_specs=(VMEM,) * 3,
        scratch_shapes=[buffer, buffer],
        compiler_params=PARAMS,
        cost_estimate=pl.CostEstimate(flops=4_000_000, bytes_accessed=900_000, transcendentals=0),
        name="sweep",
    )(flags, *arrays)


def final_kernel(flags, start_ref, previous_ref, even_ref, odd_ref, out_ref):
    group = flags[2]

    @pl.when(group == 0)
    def _():
        out_ref[...] = start_ref[...]

    @pl.when(group != 0)
    def _():
        expand = one_to_pairs()
        odd = (group & 1) == 1
        for c in range(3):
            for p in range(2):
                wide = dot(jnp.where(odd, odd_ref[c, p], even_ref[c, p]), expand)
                tall = jnp.concatenate([wide[:, :NZ], wide[:, NZ:]], axis=0)
                for i in (2 * p, 2 * p + 1):
                    for start in (0, 1):
                        at = pl.ds(start, 32, stride=2)
                        out_ref[c, i, at, :] = previous_ref[c, i, at, :] + tall


def final(flags, start, previous, even, odd):
    return pl.pallas_call(
        final_kernel,
        out_shape=jax.ShapeDtypeStruct(start.shape, f32),
        in_specs=[SMEM] + [VMEM] * 4,
        out_specs=VMEM,
        compiler_params=PARAMS,
        cost_estimate=pl.CostEstimate(flops=1_000_000, bytes_accessed=1_300_000, transcendentals=0),
        name="final",
    )(flags, start, previous, even, odd)


def handed_on(value, groups, by, place):
    table = []
    for c in groups:
        if not 0 <= c + by < GROUPS:
            continue
        for s in range(SLABS):
            if 0 <= place(s) < SLABS:
                table.append((c * SLABS + s, (c + by) * SLABS + place(s)))
    return lax.ppermute(value, AXES, table)


def both_cores(value):
    return lax.all_gather(value, "space", axis=0, tiled=False, axis_index_groups=PAIRS)


def shards(starts):
    initial = starts[0]
    group = lax.axis_index("cuts")
    slab = lax.axis_index("space")
    flags = jnp.stack(
        [slab > 0, slab < SLABS - 1, group, slab > 1, slab < SLABS - 2, slab & 1, group, group]
    ).astype(jnp.int32)
    up = [(s, s + 1) for s in range(SLABS - 1)]
    down = [(s + 1, s) for s in range(SLABS - 1)]
    field = initial
    for turn in range(ROUNDS):
        left = lax.ppermute(field, "space", up)
        right = lax.ppermute(field, "space", down)
        if turn == 0:
            oc = first_coarse(flags, left, field, right)
        if turn < ROUNDS - 1:
            field = fine_round(flags, left, field, right)
        else:
            ends, mine = fine_round(flags, left, field, right, oc)
    pair = both_cores(mine)
    whole = jnp.concatenate([pair[0], pair[1]], axis=1)
    odd_groups = range(1, GROUPS, 2)
    even_groups = range(0, GROUPS, 2)
    core = slab & 1
    state, even, odd = whole, oc, oc
    for turn in range(1, GROUPS // 2):
        outer = handed_on(state, [2 * turn - 2], 2, lambda s: s + 2 if s % 2 == 0 else s - 2)
        half = jnp.where(core == 0, state[:, :2], state[:, 2:])
        inner = handed_on(half, [2 * turn - 2], 2, lambda s: s)
        if turn == 1:
            d_left = handed_on(whole[:, 2:], odd_groups, 1, lambda s: s + 2)
            d_right = handed_on(whole[:, :2], odd_groups, 1, lambda s: s - 2)
            d_mid = handed_on(whole, odd_groups, 1, lambda s: s)
        both = both_cores(jnp.concatenate([outer, inner], axis=1))
        state, even, odd = sweep(turn, flags, both[:, :, :4], both[:, :, 4:], d_left, d_mid, d_right, whole, even, odd)
        if turn == 1:
            change = fine_change(ends, oc)
            change, state = lax.optimization_barrier((change, state))
            previous = handed_on(change, range(GROUPS), 1, lambda s: s)
    filled = handed_on(odd, even_groups, 1, lambda s: s)
    return final(flags, initial, previous, even, filled)[None]


def solution(mesh):
    placed = P("cuts", None, "space", None, None)
    return jax.shard_map(shards, mesh=mesh, in_specs=(placed,), out_specs=placed, check_vma=False)
```

time: 623 us -> 203 us (0.33)
  the two profiles are of different devices: /device:TPU:2 before, /device:TPU:124 now
where the time goes in v1:
time: 203 us; the launch traced here: 202 us
  waiting for transfers between devices  104 us (51%)
  Pallas kernels  41.6 us (20%)
  starting transfers between devices  38.4 us (19%)
  blocking collectives  16.2 us (8%)
    ppermute x19, waiting for transfers between devices, handed_on(): return lax.ppermute(value, AXES, table)  51.5 us
    ppermute x4, waiting for transfers between devices, shards(): left = lax.ppermute(field, 'space', up)  39.6 us
    pallas_call x7, Pallas kernels, sweep(): pl.pallas_call(functools.partial(sweep_kernel, turn), out_shape=(four, tw...  20.2 us
    pallas_call x4, Pallas kernels, fine_round(): pl.pallas_call(functools.partial(fine_kernel, last), out_shape=(shape, co...  18 us
    all_gather x8, blocking collectives, both_cores(): lax.all_gather(value, 'space', axis=0, tiled=False, axis_index_groups=PAIRS)  16.2 us
    ppermute x4, starting transfers between devices, shards(): right = lax.ppermute(field, 'space', down)  15.3 us
    ppermute x19, starting transfers between devices, handed_on(): return lax.ppermute(value, AXES, table)  13.9 us
    ppermute x4, waiting for transfers between devices, shards(): right = lax.ppermute(field, 'space', down)  12.6 us
  transfers between devices with their start and end apart: 27, of which 10 were waited for; matrix products, arithmetic and copies ran while one was open for 0% of the time, Pallas kernels for 4%

profile of v1, /device:TPU:124, one launch (start us, length us, event | category | flops | bytes accessed | tf_op | source)
XLA Modules:
  0.0 201.9 jit_solution(3618516716445869076)
XLA Ops:
  0.0 9.4 %collective-permute-start.1 = (f32[3,4,64,128]{3,2,1,0:T(8,128)}, f32[3,4,64,128]{3,2,1,0:T(8,128)S(1)}, u32[]{:S(2)}, u32[]{:S(2)}) collective-permute-start(f32[3,4,64,128]{3,2,1,0:T(8,128)} %bitcast.15), channel_id=1, source_target_pairs={{1,0},{2,1},{3,2},{4,3},{5,4},{6,5},{7,6},{8,7},{9,8},{10,9},{11,1... | collective-permute-start | bytes 1179656 | tf_op jit(solution)/shard_map/ppermute | solution.py:338
  11.5 5.1 %collective-permute-done.1.right_ref = f32[3,4,64,128]{3,2,1,0:T(8,128)S(1)} collective-permute-done((f32[3,4,64,128]{3,2,1,0:T(8,128)}, f32[3,4,64,128]{3,2,1,0:T(8,128)S(1)}, u32[]{:S(2)}, u32[]{:S(2)}) %collective-permute-start.1) | collective-permute-done | bytes 393248 | tf_op jit(solution)/shard_map/ppermute | solution.py:338
  16.6 9.3 %collective-permute-done.left_ref = f32[3,4,64,128]{3,2,1,0:T(8,128)S(1)} collective-permute-done((f32[3,4,64,128]{3,2,1,0:T(8,128)}, f32[3,4,64,128]{3,2,1,0:T(8,128)S(1)}, u32[]{:S(2)}, u32[]{:S(2)}) %collective-permute-start) | collective-permute-done | bytes 393248 | tf_op jit(solution)/shard_map/ppermute | solution.py:337
  27.0 4.5 %fine_steps.3.mid_ref = f32[3,4,64,128]{3,2,1,0:T(8,128)S(1)} custom-call(s32[8]{0:T(128)S(1)} %stack.45.flags, f32[3,4,64,128]{3,2,1,0:T(8,128)S(1)} %collective-permute-done.left_ref, f32[3,4,64,128]{3,2,1,0:T(8,128)S(1)} %bitcast.17, f32[3,4,64,128]{3,2,1,0:T(8,128)S(1)} %collective-permute-done.1.right_ref), custom_call_target="tpu_custom_call" | custom-call | flops 40000000 | bytes 2000000 | tf_op jit(solution)/shard_map/fine_steps/pallas_call | solution.py:158
  33.4 2.4 %collective-permute-start.2 = (f32[3,4,64,128]{3,2,1,0:T(8,128)S(1)}, f32[3,4,64,128]{3,2,1,0:T(8,128)S(1)}, u32[]{:S(2)}, u32[]{:S(2)}) collective-permute-start(f32[3,4,64,128]{3,2,1,0:T(8,128)S(1)} %fine_steps.3.mid_ref), channel_id=1, source_target_pairs={{0,1},{1,2},{2,3},{3,4},{4,5},{5,6},{6,7},{7,8},{8,9},{9,10},{10,1... | collective-permute-start | bytes 1179656 | tf_op jit(solution)/shard_map/ppermute | solution.py:337
  35.8 2.9 %collective-permute-done.3.right_ref = f32[3,4,64,128]{3,2,1,0:T(8,128)S(1)} collective-permute-done((f32[3,4,64,128]{3,2,1,0:T(8,128)S(1)}, f32[3,4,64,128]{3,2,1,0:T(8,128)S(1)}, u32[]{:S(2)}, u32[]{:S(2)}) %collective-permute-start.3) | collective-permute-done | bytes 393248 | tf_op jit(solution)/shard_map/ppermute | solution.py:338
  38.7 11.0 %collective-permute-done.2.left_ref = f32[3,4,64,128]{3,2,1,0:T(8,128)S(1)} collective-permute-done((f32[3,4,64,128]{3,2,1,0:T(8,128)S(1)}, f32[3,4,64,128]{3,2,1,0:T(8,128)S(1)}, u32[]{:S(2)}, u32[]{:S(2)}) %collective-permute-start.2) | collective-permute-done | bytes 393248 | tf_op jit(solution)/shard_map/ppermute | solution.py:337
  49.6 4.5 %fine_steps.4.mid_ref = f32[3,4,64,128]{3,2,1,0:T(8,128)S(1)} custom-call(s32[8]{0:T(128)S(1)} %stack.45.flags, f32[3,4,64,128]{3,2,1,0:T(8,128)S(1)} %collective-permute-done.2.left_ref, f32[3,4,64,128]{3,2,1,0:T(8,128)S(1)} %fine_steps.3.mid_ref, f32[3,4,64,128]{3,2,1,0:T(8,128)S(1)} %collective-permute-done.3.right_ref), custom_call_target="tpu_custom_call" | custom-call | flops 40000000 | bytes 2000000 | tf_op jit(solution)/shard_map/fine_steps/pallas_call | solution.py:158
  54.1 2.1 %collective-permute-start.5 = (f32[3,4,64,128]{3,2,1,0:T(8,128)S(1)}, f32[3,4,64,128]{3,2,1,0:T(8,128)S(1)}, u32[]{:S(2)}, u32[]{:S(2)}) collective-permute-start(f32[3,4,64,128]{3,2,1,0:T(8,128)S(1)} %fine_steps.4.mid_ref), channel_id=1, source_target_pairs={{1,0},{2,1},{3,2},{4,3},{5,4},{6,5},{7,6},{8,7},{9,8},{10,9},{11,1... | collective-permute-start | bytes 1179656 | tf_op jit(solution)/shard_map/ppermute | solution.py:338
  56.2 2.4 %collective-permute-start.4 = (f32[3,4,64,128]{3,2,1,0:T(8,128)S(1)}, f32[3,4,64,128]{3,2,1,0:T(8,128)S(1)}, u32[]{:S(2)}, u32[]{:S(2)}) collective-permute-start(f32[3,4,64,128]{3,2,1,0:T(8,128)S(1)} %fine_steps.4.mid_ref), channel_id=1, source_target_pairs={{0,1},{1,2},{2,3},{3,4},{4,5},{5,6},{6,7},{7,8},{8,9},{9,10},{10,1... | collective-permute-start | bytes 1179656 | tf_op jit(solution)/shard_map/ppermute | solution.py:337
  58.6 2.9 %collective-permute-done.5.right_ref = f32[3,4,64,128]{3,2,1,0:T(8,128)S(1)} collective-permute-done((f32[3,4,64,128]{3,2,1,0:T(8,128)S(1)}, f32[3,4,64,128]{3,2,1,0:T(8,128)S(1)}, u32[]{:S(2)}, u32[]{:S(2)}) %collective-permute-start.5) | collective-permute-done | bytes 393248 | tf_op jit(solution)/shard_map/ppermute | solution.py:338
  61.5 10.9 %collective-permute-done.4.left_ref = f32[3,4,64,128]{3,2,1,0:T(8,128)S(1)} collective-permute-done((f32[3,4,64,128]{3,2,1,0:T(8,128)S(1)}, f32[3,4,64,128]{3,2,1,0:T(8,128)S(1)}, u32[]{:S(2)}, u32[]{:S(2)}) %collective-permute-start.4) | collective-permute-done | bytes 393248 | tf_op jit(solution)/shard_map/ppermute | solution.py:337
  72.4 4.5 %fine_steps.5.mid_ref = f32[3,4,64,128]{3,2,1,0:T(8,128)S(1)} custom-call(s32[8]{0:T(128)S(1)} %stack.45.flags, f32[3,4,64,128]{3,2,1,0:T(8,128)S(1)} %collective-permute-done.4.left_ref, f32[3,4,64,128]{3,2,1,0:T(8,128)S(1)} %fine_steps.4.mid_ref, f32[3,4,64,128]{3,2,1,0:T(8,128)S(1)} %collective-permute-done.5.right_ref), custom_call_target="tpu_custom_call" | custom-call | flops 40000000 | bytes 2000000 | tf_op jit(solution)/shard_map/fine_steps/pallas_call | solution.py:158
  78.8 2.4 %collective-permute-start.6 = (f32[3,4,64,128]{3,2,1,0:T(8,128)S(1)}, f32[3,4,64,128]{3,2,1,0:T(8,128)S(1)}, u32[]{:S(2)}, u32[]{:S(2)}) collective-permute-start(f32[3,4,64,128]{3,2,1,0:T(8,128)S(1)} %fine_steps.5.mid_ref), channel_id=1, source_target_pairs={{0,1},{1,2},{2,3},{3,4},{4,5},{5,6},{6,7},{7,8},{8,9},{9,10},{10,1... | collective-permute-start | bytes 1179656 | tf_op jit(solution)/shard_map/ppermute | solution.py:337
  84.1 8.4 %collective-permute-done.6.left_ref = f32[3,4,64,128]{3,2,1,0:T(8,128)S(1)} collective-permute-done((f32[3,4,64,128]{3,2,1,0:T(8,128)S(1)}, f32[3,4,64,128]{3,2,1,0:T(8,128)S(1)}, u32[]{:S(2)}, u32[]{:S(2)}) %collective-permute-start.6) | collective-permute-done | bytes 393248 | tf_op jit(solution)/shard_map/ppermute | solution.py:337
  92.5 4.7 %fine_last.1 = (f32[3,4,64,128]{3,2,1,0:T(8,128)S(1)}, f32[3,2,16,128]{3,2,1,0:T(8,128)S(1)}) custom-call(s32[8]{0:T(128)S(1)} %stack.45.flags, f32[3,4,64,128]{3,2,1,0:T(8,128)S(1)} %collective-permute-done.6.left_ref, f32[3,4,64,128]{3,2,1,0:T(8,128)S(1)} %fine_steps.5.mid_ref, f32[3,4,64,128]{3,2,1,0:T(8,128)S(1)} %collective-permute-done.7.right_ref, ...), custom_call_target="tpu_custom_call" | custom-call | flops 40000000 | bytes 2000000 | tf_op jit(solution)/shard_map/fine_last/pallas_call | solution.py:158
  102.9 2.0 all-gather.1
  105.0 2.8 %sweep.7 = (f32[3,4,16,128]{3,2,1,0:T(8,128)S(1)}, f32[3,2,16,128]{3,2,1,0:T(8,128)S(1)}, f32[3,2,16,128]{3,2,1,0:T(8,128)S(1)}) custom-call(s32[8]{0:T(128)S(1)} %stack.45.flags, f32[2,3,4,16,128]{4,3,2,1,0:T(8,128)S(1)} %slice.116.got_ref, f32[2,3,2,16,128]{4,3,2,1,0:T(8,128)S(1)} %slice.117.before_ref, ...), custom_call_target="tpu_custom_call" | custom-call | flops 4000000 | bytes 900000 | tf_op jit(solution)/shard_map/sweep/pallas_call | solution.py:266
  109.2 2.0 all-gather.2
  111.3 2.8 %sweep.8 = (f32[3,4,16,128]{3,2,1,0:T(8,128)S(1)}, f32[3,2,16,128]{3,2,1,0:T(8,128)S(1)}, f32[3,2,16,128]{3,2,1,0:T(8,128)S(1)}) custom-call(s32[8]{0:T(128)S(1)} %stack.45.flags, f32[2,3,4,16,128]{4,3,2,1,0:T(8,128)S(1)} %slice.118.got_ref, f32[2,3,2,16,128]{4,3,2,1,0:T(8,128)S(1)} %slice.119.before_ref, ...), custom_call_target="tpu_custom_call" | custom-call | flops 4000000 | bytes 900000 | tf_op jit(solution)/shard_map/sweep/pallas_call | solution.py:266
  115.5 2.0 all-gather.3
  117.5 2.8 %sweep.9 = (f32[3,4,16,128]{3,2,1,0:T(8,128)S(1)}, f32[3,2,16,128]{3,2,1,0:T(8,128)S(1)}, f32[3,2,16,128]{3,2,1,0:T(8,128)S(1)}) custom-call(s32[8]{0:T(128)S(1)} %stack.45.flags, f32[2,3,4,16,128]{4,3,2,1,0:T(8,128)S(1)} %slice.120.got_ref, f32[2,3,2,16,128]{4,3,2,1,0:T(8,128)S(1)} %slice.121.before_ref, ...), custom_call_target="tpu_custom_call" | custom-call | flops 4000000 | bytes 900000 | tf_op jit(solution)/shard_map/sweep/pallas_call | solution.py:266
  121.7 2.0 all-gather.4
  123.8 2.8 %sweep.10 = (f32[3,4,16,128]{3,2,1,0:T(8,128)S(1)}, f32[3,2,16,128]{3,2,1,0:T(8,128)S(1)}, f32[3,2,16,128]{3,2,1,0:T(8,128)S(1)}) custom-call(s32[8]{0:T(128)S(1)} %stack.45.flags, f32[2,3,4,16,128]{4,3,2,1,0:T(8,128)S(1)} %slice.122.got_ref, f32[2,3,2,16,128]{4,3,2,1,0:T(8,128)S(1)} %slice.123.before_ref, ...), custom_call_target="tpu_custom_call" | custom-call | flops 4000000 | bytes 900000 | tf_op jit(solution)/shard_map/sweep/pallas_call | solution.py:266
  128.0 2.0 all-gather.5
  130.1 2.8 %sweep.11 = (f32[3,4,16,128]{3,2,1,0:T(8,128)S(1)}, f32[3,2,16,128]{3,2,1,0:T(8,128)S(1)}, f32[3,2,16,128]{3,2,1,0:T(8,128)S(1)}) custom-call(s32[8]{0:T(128)S(1)} %stack.45.flags, f32[2,3,4,16,128]{4,3,2,1,0:T(8,128)S(1)} %slice.124.got_ref, f32[2,3,2,16,128]{4,3,2,1,0:T(8,128)S(1)} %slice.125.before_ref, ...), custom_call_target="tpu_custom_call" | custom-call | flops 4000000 | bytes 900000 | tf_op jit(solution)/shard_map/sweep/pallas_call | solution.py:266
  135.6 2.2 %all-gather.6 = f32[6,6,16,128]{3,2,1,0:T(8,128)S(1)} all-gather(f32[3,6,16,128]{3,2,1,0:T(8,128)S(1)} %pad_maximum_fusion.5), channel_id=8, replica_groups={{0,1},{2,3},{4,5},{6,7},{8,9},{10,11},{12,13},{14,15},{16,17},{18,19},{..., dimensions={0}, use_global_device_ids=true | all-gather | bytes 442368 | tf_op jit(solution)/shard_map/all_gather | solution.py:323
  137.8 2.8 %sweep.12 = (f32[3,4,16,128]{3,2,1,0:T(8,128)S(1)}, f32[3,2,16,128]{3,2,1,0:T(8,128)S(1)}, f32[3,2,16,128]{3,2,1,0:T(8,128)S(1)}) custom-call(s32[8]{0:T(128)S(1)} %stack.45.flags, f32[2,3,4,16,128]{4,3,2,1,0:T(8,128)S(1)} %slice.126.got_ref, f32[2,3,2,16,128]{4,3,2,1,0:T(8,128)S(1)} %slice.127.before_ref, ...), custom_call_target="tpu_custom_call" | custom-call | flops 4000000 | bytes 900000 | tf_op jit(solution)/shard_map/sweep/pallas_call | solution.py:266
  142.0 2.0 all-gather.7
  144.1 3.4 %sweep.13 = (f32[3,4,16,128]{3,2,1,0:T(8,128)}, f32[3,2,16,128]{3,2,1,0:T(8,128)S(1)}, f32[3,2,16,128]{3,2,1,0:T(8,128)S(1)}) custom-call(s32[8]{0:T(128)S(1)} %stack.45.flags, f32[2,3,4,16,128]{4,3,2,1,0:T(8,128)S(1)} %slice.128.got_ref, f32[2,3,2,16,128]{4,3,2,1,0:T(8,128)S(1)} %slice.129.before_ref, f32[3,2,16,128]{3,2,1,0:T(8,128)S(1)} %collective-permute-done.10.d_left, ...), custom_call_target="tpu_custom_call" | custom-call | flops 4000000 | bytes 900000 | tf_op jit(solution)/shard_map/sweep/pallas_call | solution.py:266
  148.7 4.9 %collective-permute-done.13.previous_ref = f32[3,4,64,128]{3,2,1,0:T(8,128)S(1)} collective-permute-done((f32[3,4,64,128]{3,2,1,0:T(8,128)S(1)}, f32[3,4,64,128]{3,2,1,0:T(8,128)S(1)}, u32[]{:S(2)}, u32[]{:S(2)}) %collective-permute-start.13) | collective-permute-done | bytes 393248 | tf_op jit(solution)/shard_map/ppermute | solution.py:319
  153.6 46.6 %collective-permute-done.26.odd_ref = f32[3,2,16,128]{3,2,1,0:T(8,128)S(1)} collective-permute-done((f32[3,2,16,128]{3,2,1,0:T(8,128)S(1)}, f32[3,2,16,128]{3,2,1,0:T(8,128)S(1)}, u32[]{:S(2)}, u32[]{:S(2)}) %collective-permute-start.26) | collective-permute-done | bytes 49184 | tf_op jit(solution)/shard_map/ppermute | solution.py:319
  (78 shorter events, 28.0 us)
Async XLA Ops:
  0.0 16.6 %collective-permute-start.1 = (f32[3,4,64,128]{3,2,1,0:T(8,128)}, f32[3,4,64,128]{3,2,1,0:T(8,128)S(1)}, u32[]{:S(2)}, u32[]{:S(2)}) collective-permute-start(f32[3,4,64,128]{3,2,1,0:T(8,128)} %bitcast.15), channel_id=1, source_target_pairs={{1,0},{2,1},{3,2},{4,3},{5,4},{6,5},{7,6},{8,7},{9,8},{10,9},{11,1... | collective-permute-start | bytes 1179656 | tf_op jit(solution)/shard_map/ppermute | solution.py:338
  9.4 16.5 %collective-permute-start = (f32[3,4,64,128]{3,2,1,0:T(8,128)}, f32[3,4,64,128]{3,2,1,0:T(8,128)S(1)}, u32[]{:S(2)}, u32[]{:S(2)}) collective-permute-start(f32[3,4,64,128]{3,2,1,0:T(8,128)} %bitcast.16), channel_id=1, source_target_pairs={{0,1},{1,2},{2,3},{3,4},{4,5},{5,6},{6,7},{7,8},{8,9},{9,10},{10,1... | collective-permute-start | bytes 1179656 | tf_op jit(solution)/shard_map/ppermute | solution.py:337
  26.0 1.0 copy-start
  31.4 7.2 %collective-permute-start.3 = (f32[3,4,64,128]{3,2,1,0:T(8,128)S(1)}, f32[3,4,64,128]{3,2,1,0:T(8,128)S(1)}, u32[]{:S(2)}, u32[]{:S(2)}) collective-permute-start(f32[3,4,64,128]{3,2,1,0:T(8,128)S(1)} %fine_steps.3.mid_ref), channel_id=1, source_target_pairs={{1,0},{2,1},{3,2},{4,3},{5,4},{6,5},{7,6},{8,7},{9,8},{10,9},{11,1... | collective-permute-start | bytes 1179656 | tf_op jit(solution)/shard_map/ppermute | solution.py:338
  33.4 16.3 %collective-permute-start.2 = (f32[3,4,64,128]{3,2,1,0:T(8,128)S(1)}, f32[3,4,64,128]{3,2,1,0:T(8,128)S(1)}, u32[]{:S(2)}, u32[]{:S(2)}) collective-permute-start(f32[3,4,64,128]{3,2,1,0:T(8,128)S(1)} %fine_steps.3.mid_ref), channel_id=1, source_target_pairs={{0,1},{1,2},{2,3},{3,4},{4,5},{5,6},{6,7},{7,8},{8,9},{9,10},{10,1... | collective-permute-start | bytes 1179656 | tf_op jit(solution)/shard_map/ppermute | solution.py:337
  54.1 27.1 %copy-start.1 = (f32[1,3,4,64,128]{4,3,2,1,0:T(8,128)S(1)}, f32[1,3,4,64,128]{4,3,2,1,0:T(8,128)}, u32[]{:S(2)}) copy-start(f32[1,3,4,64,128]{4,3,2,1,0:T(8,128)} %param.1) | copy-start | bytes 1179652
  54.1 7.4 %collective-permute-start.5 = (f32[3,4,64,128]{3,2,1,0:T(8,128)S(1)}, f32[3,4,64,128]{3,2,1,0:T(8,128)S(1)}, u32[]{:S(2)}, u32[]{:S(2)}) collective-permute-start(f32[3,4,64,128]{3,2,1,0:T(8,128)S(1)} %fine_steps.4.mid_ref), channel_id=1, source_target_pairs={{1,0},{2,1},{3,2},{4,3},{5,4},{6,5},{7,6},{8,7},{9,8},{10,9},{11,1... | collective-permute-start | bytes 1179656 | tf_op jit(solution)/shard_map/ppermute | solution.py:338
  56.2 16.2 %collective-permute-start.4 = (f32[3,4,64,128]{3,2,1,0:T(8,128)S(1)}, f32[3,4,64,128]{3,2,1,0:T(8,128)S(1)}, u32[]{:S(2)}, u32[]{:S(2)}) collective-permute-start(f32[3,4,64,128]{3,2,1,0:T(8,128)S(1)} %fine_steps.4.mid_ref), channel_id=1, source_target_pairs={{0,1},{1,2},{2,3},{3,4},{4,5},{5,6},{6,7},{7,8},{8,9},{9,10},{10,1... | collective-permute-start | bytes 1179656 | tf_op jit(solution)/shard_map/ppermute | solution.py:337
  76.9 7.2 %collective-permute-start.7 = (f32[3,4,64,128]{3,2,1,0:T(8,128)S(1)}, f32[3,4,64,128]{3,2,1,0:T(8,128)S(1)}, u32[]{:S(2)}, u32[]{:S(2)}) collective-permute-start(f32[3,4,64,128]{3,2,1,0:T(8,128)S(1)} %fine_steps.5.mid_ref), channel_id=1, source_target_pairs={{1,0},{2,1},{3,2},{4,3},{5,4},{6,5},{7,6},{8,7},{9,8},{10,9},{11,1... | collective-permute-start | bytes 1179656 | tf_op jit(solution)/shard_map/ppermute | solution.py:338
  78.8 13.7 %collective-permute-start.6 = (f32[3,4,64,128]{3,2,1,0:T(8,128)S(1)}, f32[3,4,64,128]{3,2,1,0:T(8,128)S(1)}, u32[]{:S(2)}, u32[]{:S(2)}) collective-permute-start(f32[3,4,64,128]{3,2,1,0:T(8,128)S(1)} %fine_steps.5.mid_ref), channel_id=1, source_target_pairs={{0,1},{1,2},{2,3},{3,4},{4,5},{5,6},{6,7},{7,8},{8,9},{9,10},{10,1... | collective-permute-start | bytes 1179656 | tf_op jit(solution)/shard_map/ppermute | solution.py:337
  99.1 3.8 %collective-permute-start.8 = (f32[3,4,16,128]{3,2,1,0:T(8,128)S(1)}, f32[3,4,16,128]{3,2,1,0:T(8,128)S(1)}, u32[]{:S(2)}, u32[]{:S(2)}) collective-permute-start(f32[3,4,16,128]{3,2,1,0:T(8,128)S(1)} %pad_maximum_fusion.7.d_own), channel_id=1, source_target_pairs={{0,66},{2,68},{3,65},{4,70},{5,67},{6,72},{7,69},{8,74},{9,71},{10... | collective-permute-start | bytes 294920 | tf_op jit(solution)/shard_map/ppermute | solution.py:319
  99.7 3.1 %collective-permute-start.9 = (f32[3,2,16,128]{3,2,1,0:T(8,128)S(1)}, f32[3,2,16,128]{3,2,1,0:T(8,128)S(1)}, u32[]{:S(2)}, u32[]{:S(2)}) collective-permute-start(f32[3,2,16,128]{3,2,1,0:T(8,128)S(1)} %get-tuple-element.54), channel_id=1, source_target_pairs={{0,64},{1,65},{2,66},{3,67},{4,68},{5,69},{6,70},{7,71},{8,72},{9,... | collective-permute-start | bytes 147464 | tf_op jit(solution)/shard_map/ppermute | solution.py:319
  100.4 4.6 %collective-permute-start.12 = (f32[3,2,16,128]{3,2,1,0:T(8,128)S(1)}, f32[3,2,16,128]{3,2,1,0:T(8,128)S(1)}, u32[]{:S(2)}, u32[]{:S(2)}) collective-permute-start(f32[3,2,16,128]{3,2,1,0:T(8,128)S(1)} %get-tuple-element.53), channel_id=1, source_target_pairs={{34,64},{35,65},{36,66},{37,67},{38,68},{39,69},{40,70},{41,71},{4... | collective-permute-start | bytes 147464 | tf_op jit(solution)/shard_map/ppermute | solution.py:319
  101.1 3.9 %collective-permute-start.10 = (f32[3,2,16,128]{3,2,1,0:T(8,128)S(1)}, f32[3,2,16,128]{3,2,1,0:T(8,128)S(1)}, u32[]{:S(2)}, u32[]{:S(2)}) collective-permute-start(f32[3,2,16,128]{3,2,1,0:T(8,128)S(1)} %get-tuple-element.55), channel_id=1, source_target_pairs={{32,66},{33,67},{34,68},{35,69},{36,70},{37,71},{38,72},{39,73},{4... | collective-permute-start | bytes 147464 | tf_op jit(solution)/shard_map/ppermute | solution.py:319
  101.8 3.2 %collective-permute-start.11 = (f32[3,4,16,128]{3,2,1,0:T(8,128)S(1)}, f32[3,4,16,128]{3,2,1,0:T(8,128)S(1)}, u32[]{:S(2)}, u32[]{:S(2)}) collective-permute-start(f32[3,4,16,128]{3,2,1,0:T(8,128)S(1)} %pad_maximum_fusion.7.d_own), channel_id=1, source_target_pairs={{32,64},{33,65},{34,66},{35,67},{36,68},{37,69},{38,70},{39,71},{4... | collective-permute-start | bytes 294920 | tf_op jit(solution)/shard_map/ppermute | solution.py:319
  107.8 1.4 collective-permute-start.14
  108.5 0.7 collective-permute-start.15
  114.1 1.4 collective-permute-start.16
  114.8 0.7 collective-permute-start.17
  120.3 1.4 collective-permute-start.18
  121.0 0.7 collective-permute-start.19
  126.6 1.4 collective-permute-start.20
  127.3 0.7 collective-permute-start.21
  132.9 2.7 %collective-permute-start.22 = (f32[3,4,16,128]{3,2,1,0:T(8,128)S(1)}, f32[3,4,16,128]{3,2,1,0:T(8,128)S(1)}, u32[]{:S(2)}, u32[]{:S(2)}) collective-permute-start(f32[3,4,16,128]{3,2,1,0:T(8,128)S(1)} %get-tuple-element.45), channel_id=1, source_target_pairs={{320,386},{322,388},{323,385},{324,390},{325,387},{326,392},{327,3... | collective-permute-start | bytes 294920 | tf_op jit(solution)/shard_map/ppermute | solution.py:319
  133.6 2.0 collective-permute-start.23
  134.2 19.4 %collective-permute-start.13 = (f32[3,4,64,128]{3,2,1,0:T(8,128)S(1)}, f32[3,4,64,128]{3,2,1,0:T(8,128)S(1)}, u32[]{:S(2)}, u32[]{:S(2)}) collective-permute-start(f32[3,4,64,128]{3,2,1,0:T(8,128)S(1)} %fine_change.1), channel_id=1, source_target_pairs={{0,32},{1,33},{2,34},{3,35},{4,36},{5,37},{6,38},{7,39},{8,40},{9,... | collective-permute-start | bytes 1179656 | tf_op jit(solution)/shard_map/ppermute | solution.py:319
  140.6 1.4 collective-permute-start.24
  141.3 0.7 collective-permute-start.25
  147.5 52.7 %collective-permute-start.26 = (f32[3,2,16,128]{3,2,1,0:T(8,128)S(1)}, f32[3,2,16,128]{3,2,1,0:T(8,128)S(1)}, u32[]{:S(2)}, u32[]{:S(2)}) collective-permute-start(f32[3,2,16,128]{3,2,1,0:T(8,128)S(1)} %get-tuple-element.52), channel_id=1, source_target_pairs={{0,32},{1,33},{2,34},{3,35},{4,36},{5,37},{6,38},{7,39},{8,40},{9,... | collective-permute-start | bytes 147464 | tf_op jit(solution)/shard_map/ppermute | solution.py:319

commit v2 on v1

v2 whole, which is shorter than its diff:
```python
import functools

import jax
import jax.numpy as jnp
from jax import lax
from jax.experimental import pallas as pl
from jax.experimental.pallas import tpu as pltpu
from jax.sharding import PartitionSpec as P

FSTEPS = 16
HALO = 4
ROUNDS = FSTEPS // HALO
NY = 64
NZ = 128
CY = NY // 4
GROUPS = 16
SLABS = 32
AXES = ("cuts", "space")
PAIRS = [[2 * k, 2 * k + 1] for k in range(SLABS // 2)]

fine_rate = 0.08
fine_advect = 0.04
coarse_rate = 0.16
coarse_advect = 0.16

VMEM = pl.BlockSpec(memory_space=pltpu.VMEM)
PARAMS = pltpu.CompilerParams(vmem_limit_bytes=32 * 1024 * 1024)
f32 = jnp.float32


def position():
    return lax.axis_index("cuts"), lax.axis_index("space")


def one_plane(src, dst, i, rows, rate, advect, factor, left, right):
    edge = []
    for j in range(rows // 8):
        at = 8 + 8 * j
        mid = pl.ds(at, 8)
        v = [src[c, i, mid, :] for c in range(3)]
        av = [advect * v[c] for c in range(3)]
        xp, xm = rate - av[0], rate + av[0]
        yp, ym = rate - av[1], rate + av[1]
        zp = jnp.where(right, 0.0, rate - av[2])
        zm = jnp.where(left, 0.0, rate + av[2])
        row = []
        for c in range(3):
            new = v[c] * (1.0 - 6.0 * rate)
            new += xp * src[c, i + 1, mid, :] + xm * src[c, i - 1, mid, :]
            new += yp * src[c, i, pl.ds(at + 1, 8), :] + ym * src[c, i, pl.ds(at - 1, 8), :]
            new += zp * pltpu.roll(v[c], 127, 1) + zm * pltpu.roll(v[c], 1, 1)
            if factor is not None:
                new = new * factor
            dst[c, i, mid, :] = new
            row.append(new)
        edge.append(row)
    return edge[0], edge[-1]


def lanes(shape=(8, 128)):
    return lax.broadcasted_iota(jnp.int32, shape, 1)


def guards(dst, c, i, first, last, low):
    dst[c, i, 7:8, :] = jnp.where(low, 0.0, pltpu.roll(last, 64, 1))[7:8, :]
    dst[c, i, CY + 8 : CY + 9, :] = jnp.where(low, pltpu.roll(first, 64, 1), 0.0)[0:1, :]


def put_coarse(dst, c, i, plane, low):
    dst[c, i, 8 : CY + 8, :] = plane
    guards(dst, c, i, plane[:8], plane[8:], low)


def coarse_step(src, dst, begin, end, limits, guarded=True):
    lane = lanes()
    left = (lane & 63) == 0
    right = (lane & 63) == 63
    low = lane < 64
    for i in range(begin, end):
        first, last = one_plane(src, dst, i, CY, coarse_rate, coarse_advect, limits(i), left, right)
        if guarded:
            for c in range(3):
                guards(dst, c, i, first[c], last[c], low)


def pairs_to_one(scale):
    rows = lax.broadcasted_iota(jnp.int32, (256, 128), 0)
    columns = lax.broadcasted_iota(jnp.int32, (256, 128), 1)
    return jnp.where((rows >> 1) == columns, f32(scale), f32(0.0))


def one_to_pairs():
    rows = lax.broadcasted_iota(jnp.int32, (128, 256), 0)
    columns = lax.broadcasted_iota(jnp.int32, (128, 256), 1)
    return jnp.where(rows == (columns >> 1), f32(1.0), f32(0.0))


def dot(a, b):
    return jnp.dot(a, b, precision=lax.Precision.HIGHEST, preferred_element_type=f32)


def restricted(planes):
    def rows(c, p):
        total = (planes(c, 2 * p, 0) + planes(c, 2 * p, 1)) + (planes(c, 2 * p + 1, 0) + planes(c, 2 * p + 1, 1))
        return jnp.concatenate([total[:CY], total[CY:]], axis=1)

    return rows


def fine_kernel(last, left_ref, mid_ref, right_ref, *rest):
    if last:
        oc_ref, out_ref, q_ref, a, b, sums = rest
    else:
        out_ref, a, b = rest
    group, slab = position()
    lane = lanes()
    left = lane == 0
    right = lane == 127
    zero = jnp.zeros((8, 128), f32)
    for c in range(3):
        for i in range(3 * HALO):
            for buffer in (a, b):
                buffer[c, i, 0:8, :] = zero
                buffer[c, i, NY + 8 : NY + 16, :] = zero
        for at, ref in ((0, left_ref), (HALO, mid_ref), (2 * HALO, right_ref)):
            for i in range(HALO):
                a[c, at + i, 8 : NY + 8, :] = ref[c, i]
    has_left = jnp.where(slab > 0, f32(1.0), f32(0.0))
    has_right = jnp.where(slab < SLABS - 1, f32(1.0), f32(0.0))
    src, dst = a, b
    for step in range(1, HALO + 1):
        for i in range(step, 3 * HALO - step):
            factor = has_left if i < HALO else has_right if i >= 2 * HALO else None
            one_plane(src, dst, i, NY, fine_rate, fine_advect, factor, left, right)
        src, dst = dst, src
    for c in range(3):
        for i in range(HALO):
            out_ref[c, i] = src[c, HALO + i, 8 : NY + 8, :]
    if last:
        rows = restricted(lambda c, p, start: src[c, HALO + p, pl.ds(8 + start, 32, stride=2), :])
        for c in range(3):
            for p in range(2):
                sums[pl.ds((c * 2 + p) * CY, CY), :] = rows(c, p)
        ended = dot(sums[...], pairs_to_one(0.125))
        keep = jnp.where(group == 0, f32(0.0), f32(1.0))
        for c in range(3):
            for p in range(2):
                at = (c * 2 + p) * CY
                q_ref[c, p] = ended[at : at + CY] - keep * oc_ref[c, p]


def fine_round(left, mid, right, oc=None):
    last = oc is not None
    shape = jax.ShapeDtypeStruct(mid.shape, f32)
    buffer = pltpu.VMEM((3, 3 * HALO, NY + 16, NZ), f32)
    coarse = jax.ShapeDtypeStruct((3, 2, CY, NZ), f32)
    return pl.pallas_call(
        functools.partial(fine_kernel, last),
        out_shape=(shape, coarse) if last else shape,
        in_specs=[VMEM] * (4 if last else 3),
        out_specs=(VMEM, VMEM) if last else VMEM,
        scratch_shapes=[buffer, buffer] + ([pltpu.VMEM((6 * CY, 256), f32)] if last else []),
        compiler_params=PARAMS,
        cost_estimate=pl.CostEstimate(flops=40_000_000, bytes_accessed=2_000_000, transcendentals=0),
        name="fine_last" if last else "fine_steps",
    )(left, mid, right, *([oc] if last else []))


def first_coarse_kernel(left_ref, mid_ref, right_ref, out_ref, a, b, sums):
    group, slab = position()
    for c in range(3):
        for part, ref in enumerate((left_ref, mid_ref, right_ref)):
            rows = restricted(lambda c, p, start: ref[c, p, pl.ds(start, 32, stride=2), :])
            for p in range(2):
                sums[pl.ds((c * 6 + part * 2 + p) * CY, CY), :] = rows(c, p)
    averaged = dot(sums[...], pairs_to_one(0.125))
    low = lanes() < 64
    for c in range(3):
        for i in range(6):
            at = (c * 6 + i) * CY
            put_coarse(a, c, i, averaged[at : at + CY], low)
    has_left = jnp.where(slab > 0, f32(1.0), f32(0.0))
    has_right = jnp.where(slab < SLABS - 1, f32(1.0), f32(0.0))
    limits = lambda i: has_left if i < 2 else has_right if i >= 4 else None
    coarse_step(a, b, 1, 5, limits)
    coarse_step(b, a, 2, 4, limits, False)
    for c in range(3):
        for i in range(2):
            out_ref[c, i] = a[c, 2 + i, 8 : CY + 8, :]


def first_coarse(left, mid, right):
    buffer = pltpu.VMEM((3, 6, CY + 16, NZ), f32)
    return pl.pallas_call(
        first_coarse_kernel,
        out_shape=jax.ShapeDtypeStruct((3, 2, CY, NZ), f32),
        in_specs=[VMEM, VMEM, VMEM],
        out_specs=VMEM,
        scratch_shapes=[buffer, buffer, pltpu.VMEM((18 * CY, 256), f32)],
        compiler_params=PARAMS,
        cost_estimate=pl.CostEstimate(flops=4_000_000, bytes_accessed=1_300_000, transcendentals=0),
        name="first_coarse",
    )(left, mid, right)


def change_kernel(ends_ref, oc_ref, out_ref):
    expand = one_to_pairs()
    for c in range(3):
        for p in range(2):
            wide = dot(oc_ref[c, p], expand)
            tall = jnp.concatenate([wide[:, :NZ], wide[:, NZ:]], axis=0)
            for i in (2 * p, 2 * p + 1):
                for start in (0, 1):
                    at = pl.ds(start, 32, stride=2)
                    out_ref[c, i, at, :] = ends_ref[c, i, at, :] - tall


def fine_change(ends, oc):
    return pl.pallas_call(
        change_kernel,
        out_shape=jax.ShapeDtypeStruct(ends.shape, f32),
        in_specs=[VMEM, VMEM],
        out_specs=VMEM,
        compiler_params=PARAMS,
        cost_estimate=pl.CostEstimate(flops=1_000_000, bytes_accessed=900_000, transcendentals=0),
        name="fine_change",
    )(ends, oc)


def halves(count):
    outer = count - 2
    first = min(outer, 4)
    for i in range(first):
        yield 0, i, outer - first + i
        yield 1, i, outer + 4 + i
    for i in range(outer - first):
        yield 0, first + i, i
        yield 1, first + i, outer + 4 + first + i
    for i in range(2):
        yield 0, outer + i, outer + i
        yield 1, outer + i, outer + 2 + i


def sweep_kernel(target, depth, *refs):
    got_ref, before_ref, own_ref, *kept = refs[: 3 + depth]
    state_ref, *results = refs[3 + depth : 4 + 2 * depth]
    a, b = refs[4 + 2 * depth :]
    group, slab = position()
    core = slab & 1
    mine = group == target
    low = lanes() < 64
    reach = 2 * depth
    width = 2 * reach + 4
    for core_at, at, place in halves(reach + 2):
        for c in range(3):
            put_coarse(a, c, place, got_ref[core_at, c, at], low)
    chip = slab >> 1
    inside = {}
    for k in range(-reach, reach + 4):
        block = k // 4
        if block not in inside:
            there = chip + block
            inside[block] = None if block == 0 else jnp.where((there >= 0) & (there < SLABS // 2), f32(1.0), f32(0.0))
    limits = lambda i: inside[(i - reach) // 4]
    at_before = 0
    for turn in range(depth):
        edge = 2 * turn
        final_turn = turn == depth - 1
        coarse_step(a, b, edge + 1, width - edge - 1, limits)
        coarse_step(b, a, edge + 2, width - edge - 2, limits, False)
        for c in range(3):
            for i in range(2):
                value = jnp.where(core == 0, a[c, reach + i, 8 : CY + 8, :], a[c, reach + 2 + i, 8 : CY + 8, :])
                results[turn][c, i] = jnp.where(mine, value, kept[turn][c, i])
        if final_turn:
            for c in range(3):
                for i in range(4):
                    state_ref[c, i] = a[c, reach + i, 8 : CY + 8, :] + own_ref[c, i]
        else:
            count = reach - edge
            for core_at, at, place in halves(count):
                for c in range(3):
                    i = place + edge + 2
                    put_coarse(a, c, i, a[c, i, 8 : CY + 8, :] + before_ref[core_at, c, at_before + at], low)
            at_before += count


def sweep(target, depth, got, before, own, kept):
    buffer = pltpu.VMEM((3, 4 * depth + 4, CY + 16, NZ), f32)
    two = jax.ShapeDtypeStruct((3, 2, CY, NZ), f32)
    four = jax.ShapeDtypeStruct((3, 4, CY, NZ), f32)
    return pl.pallas_call(
        functools.partial(sweep_kernel, target, depth),
        out_shape=(four,) + (two,) * depth,
        in_specs=[VMEM] * (3 + depth),
        out_specs=(VMEM,) * (1 + depth),
        scratch_shapes=[buffer, buffer],
        compiler_params=PARAMS,
        cost_estimate=pl.CostEstimate(flops=4_000_000, bytes_accessed=900_000, transcendentals=0),
        name="sweep_%d" % depth,
    )(got, before, own, *kept)


def final_kernel(start_ref, previous_ref, own_ref, a_ref, b_ref, c_ref, out_ref):
    group, slab = position()

    @pl.when(group == 0)
    def _():
        out_ref[...] = start_ref[...]

    @pl.when(group != 0)
    def _():
        expand = one_to_pairs()
        chain = (group & 3) == 2
        for c in range(3):
            for p in range(2):
                others = a_ref[c, p] + b_ref[c, p] + c_ref[c, p]
                wide = dot(jnp.where(chain, own_ref[c, p], others), expand)
                tall = jnp.concatenate([wide[:, :NZ], wide[:, NZ:]], axis=0)
                for i in (2 * p, 2 * p + 1):
                    for start in (0, 1):
                        at = pl.ds(start, 32, stride=2)
                        out_ref[c, i, at, :] = previous_ref[c, i, at, :] + tall


def final(*arrays):
    return pl.pallas_call(
        final_kernel,
        out_shape=jax.ShapeDtypeStruct(arrays[0].shape, f32),
        in_specs=[VMEM] * len(arrays),
        out_specs=VMEM,
        compiler_params=PARAMS,
        cost_estimate=pl.CostEstimate(flops=1_000_000, bytes_accessed=1_300_000, transcendentals=0),
        name="final",
    )(*arrays)


def handed_on(value, groups, by, place):
    table = []
    for c in groups:
        for s in range(SLABS):
            if 0 <= place(s) < SLABS and 0 <= c + by < GROUPS:
                table.append((c * SLABS + s, (c + by) * SLABS + place(s)))
    return lax.ppermute(value, AXES, table)


def outward(chips):
    return lambda s: s + 2 * chips if s % 2 == 0 else s - 2 * chips


def here(s):
    return s


def both_cores(value):
    return lax.all_gather(value, "space", axis=0, tiled=False, axis_index_groups=PAIRS)


def joined(*parts):
    return jnp.concatenate(parts, axis=1)


def after(value, *others):
    return lax.optimization_barrier((value, *others))[0]


def shards(starts):
    initial = starts[0]
    slab = lax.axis_index("space")
    core = slab & 1
    up = [(s, s + 1) for s in range(SLABS - 1)]
    down = [(s + 1, s) for s in range(SLABS - 1)]
    field = initial
    for turn in range(ROUNDS):
        left = lax.ppermute(field, "space", up)
        right = lax.ppermute(field, "space", down)
        if turn == 0:
            oc = first_coarse(left, field, right)
        if turn < ROUNDS - 1:
            field = fine_round(left, field, right)
        else:
            ends, mine = fine_round(left, field, right, oc)
    pair = both_cores(mine)
    whole = joined(pair[0], pair[1])

    def near(value):
        return jnp.where(core == 0, value[:, 2:4], value[:, 0:2])

    s1 = handed_on(whole, [0], 2, outward(1))
    s0 = handed_on(mine, [0], 2, here)
    d1 = handed_on(near(whole), [1], 1, outward(1))
    d0 = handed_on(mine, [1], 1, here)
    sources = [c for c in range(3, GROUPS - 2) if c % 4 != 2]
    l1 = handed_on(whole, sources, 0, outward(1))
    l2 = handed_on(near(whole), sources[::3], 0, outward(2))
    y3 = handed_on(joined(l1, l2, mine), sources[::3], 3, here)
    y2 = handed_on(joined(l1, mine), sources[1::3], 2, here)
    y1 = handed_on(joined(near(l1), mine), sources[2::3], 1, here)
    before = both_cores(joined(y3, y2, y1))
    change = after(fine_change(ends, oc), before)
    previous = handed_on(change, range(GROUPS), 1, here)
    s1 = after(s1, before)
    both = both_cores(joined(s1, s0, d1, d0))
    state, own, plus = sweep(2, 2, both[:, :, :6], both[:, :, 6:], whole, (oc, oc))
    minus2 = minus1 = oc
    for target in (6, 10, 14):
        half = jnp.where(core == 0, state[:, :2], state[:, 2:])
        s2 = handed_on(state, [target - 4], 4, outward(2))
        s1 = handed_on(state, [target - 4], 4, outward(1))
        s0 = handed_on(half, [target - 4], 4, here)
        both = both_cores(joined(s1, s2, s0))
        state, minus2, minus1, own, plus = sweep(target, 4, both, before, whole, (minus2, minus1, own, plus))
    plus = handed_on(plus, [0, 2, 6, 10, 14], 1, here)
    minus1 = handed_on(minus1, [6, 10, 14], -1, here)
    minus2 = handed_on(minus2, [6, 10, 14], -2, here)
    return final(initial, previous, own, plus, minus1, minus2)[None]


def solution(mesh):
    placed = P("cuts", None, "space", None, None)
    return jax.shard_map(shards, mesh=mesh, in_specs=(placed,), out_specs=placed, check_vma=False)
```

time: 203 us -> 189 us (0.931)
  the two profiles are of different devices: /device:TPU:124 before, /device:TPU:102 now
where the time goes in v2:
time: 189 us; the launch traced here: 188 us
  waiting for transfers between devices  97.9 us (52%)
  starting transfers between devices  48.4 us (26%)
  Pallas kernels  27.2 us (14%)
  blocking collectives  13.1 us (7%)
    ppermute x22, waiting for transfers between devices, handed_on(): return lax.ppermute(value, AXES, table)  45 us
    ppermute x4, waiting for transfers between devices, shards(): left = lax.ppermute(field, 'space', up)  39.9 us
    ppermute x22, starting transfers between devices, handed_on(): return lax.ppermute(value, AXES, table)  23.7 us
    pallas_call x4, Pallas kernels, sweep(): pl.pallas_call(functools.partial(sweep_kernel, target, depth), out_shape=...  17.9 us
    ppermute x4, starting transfers between devices, shards(): right = lax.ppermute(field, 'space', down)  15.6 us
    all_gather x6, blocking collectives, both_cores(): lax.all_gather(value, 'space', axis=0, tiled=False, axis_index_groups=PAIRS)  13.1 us
    ppermute x4, waiting for transfers between devices, shards(): right = lax.ppermute(field, 'space', down)  13.1 us
    ppermute x4, starting transfers between devices, shards(): left = lax.ppermute(field, 'space', up)  9.14 us
  transfers between devices with their start and end apart: 30, of which 11 were waited for; matrix products, arithmetic and copies ran while one was open for 0% of the time, Pallas kernels for 6%

profile of v2, /device:TPU:102, one launch (start us, length us, event | category | flops | bytes accessed | tf_op | source)
XLA Modules:
  0.0 188.5 jit_solution(16664710626968482444)
XLA Ops:
  0.0 9.7 %collective-permute-start.1 = (f32[3,4,64,128]{3,2,1,0:T(8,128)}, f32[3,4,64,128]{3,2,1,0:T(8,128)S(1)}, u32[]{:S(2)}, u32[]{:S(2)}) collective-permute-start(f32[3,4,64,128]{3,2,1,0:T(8,128)} %bitcast.10), channel_id=1, source_target_pairs={{1,0},{2,1},{3,2},{4,3},{5,4},{6,5},{7,6},{8,7},{9,8},{10,9},{11,1... | collective-permute-start | bytes 1179656 | tf_op jit(solution)/shard_map/ppermute | solution.py:376
  9.7 1.9 %collective-permute-start = (f32[3,4,64,128]{3,2,1,0:T(8,128)}, f32[3,4,64,128]{3,2,1,0:T(8,128)S(1)}, u32[]{:S(2)}, u32[]{:S(2)}) collective-permute-start(f32[3,4,64,128]{3,2,1,0:T(8,128)} %bitcast.11), channel_id=1, source_target_pairs={{0,1},{1,2},{2,3},{3,4},{4,5},{5,6},{6,7},{7,8},{8,9},{9,10},{10,1... | collective-permute-start | bytes 1179656 | tf_op jit(solution)/shard_map/ppermute | solution.py:375
  11.7 5.0 %collective-permute-done.1.right_ref = f32[3,4,64,128]{3,2,1,0:T(8,128)S(1)} collective-permute-done((f32[3,4,64,128]{3,2,1,0:T(8,128)}, f32[3,4,64,128]{3,2,1,0:T(8,128)S(1)}, u32[]{:S(2)}, u32[]{:S(2)}) %collective-permute-start.1) | collective-permute-done | bytes 393248 | tf_op jit(solution)/shard_map/ppermute | solution.py:376
  16.7 9.6 %collective-permute-done.left_ref = f32[3,4,64,128]{3,2,1,0:T(8,128)S(1)} collective-permute-done((f32[3,4,64,128]{3,2,1,0:T(8,128)}, f32[3,4,64,128]{3,2,1,0:T(8,128)S(1)}, u32[]{:S(2)}, u32[]{:S(2)}) %collective-permute-start) | collective-permute-done | bytes 393248 | tf_op jit(solution)/shard_map/ppermute | solution.py:375
  27.3 1.7 fine_steps.3.mid_ref
  28.9 1.9 %collective-permute-start.3 = (f32[3,4,64,128]{3,2,1,0:T(8,128)S(1)}, f32[3,4,64,128]{3,2,1,0:T(8,128)S(1)}, u32[]{:S(2)}, u32[]{:S(2)}) collective-permute-start(f32[3,4,64,128]{3,2,1,0:T(8,128)S(1)} %fine_steps.3.mid_ref), channel_id=1, source_target_pairs={{1,0},{2,1},{3,2},{4,3},{5,4},{6,5},{7,6},{8,7},{9,8},{10,9},{11,1... | collective-permute-start | bytes 1179656 | tf_op jit(solution)/shard_map/ppermute | solution.py:376
  30.9 2.4 %collective-permute-start.2 = (f32[3,4,64,128]{3,2,1,0:T(8,128)S(1)}, f32[3,4,64,128]{3,2,1,0:T(8,128)S(1)}, u32[]{:S(2)}, u32[]{:S(2)}) collective-permute-start(f32[3,4,64,128]{3,2,1,0:T(8,128)S(1)} %fine_steps.3.mid_ref), channel_id=1, source_target_pairs={{0,1},{1,2},{2,3},{3,4},{4,5},{5,6},{6,7},{7,8},{8,9},{9,10},{10,1... | collective-permute-start | bytes 1179656 | tf_op jit(solution)/shard_map/ppermute | solution.py:375
  33.3 2.9 %collective-permute-done.3.right_ref = f32[3,4,64,128]{3,2,1,0:T(8,128)S(1)} collective-permute-done((f32[3,4,64,128]{3,2,1,0:T(8,128)S(1)}, f32[3,4,64,128]{3,2,1,0:T(8,128)S(1)}, u32[]{:S(2)}, u32[]{:S(2)}) %collective-permute-start.3) | collective-permute-done | bytes 393248 | tf_op jit(solution)/shard_map/ppermute | solution.py:376
  36.2 11.0 %collective-permute-done.2.left_ref = f32[3,4,64,128]{3,2,1,0:T(8,128)S(1)} collective-permute-done((f32[3,4,64,128]{3,2,1,0:T(8,128)S(1)}, f32[3,4,64,128]{3,2,1,0:T(8,128)S(1)}, u32[]{:S(2)}, u32[]{:S(2)}) %collective-permute-start.2) | collective-permute-done | bytes 393248 | tf_op jit(solution)/shard_map/ppermute | solution.py:375
  48.9 2.1 %collective-permute-start.5 = (f32[3,4,64,128]{3,2,1,0:T(8,128)S(1)}, f32[3,4,64,128]{3,2,1,0:T(8,128)S(1)}, u32[]{:S(2)}, u32[]{:S(2)}) collective-permute-start(f32[3,4,64,128]{3,2,1,0:T(8,128)S(1)} %fine_steps.4.mid_ref), channel_id=1, source_target_pairs={{1,0},{2,1},{3,2},{4,3},{5,4},{6,5},{7,6},{8,7},{9,8},{10,9},{11,1... | collective-permute-start | bytes 1179656 | tf_op jit(solution)/shard_map/ppermute | solution.py:376
  50.9 2.4 %collective-permute-start.4 = (f32[3,4,64,128]{3,2,1,0:T(8,128)S(1)}, f32[3,4,64,128]{3,2,1,0:T(8,128)S(1)}, u32[]{:S(2)}, u32[]{:S(2)}) collective-permute-start(f32[3,4,64,128]{3,2,1,0:T(8,128)S(1)} %fine_steps.4.mid_ref), channel_id=1, source_target_pairs={{0,1},{1,2},{2,3},{3,4},{4,5},{5,6},{6,7},{7,8},{8,9},{9,10},{10,1... | collective-permute-start | bytes 1179656 | tf_op jit(solution)/shard_map/ppermute | solution.py:375
  53.3 2.9 %collective-permute-done.5.right_ref = f32[3,4,64,128]{3,2,1,0:T(8,128)S(1)} collective-permute-done((f32[3,4,64,128]{3,2,1,0:T(8,128)S(1)}, f32[3,4,64,128]{3,2,1,0:T(8,128)S(1)}, u32[]{:S(2)}, u32[]{:S(2)}) %collective-permute-start.5) | collective-permute-done | bytes 393248 | tf_op jit(solution)/shard_map/ppermute | solution.py:376
  56.2 10.9 %collective-permute-done.4.left_ref = f32[3,4,64,128]{3,2,1,0:T(8,128)S(1)} collective-permute-done((f32[3,4,64,128]{3,2,1,0:T(8,128)S(1)}, f32[3,4,64,128]{3,2,1,0:T(8,128)S(1)}, u32[]{:S(2)}, u32[]{:S(2)}) %collective-permute-start.4) | collective-permute-done | bytes 393248 | tf_op jit(solution)/shard_map/ppermute | solution.py:375
  68.8 1.9 %collective-permute-start.7 = (f32[3,4,64,128]{3,2,1,0:T(8,128)S(1)}, f32[3,4,64,128]{3,2,1,0:T(8,128)S(1)}, u32[]{:S(2)}, u32[]{:S(2)}) collective-permute-start(f32[3,4,64,128]{3,2,1,0:T(8,128)S(1)} %fine_steps.5.mid_ref), channel_id=1, source_target_pairs={{1,0},{2,1},{3,2},{4,3},{5,4},{6,5},{7,6},{8,7},{9,8},{10,9},{11,1... | collective-permute-start | bytes 1179656 | tf_op jit(solution)/shard_map/ppermute | solution.py:376
  70.8 2.4 %collective-permute-start.6 = (f32[3,4,64,128]{3,2,1,0:T(8,128)S(1)}, f32[3,4,64,128]{3,2,1,0:T(8,128)S(1)}, u32[]{:S(2)}, u32[]{:S(2)}) collective-permute-start(f32[3,4,64,128]{3,2,1,0:T(8,128)S(1)} %fine_steps.5.mid_ref), channel_id=1, source_target_pairs={{0,1},{1,2},{2,3},{3,4},{4,5},{5,6},{6,7},{7,8},{8,9},{9,10},{10,1... | collective-permute-start | bytes 1179656 | tf_op jit(solution)/shard_map/ppermute | solution.py:375
  73.8 2.3 %collective-permute-done.7.right_ref = f32[3,4,64,128]{3,2,1,0:T(8,128)S(1)} collective-permute-done((f32[3,4,64,128]{3,2,1,0:T(8,128)S(1)}, f32[3,4,64,128]{3,2,1,0:T(8,128)S(1)}, u32[]{:S(2)}, u32[]{:S(2)}) %collective-permute-start.7) | collective-permute-done | bytes 393248 | tf_op jit(solution)/shard_map/ppermute | solution.py:376
  76.1 8.4 %collective-permute-done.6.left_ref = f32[3,4,64,128]{3,2,1,0:T(8,128)S(1)} collective-permute-done((f32[3,4,64,128]{3,2,1,0:T(8,128)S(1)}, f32[3,4,64,128]{3,2,1,0:T(8,128)S(1)}, u32[]{:S(2)}, u32[]{:S(2)}) %collective-permute-start.6) | collective-permute-done | bytes 393248 | tf_op jit(solution)/shard_map/ppermute | solution.py:375
  84.5 2.0 %fine_last.1 = (f32[3,4,64,128]{3,2,1,0:T(8,128)S(1)}, f32[3,2,16,128]{3,2,1,0:T(8,128)S(1)}) custom-call(f32[3,4,64,128]{3,2,1,0:T(8,128)S(1)} %collective-permute-done.6.left_ref, f32[3,4,64,128]{3,2,1,0:T(8,128)S(1)} %fine_steps.5.mid_ref, f32[3,4,64,128]{3,2,1,0:T(8,128)S(1)} %collective-permute-done.7.right_ref, ...), custom_call_target="tpu_custom_call" | custom-call | flops 40000000 | bytes 2000000 | tf_op jit(solution)/shard_map/fine_last/pallas_call | solution.py:157
  86.5 1.9 all-gather
  88.4 1.9 %collective-permute-start.8 = (f32[3,4,16,128]{3,2,1,0:T(8,128)S(1)}, f32[3,4,16,128]{3,2,1,0:T(8,128)S(1)}, u32[]{:S(2)}, u32[]{:S(2)}) collective-permute-start(f32[3,4,16,128]{3,2,1,0:T(8,128)S(1)} %pad_maximum_fusion.7.refs_2_), channel_id=1, source_target_pairs={{96,98},{98,100},{99,97},{100,102},{101,99},{102,104},{103,101},{1... | collective-permute-start | bytes 294920 | tf_op jit(solution)/shard_map/ppermute | solution.py:344
  91.0 6.9 %collective-permute-done.8 = f32[3,4,16,128]{3,2,1,0:T(8,128)S(1)} collective-permute-done((f32[3,4,16,128]{3,2,1,0:T(8,128)S(1)}, f32[3,4,16,128]{3,2,1,0:T(8,128)S(1)}, u32[]{:S(2)}, u32[]{:S(2)}) %collective-permute-start.8) | collective-permute-done | bytes 98336 | tf_op jit(solution)/shard_map/ppermute | solution.py:344
  104.7 2.4 %all-gather.1 = f32[6,18,16,128]{3,2,1,0:T(8,128)S(1)} all-gather(f32[3,18,16,128]{3,2,1,0:T(8,128)S(1)} %pad_maximum_fusion), channel_id=3, replica_groups={{0,1},{2,3},{4,5},{6,7},{8,9},{10,11},{12,13},{14,15},{16,17},{18,19},{..., dimensions={0}, use_global_device_ids=true | all-gather | bytes 1327104 | tf_op jit(solution)/shard_map/all_gather | solution.py:356
  107.1 2.2 %all-gather.2 = f32[6,10,16,128]{3,2,1,0:T(8,128)S(1)} all-gather(f32[3,10,16,128]{3,2,1,0:T(8,128)S(1)} %pad_maximum_fusion.1), channel_id=4, replica_groups={{0,1},{2,3},{4,5},{6,7},{8,9},{10,11},{12,13},{14,15},{16,17},{18,19},{..., dimensions={0}, use_global_device_ids=true | all-gather | bytes 737280 | tf_op jit(solution)/shard_map/all_gather | solution.py:356
  109.4 1.8 sweep_2.1
  113.2 2.3 %all-gather.3 = f32[6,10,16,128]{3,2,1,0:T(8,128)S(1)} all-gather(f32[3,10,16,128]{3,2,1,0:T(8,128)S(1)} %pad_maximum_fusion.2), channel_id=5, replica_groups={{0,1},{2,3},{4,5},{6,7},{8,9},{10,11},{12,13},{14,15},{16,17},{18,19},{..., dimensions={0}, use_global_device_ids=true | all-gather | bytes 737280 | tf_op jit(solution)/shard_map/all_gather | solution.py:356
  115.6 5.2 %sweep_4.3 = (f32[3,4,16,128]{3,2,1,0:T(8,128)S(1)}, f32[3,2,16,128]{3,2,1,0:T(8,128)S(1)}, f32[3,2,16,128]{3,2,1,0:T(8,128)S(1)}, f32[3,2,16,128]{3,2,1,0:T(8,128)S(1)}, f32[3,2,16,128]{3,2,1,0:T(8,128)S(1)}) custom-call(f32[2,3,10,16,128]{4,3,2,1,0:T(8,128)S(1)} %bitcast.17, f32[2,3,18,16,128]{4,3,2,1,0:T(8,128)S(1)} %bitcast.7, ...), custom_call_target="tpu_custom_call" | custom-call | flops 4000000 | bytes 900000 | tf_op jit(solution)/shard_map/sweep_4/pallas_call | solution.py:292
  123.2 7.2 %collective-permute-start.13 = (f32[3,4,64,128]{3,2,1,0:T(8,128)S(1)}, f32[3,4,64,128]{3,2,1,0:T(8,128)S(1)}, u32[]{:S(2)}, u32[]{:S(2)}) collective-permute-start(f32[3,4,64,128]{3,2,1,0:T(8,128)S(1)} %fine_change.1), channel_id=1, source_target_pairs={{0,32},{1,33},{2,34},{3,35},{4,36},{5,37},{6,38},{7,39},{8,40},{9,... | collective-permute-start | bytes 1179656 | tf_op jit(solution)/shard_map/ppermute | solution.py:344
  130.5 2.2 %all-gather.4 = f32[6,10,16,128]{3,2,1,0:T(8,128)S(1)} all-gather(f32[3,10,16,128]{3,2,1,0:T(8,128)S(1)} %pad_maximum_fusion.3), channel_id=6, replica_groups={{0,1},{2,3},{4,5},{6,7},{8,9},{10,11},{12,13},{14,15},{16,17},{18,19},{..., dimensions={0}, use_global_device_ids=true | all-gather | bytes 737280 | tf_op jit(solution)/shard_map/all_gather | solution.py:356
  132.7 5.2 %sweep_4.4 = (f32[3,4,16,128]{3,2,1,0:T(8,128)S(1)}, f32[3,2,16,128]{3,2,1,0:T(8,128)S(1)}, f32[3,2,16,128]{3,2,1,0:T(8,128)S(1)}, f32[3,2,16,128]{3,2,1,0:T(8,128)S(1)}, f32[3,2,16,128]{3,2,1,0:T(8,128)S(1)}) custom-call(f32[2,3,10,16,128]{4,3,2,1,0:T(8,128)S(1)} %bitcast.16, f32[2,3,18,16,128]{4,3,2,1,0:T(8,128)S(1)} %bitcast.8, ...), custom_call_target="tpu_custom_call" | custom-call | flops 4000000 | bytes 900000 | tf_op jit(solution)/shard_map/sweep_4/pallas_call | solution.py:292
  139.9 2.2 %all-gather.5 = f32[6,10,16,128]{3,2,1,0:T(8,128)S(1)} all-gather(f32[3,10,16,128]{3,2,1,0:T(8,128)S(1)} %pad_maximum_fusion.4), channel_id=7, replica_groups={{0,1},{2,3},{4,5},{6,7},{8,9},{10,11},{12,13},{14,15},{16,17},{18,19},{..., dimensions={0}, use_global_device_ids=true | all-gather | bytes 737280 | tf_op jit(solution)/shard_map/all_gather | solution.py:356
  142.1 5.8 %sweep_4.5 = (f32[3,4,16,128]{3,2,1,0:T(8,128)}, f32[3,2,16,128]{3,2,1,0:T(8,128)S(1)}, f32[3,2,16,128]{3,2,1,0:T(8,128)S(1)}, f32[3,2,16,128]{3,2,1,0:T(8,128)S(1)}, f32[3,2,16,128]{3,2,1,0:T(8,128)S(1)}) custom-call(f32[2,3,10,16,128]{4,3,2,1,0:T(8,128)S(1)} %bitcast.15, f32[2,3,18,16,128]{4,3,2,1,0:T(8,128)S(1)} %bitcast.9, ...), custom_call_target="tpu_custom_call" | custom-call | flops 4000000 | bytes 900000 | tf_op jit(solution)/shard_map/sweep_4/pallas_call | solution.py:292
  150.6 36.7 %collective-permute-done.29.c_ref = f32[3,2,16,128]{3,2,1,0:T(8,128)S(1)} collective-permute-done((f32[3,2,16,128]{3,2,1,0:T(8,128)S(1)}, f32[3,2,16,128]{3,2,1,0:T(8,128)S(1)}, u32[]{:S(2)}, u32[]{:S(2)}) %collective-permute-start.29) | collective-permute-done | bytes 49184 | tf_op jit(solution)/shard_map/ppermute | solution.py:344
  (65 shorter events, 22.7 us)
Async XLA Ops:
  0.0 16.7 %collective-permute-start.1 = (f32[3,4,64,128]{3,2,1,0:T(8,128)}, f32[3,4,64,128]{3,2,1,0:T(8,128)S(1)}, u32[]{:S(2)}, u32[]{:S(2)}) collective-permute-start(f32[3,4,64,128]{3,2,1,0:T(8,128)} %bitcast.10), channel_id=1, source_target_pairs={{1,0},{2,1},{3,2},{4,3},{5,4},{6,5},{7,6},{8,7},{9,8},{10,9},{11,1... | collective-permute-start | bytes 1179656 | tf_op jit(solution)/shard_map/ppermute | solution.py:376
  9.7 16.5 %collective-permute-start = (f32[3,4,64,128]{3,2,1,0:T(8,128)}, f32[3,4,64,128]{3,2,1,0:T(8,128)S(1)}, u32[]{:S(2)}, u32[]{:S(2)}) collective-permute-start(f32[3,4,64,128]{3,2,1,0:T(8,128)} %bitcast.11), channel_id=1, source_target_pairs={{0,1},{1,2},{2,3},{3,4},{4,5},{5,6},{6,7},{7,8},{8,9},{9,10},{10,1... | collective-permute-start | bytes 1179656 | tf_op jit(solution)/shard_map/ppermute | solution.py:375
  26.3 1.0 copy-start
  28.9 7.2 %collective-permute-start.3 = (f32[3,4,64,128]{3,2,1,0:T(8,128)S(1)}, f32[3,4,64,128]{3,2,1,0:T(8,128)S(1)}, u32[]{:S(2)}, u32[]{:S(2)}) collective-permute-start(f32[3,4,64,128]{3,2,1,0:T(8,128)S(1)} %fine_steps.3.mid_ref), channel_id=1, source_target_pairs={{1,0},{2,1},{3,2},{4,3},{5,4},{6,5},{7,6},{8,7},{9,8},{10,9},{11,1... | collective-permute-start | bytes 1179656 | tf_op jit(solution)/shard_map/ppermute | solution.py:376
  30.9 16.3 %collective-permute-start.2 = (f32[3,4,64,128]{3,2,1,0:T(8,128)S(1)}, f32[3,4,64,128]{3,2,1,0:T(8,128)S(1)}, u32[]{:S(2)}, u32[]{:S(2)}) collective-permute-start(f32[3,4,64,128]{3,2,1,0:T(8,128)S(1)} %fine_steps.3.mid_ref), channel_id=1, source_target_pairs={{0,1},{1,2},{2,3},{3,4},{4,5},{5,6},{6,7},{7,8},{8,9},{9,10},{10,1... | collective-permute-start | bytes 1179656 | tf_op jit(solution)/shard_map/ppermute | solution.py:375
  48.8 24.4 %copy-start.1 = (f32[1,3,4,64,128]{4,3,2,1,0:T(8,128)S(1)}, f32[1,3,4,64,128]{4,3,2,1,0:T(8,128)}, u32[]{:S(2)}) copy-start(f32[1,3,4,64,128]{4,3,2,1,0:T(8,128)} %param.1) | copy-start | bytes 1179652
  48.9 7.4 %collective-permute-start.5 = (f32[3,4,64,128]{3,2,1,0:T(8,128)S(1)}, f32[3,4,64,128]{3,2,1,0:T(8,128)S(1)}, u32[]{:S(2)}, u32[]{:S(2)}) collective-permute-start(f32[3,4,64,128]{3,2,1,0:T(8,128)S(1)} %fine_steps.4.mid_ref), channel_id=1, source_target_pairs={{1,0},{2,1},{3,2},{4,3},{5,4},{6,5},{7,6},{8,7},{9,8},{10,9},{11,1... | collective-permute-start | bytes 1179656 | tf_op jit(solution)/shard_map/ppermute | solution.py:376
  50.9 16.2 %collective-permute-start.4 = (f32[3,4,64,128]{3,2,1,0:T(8,128)S(1)}, f32[3,4,64,128]{3,2,1,0:T(8,128)S(1)}, u32[]{:S(2)}, u32[]{:S(2)}) collective-permute-start(f32[3,4,64,128]{3,2,1,0:T(8,128)S(1)} %fine_steps.4.mid_ref), channel_id=1, source_target_pairs={{0,1},{1,2},{2,3},{3,4},{4,5},{5,6},{6,7},{7,8},{8,9},{9,10},{10,1... | collective-permute-start | bytes 1179656 | tf_op jit(solution)/shard_map/ppermute | solution.py:375
  68.8 7.2 %collective-permute-start.7 = (f32[3,4,64,128]{3,2,1,0:T(8,128)S(1)}, f32[3,4,64,128]{3,2,1,0:T(8,128)S(1)}, u32[]{:S(2)}, u32[]{:S(2)}) collective-permute-start(f32[3,4,64,128]{3,2,1,0:T(8,128)S(1)} %fine_steps.5.mid_ref), channel_id=1, source_target_pairs={{1,0},{2,1},{3,2},{4,3},{5,4},{6,5},{7,6},{8,7},{9,8},{10,9},{11,1... | collective-permute-start | bytes 1179656 | tf_op jit(solution)/shard_map/ppermute | solution.py:376
  70.8 13.7 %collective-permute-start.6 = (f32[3,4,64,128]{3,2,1,0:T(8,128)S(1)}, f32[3,4,64,128]{3,2,1,0:T(8,128)S(1)}, u32[]{:S(2)}, u32[]{:S(2)}) collective-permute-start(f32[3,4,64,128]{3,2,1,0:T(8,128)S(1)} %fine_steps.5.mid_ref), channel_id=1, source_target_pairs={{0,1},{1,2},{2,3},{3,4},{4,5},{5,6},{6,7},{7,8},{8,9},{9,10},{10,1... | collective-permute-start | bytes 1179656 | tf_op jit(solution)/shard_map/ppermute | solution.py:375
  88.4 9.5 %collective-permute-start.8 = (f32[3,4,16,128]{3,2,1,0:T(8,128)S(1)}, f32[3,4,16,128]{3,2,1,0:T(8,128)S(1)}, u32[]{:S(2)}, u32[]{:S(2)}) collective-permute-start(f32[3,4,16,128]{3,2,1,0:T(8,128)S(1)} %pad_maximum_fusion.7.refs_2_), channel_id=1, source_target_pairs={{96,98},{98,100},{99,97},{100,102},{101,99},{102,104},{103,101},{1... | collective-permute-start | bytes 294920 | tf_op jit(solution)/shard_map/ppermute | solution.py:344
  90.3 8.9 %collective-permute-start.9 = (f32[3,2,16,128]{3,2,1,0:T(8,128)S(1)}, f32[3,2,16,128]{3,2,1,0:T(8,128)S(1)}, u32[]{:S(2)}, u32[]{:S(2)}) collective-permute-start(f32[3,2,16,128]{3,2,1,0:T(8,128)S(1)} %get-tuple-element.47), channel_id=1, source_target_pairs={{96,100},{98,102},{100,104},{101,97},{102,106},{103,99},{104,108},... | collective-permute-start | bytes 147464 | tf_op jit(solution)/shard_map/ppermute | solution.py:344
  97.9 6.0 %collective-permute-start.11 = (f32[3,6,16,128]{3,2,1,0:T(8,128)S(1)}, f32[3,6,16,128]{3,2,1,0:T(8,128)S(1)}, u32[]{:S(2)}, u32[]{:S(2)}) collective-permute-start(f32[3,6,16,128]{3,2,1,0:T(8,128)S(1)} %pad_maximum_fusion.6), channel_id=1, source_target_pairs={{128,192},{129,193},{130,194},{131,195},{132,196},{133,197},{134,1... | collective-permute-start | bytes 442376 | tf_op jit(solution)/shard_map/ppermute | solution.py:344
  99.2 5.4 %collective-permute-start.10 = (f32[3,8,16,128]{3,2,1,0:T(8,128)S(1)}, f32[3,8,16,128]{3,2,1,0:T(8,128)S(1)}, u32[]{:S(2)}, u32[]{:S(2)}) collective-permute-start(f32[3,8,16,128]{3,2,1,0:T(8,128)S(1)} %pad_maximum_fusion.5), channel_id=1, source_target_pairs={{96,192},{97,193},{98,194},{99,195},{100,196},{101,197},{102,198},... | collective-permute-start | bytes 589832 | tf_op jit(solution)/shard_map/ppermute | solution.py:344
  100.0 2.0 %collective-permute-start.12 = (f32[3,4,16,128]{3,2,1,0:T(8,128)S(1)}, f32[3,4,16,128]{3,2,1,0:T(8,128)S(1)}, u32[]{:S(2)}, u32[]{:S(2)}) collective-permute-start(f32[3,4,16,128]{3,2,1,0:T(8,128)S(1)} %pad_maximum_fusion.8), channel_id=1, source_target_pairs={{160,192},{161,193},{162,194},{163,195},{164,196},{165,197},{166,1... | collective-permute-start | bytes 294920 | tf_op jit(solution)/shard_map/ppermute | solution.py:344
  100.6 6.5 %collective-permute-start.17 = (f32[3,2,16,128]{3,2,1,0:T(8,128)S(1)}, f32[3,2,16,128]{3,2,1,0:T(8,128)S(1)}, u32[]{:S(2)}, u32[]{:S(2)}) collective-permute-start(f32[3,2,16,128]{3,2,1,0:T(8,128)S(1)} %get-tuple-element.27), channel_id=1, source_target_pairs={{32,64},{33,65},{34,66},{35,67},{36,68},{37,69},{38,70},{39,71},{4... | collective-permute-start | bytes 147464 | tf_op jit(solution)/shard_map/ppermute | solution.py:344
  101.3 5.8 %collective-permute-start.15 = (f32[3,2,16,128]{3,2,1,0:T(8,128)S(1)}, f32[3,2,16,128]{3,2,1,0:T(8,128)S(1)}, u32[]{:S(2)}, u32[]{:S(2)}) collective-permute-start(f32[3,2,16,128]{3,2,1,0:T(8,128)S(1)} %get-tuple-element.27), channel_id=1, source_target_pairs={{0,64},{1,65},{2,66},{3,67},{4,68},{5,69},{6,70},{7,71},{8,72},{9,... | collective-permute-start | bytes 147464 | tf_op jit(solution)/shard_map/ppermute | solution.py:344
  102.0 5.1 %collective-permute-start.16 = (f32[3,2,16,128]{3,2,1,0:T(8,128)S(1)}, f32[3,2,16,128]{3,2,1,0:T(8,128)S(1)}, u32[]{:S(2)}, u32[]{:S(2)}) collective-permute-start(f32[3,2,16,128]{3,2,1,0:T(8,128)S(1)} %get-tuple-element.47), channel_id=1, source_target_pairs={{32,66},{34,68},{35,65},{36,70},{37,67},{38,72},{39,69},{40,74},{4... | collective-permute-start | bytes 147464 | tf_op jit(solution)/shard_map/ppermute | solution.py:344
  103.9 3.2 %collective-permute-start.14 = (f32[3,4,16,128]{3,2,1,0:T(8,128)S(1)}, f32[3,4,16,128]{3,2,1,0:T(8,128)S(1)}, u32[]{:S(2)}, u32[]{:S(2)}) collective-permute-start(f32[3,4,16,128]{3,2,1,0:T(8,128)S(1)} %pad_maximum_fusion.7.refs_2_), channel_id=1, source_target_pairs={{0,66},{2,68},{3,65},{4,70},{5,67},{6,72},{7,69},{8,74},{9,71},{10... | collective-permute-start | bytes 294920 | tf_op jit(solution)/shard_map/ppermute | solution.py:344
  111.1 2.1 %collective-permute-start.19 = (f32[3,4,16,128]{3,2,1,0:T(8,128)S(1)}, f32[3,4,16,128]{3,2,1,0:T(8,128)S(1)}, u32[]{:S(2)}, u32[]{:S(2)}) collective-permute-start(f32[3,4,16,128]{3,2,1,0:T(8,128)S(1)} %get-tuple-element.30), channel_id=1, source_target_pairs={{64,196},{66,198},{68,200},{69,193},{70,202},{71,195},{72,204},{73... | collective-permute-start | bytes 294920 | tf_op jit(solution)/shard_map/ppermute | solution.py:344
  111.8 1.4 collective-permute-start.18
  112.5 0.7 collective-permute-start.20
  120.7 9.7 %collective-permute-start.22 = (f32[3,4,16,128]{3,2,1,0:T(8,128)S(1)}, f32[3,4,16,128]{3,2,1,0:T(8,128)S(1)}, u32[]{:S(2)}, u32[]{:S(2)}) collective-permute-start(f32[3,4,16,128]{3,2,1,0:T(8,128)S(1)} %get-tuple-element.33), channel_id=1, source_target_pairs={{192,324},{194,326},{196,328},{197,321},{198,330},{199,323},{200,3... | collective-permute-start | bytes 294920 | tf_op jit(solution)/shard_map/ppermute | solution.py:344
  121.4 9.1 %collective-permute-start.21 = (f32[3,4,16,128]{3,2,1,0:T(8,128)S(1)}, f32[3,4,16,128]{3,2,1,0:T(8,128)S(1)}, u32[]{:S(2)}, u32[]{:S(2)}) collective-permute-start(f32[3,4,16,128]{3,2,1,0:T(8,128)S(1)} %get-tuple-element.33), channel_id=1, source_target_pairs={{192,322},{194,324},{195,321},{196,326},{197,323},{198,328},{199,3... | collective-permute-start | bytes 294920 | tf_op jit(solution)/shard_map/ppermute | solution.py:344
  122.1 8.3 %collective-permute-start.23 = (f32[3,2,16,128]{3,2,1,0:T(8,128)S(1)}, f32[3,2,16,128]{3,2,1,0:T(8,128)S(1)}, u32[]{:S(2)}, u32[]{:S(2)}) collective-permute-start(f32[3,2,16,128]{3,2,1,0:T(8,128)S(1)} %slice_select_fusion.2), channel_id=1, source_target_pairs={{192,320},{193,321},{194,322},{195,323},{196,324},{197,325},{198,3... | collective-permute-start | bytes 147464 | tf_op jit(solution)/shard_map/ppermute | solution.py:344
  123.2 64.1 %collective-permute-start.13 = (f32[3,4,64,128]{3,2,1,0:T(8,128)S(1)}, f32[3,4,64,128]{3,2,1,0:T(8,128)S(1)}, u32[]{:S(2)}, u32[]{:S(2)}) collective-permute-start(f32[3,4,64,128]{3,2,1,0:T(8,128)S(1)} %fine_change.1), channel_id=1, source_target_pairs={{0,32},{1,33},{2,34},{3,35},{4,36},{5,37},{6,38},{7,39},{8,40},{9,... | collective-permute-start | bytes 1179656 | tf_op jit(solution)/shard_map/ppermute | solution.py:344
  137.8 2.1 %collective-permute-start.25 = (f32[3,4,16,128]{3,2,1,0:T(8,128)S(1)}, f32[3,4,16,128]{3,2,1,0:T(8,128)S(1)}, u32[]{:S(2)}, u32[]{:S(2)}) collective-permute-start(f32[3,4,16,128]{3,2,1,0:T(8,128)S(1)} %get-tuple-element.38), channel_id=1, source_target_pairs={{320,452},{322,454},{324,456},{325,449},{326,458},{327,451},{328,4... | collective-permute-start | bytes 294920 | tf_op jit(solution)/shard_map/ppermute | solution.py:344
  138.5 1.4 collective-permute-start.24
  139.2 0.7 collective-permute-start.26
  147.9 2.6 %collective-permute-start.27 = (f32[3,2,16,128]{3,2,1,0:T(8,128)S(1)}, f32[3,2,16,128]{3,2,1,0:T(8,128)S(1)}, u32[]{:S(2)}, u32[]{:S(2)}) collective-permute-start(f32[3,2,16,128]{3,2,1,0:T(8,128)S(1)} %get-tuple-element.44), channel_id=1, source_target_pairs={{0,32},{1,33},{2,34},{3,35},{4,36},{5,37},{6,38},{7,39},{8,40},{9,... | collective-permute-start | bytes 147464 | tf_op jit(solution)/shard_map/ppermute | solution.py:344
  148.6 2.0 %collective-permute-start.28 = (f32[3,2,16,128]{3,2,1,0:T(8,128)S(1)}, f32[3,2,16,128]{3,2,1,0:T(8,128)S(1)}, u32[]{:S(2)}, u32[]{:S(2)}) collective-permute-start(f32[3,2,16,128]{3,2,1,0:T(8,128)S(1)} %get-tuple-element.45), channel_id=1, source_target_pairs={{192,160},{193,161},{194,162},{195,163},{196,164},{197,165},{198,1... | collective-permute-start | bytes 147464 | tf_op jit(solution)/shard_map/ppermute | solution.py:344
  149.2 38.0 %collective-permute-start.29 = (f32[3,2,16,128]{3,2,1,0:T(8,128)S(1)}, f32[3,2,16,128]{3,2,1,0:T(8,128)S(1)}, u32[]{:S(2)}, u32[]{:S(2)}) collective-permute-start(f32[3,2,16,128]{3,2,1,0:T(8,128)S(1)} %get-tuple-element.46), channel_id=1, source_target_pairs={{192,128},{193,129},{194,130},{195,131},{196,132},{197,133},{198,1... | collective-permute-start | bytes 147464 | tf_op jit(solution)/shard_map/ppermute | solution.py:344

commit v3 on v2

--- a/solution.py
+++ b/solution.py
@@ -61,26 +61,51 @@
     return lax.broadcasted_iota(jnp.int32, shape, 1)
 
 
-def guards(dst, c, i, first, last, low):
-    dst[c, i, 7:8, :] = jnp.where(low, 0.0, pltpu.roll(last, 64, 1))[7:8, :]
-    dst[c, i, CY + 8 : CY + 9, :] = jnp.where(low, pltpu.roll(first, 64, 1), 0.0)[0:1, :]
-
-
-def put_coarse(dst, c, i, plane, low):
-    dst[c, i, 8 : CY + 8, :] = plane
-    guards(dst, c, i, plane[:8], plane[8:], low)
-
-
-def coarse_step(src, dst, begin, end, limits, guarded=True):
+def coarse_plane(at, put, i, factor):
     lane = lanes()
-    left = (lane & 63) == 0
-    right = (lane & 63) == 63
-    low = lane < 64
+    row = lax.broadcasted_iota(jnp.int32, (8, 128), 0)
+    z_first, z_last = (lane & 63) == 0, (lane & 63) == 63
+    y_first, y_last = (row == 0) & (lane < 64), (row == 7) & (lane >= 64)
+    row_first, row_last = row == 0, row == 7
+    v = [[at(c, i, j) for j in range(2)] for c in range(3)]
+    for j in range(2):
+        av = [coarse_advect * v[c][j] for c in range(3)]
+        xp, xm = coarse_rate - av[0], coarse_rate + av[0]
+        yp, ym = coarse_rate - av[1], coarse_rate + av[1]
+        if j == 0:
+            ym = jnp.where(y_first, 0.0, ym)
+        else:
+            yp = jnp.where(y_last, 0.0, yp)
+        zp = jnp.where(z_last, 0.0, coarse_rate - av[2])
+        zm = jnp.where(z_first, 0.0, coarse_rate + av[2])
+        for c in range(3):
+            here_, other = v[c][j], v[c][1 - j]
+            swapped = pltpu.roll(other, 64, 1)
+            below = jnp.where(row_last, swapped if j == 0 else other, here_)
+            above = jnp.where(row_first, other if j == 0 else swapped, here_)
+            new = here_ * (1.0 - 6.0 * coarse_rate)
+            new += xp * at(c, i + 1, j) + xm * at(c, i - 1, j)
+            new += yp * pltpu.roll(above, 7, 0) + ym * pltpu.roll(below, 1, 0)
+            new += zp * pltpu.roll(here_, 127, 1) + zm * pltpu.roll(here_, 1, 1)
+            if factor is not None:
+                new = new * factor
+            put(c, i, j, new)
+
+
+def reads(ref):
+    return lambda c, i, j: ref[c, i, 8 * j : 8 * j + 8, :]
+
+
+def writes(ref):
+    def put(c, i, j, value):
+        ref[c, i, 8 * j : 8 * j + 8, :] = value
+
+    return put
+
+
+def coarse_step(at, put, begin, end, limits):
     for i in range(begin, end):
-        first, last = one_plane(src, dst, i, CY, coarse_rate, coarse_advect, limits(i), left, right)
-        if guarded:
-            for c in range(3):
-                guards(dst, c, i, first[c], last[c], low)
+        coarse_plane(at, put, i, limits(i))
 
 
 def pairs_to_one(scale):
@@ -174,23 +199,20 @@
             for p in range(2):
                 sums[pl.ds((c * 6 + part * 2 + p) * CY, CY), :] = rows(c, p)
     averaged = dot(sums[...], pairs_to_one(0.125))
-    low = lanes() < 64
     for c in range(3):
         for i in range(6):
             at = (c * 6 + i) * CY
-            put_coarse(a, c, i, averaged[at : at + CY], low)
+            a[c, i] = averaged[at : at + CY]
     has_left = jnp.where(slab > 0, f32(1.0), f32(0.0))
     has_right = jnp.where(slab < SLABS - 1, f32(1.0), f32(0.0))
     limits = lambda i: has_left if i < 2 else has_right if i >= 4 else None
-    coarse_step(a, b, 1, 5, limits)
-    coarse_step(b, a, 2, 4, limits, False)
-    for c in range(3):
-        for i in range(2):
-            out_ref[c, i] = a[c, 2 + i, 8 : CY + 8, :]
+    coarse_step(reads(a), writes(b), 1, 5, limits)
+    into = writes(out_ref)
+    coarse_step(reads(b), lambda c, i, j, value: into(c, i - 2, j, value), 2, 4, limits)
 
 
 def first_coarse(left, mid, right):
-    buffer = pltpu.VMEM((3, 6, CY + 16, NZ), f32)
+    buffer = pltpu.VMEM((3, 6, CY, NZ), f32)
     return pl.pallas_call(
         first_coarse_kernel,
         out_shape=jax.ShapeDtypeStruct((3, 2, CY, NZ), f32),
@@ -248,12 +270,14 @@
     group, slab = position()
     core = slab & 1
     mine = group == target
-    low = lanes() < 64
     reach = 2 * depth
     width = 2 * reach + 4
-    for core_at, at, place in halves(reach + 2):
-        for c in range(3):
-            put_coarse(a, c, place, got_ref[core_at, c, at], low)
+    source = {place: (core_at, at) for core_at, at, place in halves(reach + 2)}
+
+    def got(c, i, j):
+        core_at, at = source[i]
+        return got_ref[core_at, c, at, 8 * j : 8 * j + 8, :]
+
     chip = slab >> 1
     inside = {}
     for k in range(-reach, reach + 4):
@@ -265,28 +289,27 @@
     at_before = 0
     for turn in range(depth):
         edge = 2 * turn
-        final_turn = turn == depth - 1
-        coarse_step(a, b, edge + 1, width - edge - 1, limits)
-        coarse_step(b, a, edge + 2, width - edge - 2, limits, False)
+        coarse_step(reads(a) if turn else got, writes(b), edge + 1, width - edge - 1, limits)
+        coarse_step(reads(b), writes(a), edge + 2, width - edge - 2, limits)
         for c in range(3):
             for i in range(2):
-                value = jnp.where(core == 0, a[c, reach + i, 8 : CY + 8, :], a[c, reach + 2 + i, 8 : CY + 8, :])
+                value = jnp.where(core == 0, a[c, reach + i], a[c, reach + 2 + i])
                 results[turn][c, i] = jnp.where(mine, value, kept[turn][c, i])
-        if final_turn:
+        if turn == depth - 1:
             for c in range(3):
                 for i in range(4):
-                    state_ref[c, i] = a[c, reach + i, 8 : CY + 8, :] + own_ref[c, i]
+                    state_ref[c, i] = a[c, reach + i] + own_ref[c, i]
         else:
             count = reach - edge
             for core_at, at, place in halves(count):
                 for c in range(3):
                     i = place + edge + 2
-                    put_coarse(a, c, i, a[c, i, 8 : CY + 8, :] + before_ref[core_at, c, at_before + at], low)
+                    a[c, i] = a[c, i] + before_ref[core_at, c, at_before + at]
             at_before += count
 
 
 def sweep(target, depth, got, before, own, kept):
-    buffer = pltpu.VMEM((3, 4 * depth + 4, CY + 16, NZ), f32)
+    buffer = pltpu.VMEM((3, 4 * depth + 4, CY, NZ), f32)
     two = jax.ShapeDtypeStruct((3, 2, CY, NZ), f32)
     four = jax.ShapeDtypeStruct((3, 4, CY, NZ), f32)
     return pl.pallas_call(
@@ -396,18 +419,20 @@
     y3 = handed_on(joined(l1, l2, mine), sources[::3], 3, here)
     y2 = handed_on(joined(l1, mine), sources[1::3], 2, here)
     y1 = handed_on(joined(near(l1), mine), sources[2::3], 1, here)
-    before = both_cores(joined(y3, y2, y1))
-    change = after(fine_change(ends, oc), before)
-    previous = handed_on(change, range(GROUPS), 1, here)
-    s1 = after(s1, before)
     both = both_cores(joined(s1, s0, d1, d0))
     state, own, plus = sweep(2, 2, both[:, :, :6], both[:, :, 6:], whole, (oc, oc))
     minus2 = minus1 = oc
+    before = None
     for target in (6, 10, 14):
         half = jnp.where(core == 0, state[:, :2], state[:, 2:])
         s2 = handed_on(state, [target - 4], 4, outward(2))
         s1 = handed_on(state, [target - 4], 4, outward(1))
         s0 = handed_on(half, [target - 4], 4, here)
+        if before is None:
+            before = both_cores(joined(after(y3, state), y2, y1))
+            change = after(fine_change(ends, oc), before)
+            previous = handed_on(change, range(GROUPS), 1, here)
+            s1 = after(s1, before)
         both = both_cores(joined(s1, s2, s0))
         state, minus2, minus1, own, plus = sweep(target, 4, both, before, whole, (minus2, minus1, own, plus))
     plus = handed_on(plus, [0, 2, 6, 10, 14], 1, here)

time: 189 us -> 170 us (0.90)
  Pallas kernels: 27.2 us -> 15.9 us
  starting transfers between devices: 48.4 us -> 43.2 us
  waiting for transfers between devices: 97.9 us -> 95.6 us
    pallas_call x4, Pallas kernels: 17.9 us -> 6.67 us  [sweep(): pl.pallas_call(functools.partial(sweep_kernel, target, depth), out_shape=...]
    ppermute x22, starting transfers between devices: 23.7 us -> 18.4 us  [handed_on(): return lax.ppermute(value, AXES, table)]
    ppermute x22, waiting for transfers between devices: 45 us -> 42.6 us  [handed_on(): return lax.ppermute(value, AXES, table)]
  transfers between devices with their start and end apart: 30 -> 30, of which waited for: 11 -> 11; matrix products, arithmetic and copies ran while one was open for 0% -> 0% of each run, Pallas kernels for 6% -> 3%
where the time goes in v3:
time: 170 us
  waiting for transfers between devices  95.6 us (56%)
  starting transfers between devices  43.2 us (25%)
  Pallas kernels  15.9 us (9%)
  blocking collectives  13.1 us (8%)
    ppermute x22, waiting for transfers between devices, handed_on(): return lax.ppermute(value, AXES, table)  42.6 us
    ppermute x4, waiting for transfers between devices, shards(): left = lax.ppermute(field, 'space', up)  39.9 us
    ppermute x22, starting transfers between devices, handed_on(): return lax.ppermute(value, AXES, table)  18.4 us
    ppermute x4, starting transfers between devices, shards(): right = lax.ppermute(field, 'space', down)  15.6 us
    all_gather x6, blocking collectives, both_cores(): lax.all_gather(value, 'space', axis=0, tiled=False, axis_index_groups=PAIRS)  13.1 us
    ppermute x4, waiting for transfers between devices, shards(): right = lax.ppermute(field, 'space', down)  13.1 us
    ppermute x4, starting transfers between devices, shards(): left = lax.ppermute(field, 'space', up)  9.14 us
    pallas_call x4, Pallas kernels, fine_round(): pl.pallas_call(functools.partial(fine_kernel, last), out_shape=(shape, co...  7.04 us
  transfers between devices with their start and end apart: 30, of which 11 were waited for; matrix products, arithmetic and copies ran while one was open for 0% of the time, Pallas kernels for 3%

profile of v3, /device:TPU:102, one launch (start us, length us, event | category | flops | bytes accessed | tf_op | source)
XLA Modules:
  0.0 169.6 jit_solution(6800964511425925764)
XLA Ops:
  0.0 9.7 %collective-permute-start.1 = (f32[3,4,64,128]{3,2,1,0:T(8,128)}, f32[3,4,64,128]{3,2,1,0:T(8,128)S(1)}, u32[]{:S(2)}, u32[]{:S(2)}) collective-permute-start(f32[3,4,64,128]{3,2,1,0:T(8,128)} %bitcast.10), channel_id=1, source_target_pairs={{1,0},{2,1},{3,2},{4,3},{5,4},{6,5},{7,6},{8,7},{9,8},{10,9},{11,1... | collective-permute-start | bytes 1179656 | tf_op jit(solution)/shard_map/ppermute | solution.py:399
  9.7 1.9 %collective-permute-start = (f32[3,4,64,128]{3,2,1,0:T(8,128)}, f32[3,4,64,128]{3,2,1,0:T(8,128)S(1)}, u32[]{:S(2)}, u32[]{:S(2)}) collective-permute-start(f32[3,4,64,128]{3,2,1,0:T(8,128)} %bitcast.11), channel_id=1, source_target_pairs={{0,1},{1,2},{2,3},{3,4},{4,5},{5,6},{6,7},{7,8},{8,9},{9,10},{10,1... | collective-permute-start | bytes 1179656 | tf_op jit(solution)/shard_map/ppermute | solution.py:398
  11.7 5.0 %collective-permute-done.1.right_ref = f32[3,4,64,128]{3,2,1,0:T(8,128)S(1)} collective-permute-done((f32[3,4,64,128]{3,2,1,0:T(8,128)}, f32[3,4,64,128]{3,2,1,0:T(8,128)S(1)}, u32[]{:S(2)}, u32[]{:S(2)}) %collective-permute-start.1) | collective-permute-done | bytes 393248 | tf_op jit(solution)/shard_map/ppermute | solution.py:399
  16.7 9.6 %collective-permute-done.left_ref = f32[3,4,64,128]{3,2,1,0:T(8,128)S(1)} collective-permute-done((f32[3,4,64,128]{3,2,1,0:T(8,128)}, f32[3,4,64,128]{3,2,1,0:T(8,128)S(1)}, u32[]{:S(2)}, u32[]{:S(2)}) %collective-permute-start) | collective-permute-done | bytes 393248 | tf_op jit(solution)/shard_map/ppermute | solution.py:398
  27.3 1.7 fine_steps.3.mid_ref
  28.9 1.9 %collective-permute-start.3 = (f32[3,4,64,128]{3,2,1,0:T(8,128)S(1)}, f32[3,4,64,128]{3,2,1,0:T(8,128)S(1)}, u32[]{:S(2)}, u32[]{:S(2)}) collective-permute-start(f32[3,4,64,128]{3,2,1,0:T(8,128)S(1)} %fine_steps.3.mid_ref), channel_id=1, source_target_pairs={{1,0},{2,1},{3,2},{4,3},{5,4},{6,5},{7,6},{8,7},{9,8},{10,9},{11,1... | collective-permute-start | bytes 1179656 | tf_op jit(solution)/shard_map/ppermute | solution.py:399
  30.9 2.4 %collective-permute-start.2 = (f32[3,4,64,128]{3,2,1,0:T(8,128)S(1)}, f32[3,4,64,128]{3,2,1,0:T(8,128)S(1)}, u32[]{:S(2)}, u32[]{:S(2)}) collective-permute-start(f32[3,4,64,128]{3,2,1,0:T(8,128)S(1)} %fine_steps.3.mid_ref), channel_id=1, source_target_pairs={{0,1},{1,2},{2,3},{3,4},{4,5},{5,6},{6,7},{7,8},{8,9},{9,10},{10,1... | collective-permute-start | bytes 1179656 | tf_op jit(solution)/shard_map/ppermute | solution.py:398
  33.3 2.9 %collective-permute-done.3.right_ref = f32[3,4,64,128]{3,2,1,0:T(8,128)S(1)} collective-permute-done((f32[3,4,64,128]{3,2,1,0:T(8,128)S(1)}, f32[3,4,64,128]{3,2,1,0:T(8,128)S(1)}, u32[]{:S(2)}, u32[]{:S(2)}) %collective-permute-start.3) | collective-permute-done | bytes 393248 | tf_op jit(solution)/shard_map/ppermute | solution.py:399
  36.2 11.0 %collective-permute-done.2.left_ref = f32[3,4,64,128]{3,2,1,0:T(8,128)S(1)} collective-permute-done((f32[3,4,64,128]{3,2,1,0:T(8,128)S(1)}, f32[3,4,64,128]{3,2,1,0:T(8,128)S(1)}, u32[]{:S(2)}, u32[]{:S(2)}) %collective-permute-start.2) | collective-permute-done | bytes 393248 | tf_op jit(solution)/shard_map/ppermute | solution.py:398
  48.9 2.1 %collective-permute-start.5 = (f32[3,4,64,128]{3,2,1,0:T(8,128)S(1)}, f32[3,4,64,128]{3,2,1,0:T(8,128)S(1)}, u32[]{:S(2)}, u32[]{:S(2)}) collective-permute-start(f32[3,4,64,128]{3,2,1,0:T(8,128)S(1)} %fine_steps.4.mid_ref), channel_id=1, source_target_pairs={{1,0},{2,1},{3,2},{4,3},{5,4},{6,5},{7,6},{8,7},{9,8},{10,9},{11,1... | collective-permute-start | bytes 1179656 | tf_op jit(solution)/shard_map/ppermute | solution.py:399
  50.9 2.4 %collective-permute-start.4 = (f32[3,4,64,128]{3,2,1,0:T(8,128)S(1)}, f32[3,4,64,128]{3,2,1,0:T(8,128)S(1)}, u32[]{:S(2)}, u32[]{:S(2)}) collective-permute-start(f32[3,4,64,128]{3,2,1,0:T(8,128)S(1)} %fine_steps.4.mid_ref), channel_id=1, source_target_pairs={{0,1},{1,2},{2,3},{3,4},{4,5},{5,6},{6,7},{7,8},{8,9},{9,10},{10,1... | collective-permute-start | bytes 1179656 | tf_op jit(solution)/shard_map/ppermute | solution.py:398
  53.3 2.9 %collective-permute-done.5.right_ref = f32[3,4,64,128]{3,2,1,0:T(8,128)S(1)} collective-permute-done((f32[3,4,64,128]{3,2,1,0:T(8,128)S(1)}, f32[3,4,64,128]{3,2,1,0:T(8,128)S(1)}, u32[]{:S(2)}, u32[]{:S(2)}) %collective-permute-start.5) | collective-permute-done | bytes 393248 | tf_op jit(solution)/shard_map/ppermute | solution.py:399
  56.2 10.9 %collective-permute-done.4.left_ref = f32[3,4,64,128]{3,2,1,0:T(8,128)S(1)} collective-permute-done((f32[3,4,64,128]{3,2,1,0:T(8,128)S(1)}, f32[3,4,64,128]{3,2,1,0:T(8,128)S(1)}, u32[]{:S(2)}, u32[]{:S(2)}) %collective-permute-start.4) | collective-permute-done | bytes 393248 | tf_op jit(solution)/shard_map/ppermute | solution.py:398
  68.8 1.9 %collective-permute-start.7 = (f32[3,4,64,128]{3,2,1,0:T(8,128)S(1)}, f32[3,4,64,128]{3,2,1,0:T(8,128)S(1)}, u32[]{:S(2)}, u32[]{:S(2)}) collective-permute-start(f32[3,4,64,128]{3,2,1,0:T(8,128)S(1)} %fine_steps.5.mid_ref), channel_id=1, source_target_pairs={{1,0},{2,1},{3,2},{4,3},{5,4},{6,5},{7,6},{8,7},{9,8},{10,9},{11,1... | collective-permute-start | bytes 1179656 | tf_op jit(solution)/shard_map/ppermute | solution.py:399
  70.8 2.4 %collective-permute-start.6 = (f32[3,4,64,128]{3,2,1,0:T(8,128)S(1)}, f32[3,4,64,128]{3,2,1,0:T(8,128)S(1)}, u32[]{:S(2)}, u32[]{:S(2)}) collective-permute-start(f32[3,4,64,128]{3,2,1,0:T(8,128)S(1)} %fine_steps.5.mid_ref), channel_id=1, source_target_pairs={{0,1},{1,2},{2,3},{3,4},{4,5},{5,6},{6,7},{7,8},{8,9},{9,10},{10,1... | collective-permute-start | bytes 1179656 | tf_op jit(solution)/shard_map/ppermute | solution.py:398
  73.8 2.3 %collective-permute-done.7.right_ref = f32[3,4,64,128]{3,2,1,0:T(8,128)S(1)} collective-permute-done((f32[3,4,64,128]{3,2,1,0:T(8,128)S(1)}, f32[3,4,64,128]{3,2,1,0:T(8,128)S(1)}, u32[]{:S(2)}, u32[]{:S(2)}) %collective-permute-start.7) | collective-permute-done | bytes 393248 | tf_op jit(solution)/shard_map/ppermute | solution.py:399
  76.1 8.4 %collective-permute-done.6.left_ref = f32[3,4,64,128]{3,2,1,0:T(8,128)S(1)} collective-permute-done((f32[3,4,64,128]{3,2,1,0:T(8,128)S(1)}, f32[3,4,64,128]{3,2,1,0:T(8,128)S(1)}, u32[]{:S(2)}, u32[]{:S(2)}) %collective-permute-start.6) | collective-permute-done | bytes 393248 | tf_op jit(solution)/shard_map/ppermute | solution.py:398
  84.5 2.0 %fine_last.1 = (f32[3,4,64,128]{3,2,1,0:T(8,128)S(1)}, f32[3,2,16,128]{3,2,1,0:T(8,128)S(1)}) custom-call(f32[3,4,64,128]{3,2,1,0:T(8,128)S(1)} %collective-permute-done.6.left_ref, f32[3,4,64,128]{3,2,1,0:T(8,128)S(1)} %fine_steps.5.mid_ref, f32[3,4,64,128]{3,2,1,0:T(8,128)S(1)} %collective-permute-done.7.right_ref, ...), custom_call_target="tpu_custom_call" | custom-call | flops 40000000 | bytes 2000000 | tf_op jit(solution)/shard_map/fine_last/pallas_call | solution.py:182
  86.5 1.9 %all-gather = f32[6,2,16,128]{3,2,1,0:T(8,128)S(1)} all-gather(f32[3,2,16,128]{3,2,1,0:T(8,128)S(1)} %get-tuple-element.28), channel_id=2, replica_groups={{0,1},{2,3},{4,5},{6,7},{8,9},{10,11},{12,13},{14,15},{16,17},{18,19},{..., dimensions={0}, use_global_device_ids=true | all-gather | bytes 147456 | tf_op jit(solution)/shard_map/all_gather | solution.py:379
  91.7 1.9 %collective-permute-start.8 = (f32[3,4,16,128]{3,2,1,0:T(8,128)S(1)}, f32[3,4,16,128]{3,2,1,0:T(8,128)S(1)}, u32[]{:S(2)}, u32[]{:S(2)}) collective-permute-start(f32[3,4,16,128]{3,2,1,0:T(8,128)S(1)} %pad_maximum_fusion.7.refs_2_), channel_id=1, source_target_pairs={{96,98},{98,100},{99,97},{100,102},{101,99},{102,104},{103,101},{1... | collective-permute-start | bytes 294920 | tf_op jit(solution)/shard_map/ppermute | solution.py:367
  93.7 2.2 %all-gather.1 = f32[6,10,16,128]{3,2,1,0:T(8,128)S(1)} all-gather(f32[3,10,16,128]{3,2,1,0:T(8,128)S(1)} %pad_maximum_fusion.1), channel_id=3, replica_groups={{0,1},{2,3},{4,5},{6,7},{8,9},{10,11},{12,13},{14,15},{16,17},{18,19},{..., dimensions={0}, use_global_device_ids=true | all-gather | bytes 737280 | tf_op jit(solution)/shard_map/all_gather | solution.py:379
  95.9 5.3 %collective-permute-done.8 = f32[3,4,16,128]{3,2,1,0:T(8,128)S(1)} collective-permute-done((f32[3,4,16,128]{3,2,1,0:T(8,128)S(1)}, f32[3,4,16,128]{3,2,1,0:T(8,128)S(1)}, u32[]{:S(2)}, u32[]{:S(2)}) %collective-permute-start.8) | collective-permute-done | bytes 98336 | tf_op jit(solution)/shard_map/ppermute | solution.py:367
  106.7 3.4 %collective-permute-done.15 = f32[3,6,16,128]{3,2,1,0:T(8,128)S(1)} collective-permute-done((f32[3,6,16,128]{3,2,1,0:T(8,128)S(1)}, f32[3,6,16,128]{3,2,1,0:T(8,128)S(1)}, u32[]{:S(2)}, u32[]{:S(2)}) %collective-permute-start.15) | collective-permute-done | bytes 147488 | tf_op jit(solution)/shard_map/ppermute | solution.py:367
  110.1 2.4 %all-gather.2 = f32[6,18,16,128]{3,2,1,0:T(8,128)S(1)} all-gather(f32[3,18,16,128]{3,2,1,0:T(8,128)S(1)} %pad_maximum_fusion), channel_id=4, replica_groups={{0,1},{2,3},{4,5},{6,7},{8,9},{10,11},{12,13},{14,15},{16,17},{18,19},{..., dimensions={0}, use_global_device_ids=true | all-gather | bytes 1327104 | tf_op jit(solution)/shard_map/all_gather | solution.py:379
  112.6 2.3 %all-gather.3 = f32[6,10,16,128]{3,2,1,0:T(8,128)S(1)} all-gather(f32[3,10,16,128]{3,2,1,0:T(8,128)S(1)} %pad_maximum_fusion.2), channel_id=5, replica_groups={{0,1},{2,3},{4,5},{6,7},{8,9},{10,11},{12,13},{14,15},{16,17},{18,19},{..., dimensions={0}, use_global_device_ids=true | all-gather | bytes 737280 | tf_op jit(solution)/shard_map/all_gather | solution.py:379
  114.9 1.8 %sweep_4.3 = (f32[3,4,16,128]{3,2,1,0:T(8,128)S(1)}, f32[3,2,16,128]{3,2,1,0:T(8,128)S(1)}, f32[3,2,16,128]{3,2,1,0:T(8,128)S(1)}, f32[3,2,16,128]{3,2,1,0:T(8,128)S(1)}, f32[3,2,16,128]{3,2,1,0:T(8,128)S(1)}) custom-call(f32[2,3,10,16,128]{4,3,2,1,0:T(8,128)S(1)} %bitcast.17, f32[2,3,18,16,128]{4,3,2,1,0:T(8,128)S(1)} %bitcast.7, ...), custom_call_target="tpu_custom_call" | custom-call | flops 4000000 | bytes 900000 | tf_op jit(solution)/shard_map/sweep_4/pallas_call | solution.py:315
  119.2 1.9 %collective-permute-start.17 = (f32[3,4,64,128]{3,2,1,0:T(8,128)S(1)}, f32[3,4,64,128]{3,2,1,0:T(8,128)S(1)}, u32[]{:S(2)}, u32[]{:S(2)}) collective-permute-start(f32[3,4,64,128]{3,2,1,0:T(8,128)S(1)} %fine_change.1), channel_id=1, source_target_pairs={{0,32},{1,33},{2,34},{3,35},{4,36},{5,37},{6,38},{7,39},{8,40},{9,... | collective-permute-start | bytes 1179656 | tf_op jit(solution)/shard_map/ppermute | solution.py:367
  121.2 2.2 %all-gather.4 = f32[6,10,16,128]{3,2,1,0:T(8,128)S(1)} all-gather(f32[3,10,16,128]{3,2,1,0:T(8,128)S(1)} %pad_maximum_fusion.3), channel_id=6, replica_groups={{0,1},{2,3},{4,5},{6,7},{8,9},{10,11},{12,13},{14,15},{16,17},{18,19},{..., dimensions={0}, use_global_device_ids=true | all-gather | bytes 737280 | tf_op jit(solution)/shard_map/all_gather | solution.py:379
  123.4 1.8 %sweep_4.4 = (f32[3,4,16,128]{3,2,1,0:T(8,128)S(1)}, f32[3,2,16,128]{3,2,1,0:T(8,128)S(1)}, f32[3,2,16,128]{3,2,1,0:T(8,128)S(1)}, f32[3,2,16,128]{3,2,1,0:T(8,128)S(1)}, f32[3,2,16,128]{3,2,1,0:T(8,128)S(1)}) custom-call(f32[2,3,10,16,128]{4,3,2,1,0:T(8,128)S(1)} %bitcast.16, f32[2,3,18,16,128]{4,3,2,1,0:T(8,128)S(1)} %bitcast.8, ...), custom_call_target="tpu_custom_call" | custom-call | flops 4000000 | bytes 900000 | tf_op jit(solution)/shard_map/sweep_4/pallas_call | solution.py:315
  127.3 2.2 %all-gather.5 = f32[6,10,16,128]{3,2,1,0:T(8,128)S(1)} all-gather(f32[3,10,16,128]{3,2,1,0:T(8,128)S(1)} %pad_maximum_fusion.4), channel_id=7, replica_groups={{0,1},{2,3},{4,5},{6,7},{8,9},{10,11},{12,13},{14,15},{16,17},{18,19},{..., dimensions={0}, use_global_device_ids=true | all-gather | bytes 737280 | tf_op jit(solution)/shard_map/all_gather | solution.py:379
  129.4 2.4 %sweep_4.5 = (f32[3,4,16,128]{3,2,1,0:T(8,128)}, f32[3,2,16,128]{3,2,1,0:T(8,128)S(1)}, f32[3,2,16,128]{3,2,1,0:T(8,128)S(1)}, f32[3,2,16,128]{3,2,1,0:T(8,128)S(1)}, f32[3,2,16,128]{3,2,1,0:T(8,128)S(1)}) custom-call(f32[2,3,10,16,128]{4,3,2,1,0:T(8,128)S(1)} %bitcast.15, f32[2,3,18,16,128]{4,3,2,1,0:T(8,128)S(1)} %bitcast.9, ...), custom_call_target="tpu_custom_call" | custom-call | flops 4000000 | bytes 900000 | tf_op jit(solution)/shard_map/sweep_4/pallas_call | solution.py:315
  134.5 33.8 %collective-permute-done.29.c_ref = f32[3,2,16,128]{3,2,1,0:T(8,128)S(1)} collective-permute-done((f32[3,2,16,128]{3,2,1,0:T(8,128)S(1)}, f32[3,2,16,128]{3,2,1,0:T(8,128)S(1)}, u32[]{:S(2)}, u32[]{:S(2)}) %collective-permute-start.29) | collective-permute-done | bytes 49184 | tf_op jit(solution)/shard_map/ppermute | solution.py:367
  (65 shorter events, 22.0 us)
Async XLA Ops:
  0.0 16.7 %collective-permute-start.1 = (f32[3,4,64,128]{3,2,1,0:T(8,128)}, f32[3,4,64,128]{3,2,1,0:T(8,128)S(1)}, u32[]{:S(2)}, u32[]{:S(2)}) collective-permute-start(f32[3,4,64,128]{3,2,1,0:T(8,128)} %bitcast.10), channel_id=1, source_target_pairs={{1,0},{2,1},{3,2},{4,3},{5,4},{6,5},{7,6},{8,7},{9,8},{10,9},{11,1... | collective-permute-start | bytes 1179656 | tf_op jit(solution)/shard_map/ppermute | solution.py:399
  9.7 16.5 %collective-permute-start = (f32[3,4,64,128]{3,2,1,0:T(8,128)}, f32[3,4,64,128]{3,2,1,0:T(8,128)S(1)}, u32[]{:S(2)}, u32[]{:S(2)}) collective-permute-start(f32[3,4,64,128]{3,2,1,0:T(8,128)} %bitcast.11), channel_id=1, source_target_pairs={{0,1},{1,2},{2,3},{3,4},{4,5},{5,6},{6,7},{7,8},{8,9},{9,10},{10,1... | collective-permute-start | bytes 1179656 | tf_op jit(solution)/shard_map/ppermute | solution.py:398
  26.3 1.0 copy-start
  28.9 7.2 %collective-permute-start.3 = (f32[3,4,64,128]{3,2,1,0:T(8,128)S(1)}, f32[3,4,64,128]{3,2,1,0:T(8,128)S(1)}, u32[]{:S(2)}, u32[]{:S(2)}) collective-permute-start(f32[3,4,64,128]{3,2,1,0:T(8,128)S(1)} %fine_steps.3.mid_ref), channel_id=1, source_target_pairs={{1,0},{2,1},{3,2},{4,3},{5,4},{6,5},{7,6},{8,7},{9,8},{10,9},{11,1... | collective-permute-start | bytes 1179656 | tf_op jit(solution)/shard_map/ppermute | solution.py:399
  30.9 16.3 %collective-permute-start.2 = (f32[3,4,64,128]{3,2,1,0:T(8,128)S(1)}, f32[3,4,64,128]{3,2,1,0:T(8,128)S(1)}, u32[]{:S(2)}, u32[]{:S(2)}) collective-permute-start(f32[3,4,64,128]{3,2,1,0:T(8,128)S(1)} %fine_steps.3.mid_ref), channel_id=1, source_target_pairs={{0,1},{1,2},{2,3},{3,4},{4,5},{5,6},{6,7},{7,8},{8,9},{9,10},{10,1... | collective-permute-start | bytes 1179656 | tf_op jit(solution)/shard_map/ppermute | solution.py:398
  48.8 24.4 %copy-start.1 = (f32[1,3,4,64,128]{4,3,2,1,0:T(8,128)S(1)}, f32[1,3,4,64,128]{4,3,2,1,0:T(8,128)}, u32[]{:S(2)}) copy-start(f32[1,3,4,64,128]{4,3,2,1,0:T(8,128)} %param.1) | copy-start | bytes 1179652
  48.9 7.4 %collective-permute-start.5 = (f32[3,4,64,128]{3,2,1,0:T(8,128)S(1)}, f32[3,4,64,128]{3,2,1,0:T(8,128)S(1)}, u32[]{:S(2)}, u32[]{:S(2)}) collective-permute-start(f32[3,4,64,128]{3,2,1,0:T(8,128)S(1)} %fine_steps.4.mid_ref), channel_id=1, source_target_pairs={{1,0},{2,1},{3,2},{4,3},{5,4},{6,5},{7,6},{8,7},{9,8},{10,9},{11,1... | collective-permute-start | bytes 1179656 | tf_op jit(solution)/shard_map/ppermute | solution.py:399
  50.9 16.2 %collective-permute-start.4 = (f32[3,4,64,128]{3,2,1,0:T(8,128)S(1)}, f32[3,4,64,128]{3,2,1,0:T(8,128)S(1)}, u32[]{:S(2)}, u32[]{:S(2)}) collective-permute-start(f32[3,4,64,128]{3,2,1,0:T(8,128)S(1)} %fine_steps.4.mid_ref), channel_id=1, source_target_pairs={{0,1},{1,2},{2,3},{3,4},{4,5},{5,6},{6,7},{7,8},{8,9},{9,10},{10,1... | collective-permute-start | bytes 1179656 | tf_op jit(solution)/shard_map/ppermute | solution.py:398
  68.8 7.2 %collective-permute-start.7 = (f32[3,4,64,128]{3,2,1,0:T(8,128)S(1)}, f32[3,4,64,128]{3,2,1,0:T(8,128)S(1)}, u32[]{:S(2)}, u32[]{:S(2)}) collective-permute-start(f32[3,4,64,128]{3,2,1,0:T(8,128)S(1)} %fine_steps.5.mid_ref), channel_id=1, source_target_pairs={{1,0},{2,1},{3,2},{4,3},{5,4},{6,5},{7,6},{8,7},{9,8},{10,9},{11,1... | collective-permute-start | bytes 1179656 | tf_op jit(solution)/shard_map/ppermute | solution.py:399
  70.8 13.7 %collective-permute-start.6 = (f32[3,4,64,128]{3,2,1,0:T(8,128)S(1)}, f32[3,4,64,128]{3,2,1,0:T(8,128)S(1)}, u32[]{:S(2)}, u32[]{:S(2)}) collective-permute-start(f32[3,4,64,128]{3,2,1,0:T(8,128)S(1)} %fine_steps.5.mid_ref), channel_id=1, source_target_pairs={{0,1},{1,2},{2,3},{3,4},{4,5},{5,6},{6,7},{7,8},{8,9},{9,10},{10,1... | collective-permute-start | bytes 1179656 | tf_op jit(solution)/shard_map/ppermute | solution.py:398
  88.4 5.3 %collective-permute-start.11 = (f32[3,4,16,128]{3,2,1,0:T(8,128)S(1)}, f32[3,4,16,128]{3,2,1,0:T(8,128)S(1)}, u32[]{:S(2)}, u32[]{:S(2)}) collective-permute-start(f32[3,4,16,128]{3,2,1,0:T(8,128)S(1)} %pad_maximum_fusion.7.refs_2_), channel_id=1, source_target_pairs={{0,66},{2,68},{3,65},{4,70},{5,67},{6,72},{7,69},{8,74},{9,71},{10... | collective-permute-start | bytes 294920 | tf_op jit(solution)/shard_map/ppermute | solution.py:367
  89.0 2.7 %collective-permute-start.14 = (f32[3,2,16,128]{3,2,1,0:T(8,128)S(1)}, f32[3,2,16,128]{3,2,1,0:T(8,128)S(1)}, u32[]{:S(2)}, u32[]{:S(2)}) collective-permute-start(f32[3,2,16,128]{3,2,1,0:T(8,128)S(1)} %get-tuple-element.28), channel_id=1, source_target_pairs={{32,64},{33,65},{34,66},{35,67},{36,68},{37,69},{38,70},{39,71},{4... | collective-permute-start | bytes 147464 | tf_op jit(solution)/shard_map/ppermute | solution.py:367
  89.7 4.0 %collective-permute-start.12 = (f32[3,2,16,128]{3,2,1,0:T(8,128)S(1)}, f32[3,2,16,128]{3,2,1,0:T(8,128)S(1)}, u32[]{:S(2)}, u32[]{:S(2)}) collective-permute-start(f32[3,2,16,128]{3,2,1,0:T(8,128)S(1)} %get-tuple-element.28), channel_id=1, source_target_pairs={{0,64},{1,65},{2,66},{3,67},{4,68},{5,69},{6,70},{7,71},{8,72},{9,... | collective-permute-start | bytes 147464 | tf_op jit(solution)/shard_map/ppermute | solution.py:367
  90.4 3.3 %collective-permute-start.13 = (f32[3,2,16,128]{3,2,1,0:T(8,128)S(1)}, f32[3,2,16,128]{3,2,1,0:T(8,128)S(1)}, u32[]{:S(2)}, u32[]{:S(2)}) collective-permute-start(f32[3,2,16,128]{3,2,1,0:T(8,128)S(1)} %get-tuple-element.49), channel_id=1, source_target_pairs={{32,66},{34,68},{35,65},{36,70},{37,67},{38,72},{39,69},{40,74},{4... | collective-permute-start | bytes 147464 | tf_op jit(solution)/shard_map/ppermute | solution.py:367
  91.1 12.2 %collective-permute-start.9 = (f32[3,2,16,128]{3,2,1,0:T(8,128)S(1)}, f32[3,2,16,128]{3,2,1,0:T(8,128)S(1)}, u32[]{:S(2)}, u32[]{:S(2)}) collective-permute-start(f32[3,2,16,128]{3,2,1,0:T(8,128)S(1)} %get-tuple-element.49), channel_id=1, source_target_pairs={{96,100},{98,102},{100,104},{101,97},{102,106},{103,99},{104,108},... | collective-permute-start | bytes 147464 | tf_op jit(solution)/shard_map/ppermute | solution.py:367
  91.7 9.5 %collective-permute-start.8 = (f32[3,4,16,128]{3,2,1,0:T(8,128)S(1)}, f32[3,4,16,128]{3,2,1,0:T(8,128)S(1)}, u32[]{:S(2)}, u32[]{:S(2)}) collective-permute-start(f32[3,4,16,128]{3,2,1,0:T(8,128)S(1)} %pad_maximum_fusion.7.refs_2_), channel_id=1, source_target_pairs={{96,98},{98,100},{99,97},{100,102},{101,99},{102,104},{103,101},{1... | collective-permute-start | bytes 294920 | tf_op jit(solution)/shard_map/ppermute | solution.py:367
  101.3 5.4 %collective-permute-start.16 = (f32[3,4,16,128]{3,2,1,0:T(8,128)S(1)}, f32[3,4,16,128]{3,2,1,0:T(8,128)S(1)}, u32[]{:S(2)}, u32[]{:S(2)}) collective-permute-start(f32[3,4,16,128]{3,2,1,0:T(8,128)S(1)} %pad_maximum_fusion.8), channel_id=1, source_target_pairs={{160,192},{161,193},{162,194},{163,195},{164,196},{165,197},{166,1... | collective-permute-start | bytes 294920 | tf_op jit(solution)/shard_map/ppermute | solution.py:367
  102.0 8.1 %collective-permute-start.15 = (f32[3,6,16,128]{3,2,1,0:T(8,128)S(1)}, f32[3,6,16,128]{3,2,1,0:T(8,128)S(1)}, u32[]{:S(2)}, u32[]{:S(2)}) collective-permute-start(f32[3,6,16,128]{3,2,1,0:T(8,128)S(1)} %pad_maximum_fusion.6), channel_id=1, source_target_pairs={{128,192},{129,193},{130,194},{131,195},{132,196},{133,197},{134,1... | collective-permute-start | bytes 442376 | tf_op jit(solution)/shard_map/ppermute | solution.py:367
  103.3 2.7 %collective-permute-start.10 = (f32[3,8,16,128]{3,2,1,0:T(8,128)S(1)}, f32[3,8,16,128]{3,2,1,0:T(8,128)S(1)}, u32[]{:S(2)}, u32[]{:S(2)}) collective-permute-start(f32[3,8,16,128]{3,2,1,0:T(8,128)S(1)} %pad_maximum_fusion.5), channel_id=1, source_target_pairs={{96,192},{97,193},{98,194},{99,195},{100,196},{101,197},{102,198},... | collective-permute-start | bytes 589832 | tf_op jit(solution)/shard_map/ppermute | solution.py:367
  104.6 7.9 %collective-permute-start.19 = (f32[3,4,16,128]{3,2,1,0:T(8,128)S(1)}, f32[3,4,16,128]{3,2,1,0:T(8,128)S(1)}, u32[]{:S(2)}, u32[]{:S(2)}) collective-permute-start(f32[3,4,16,128]{3,2,1,0:T(8,128)S(1)} %get-tuple-element.29), channel_id=1, source_target_pairs={{64,196},{66,198},{68,200},{69,193},{70,202},{71,195},{72,204},{73... | collective-permute-start | bytes 294920 | tf_op jit(solution)/shard_map/ppermute | solution.py:367
  105.3 7.2 %collective-permute-start.18 = (f32[3,4,16,128]{3,2,1,0:T(8,128)S(1)}, f32[3,4,16,128]{3,2,1,0:T(8,128)S(1)}, u32[]{:S(2)}, u32[]{:S(2)}) collective-permute-start(f32[3,4,16,128]{3,2,1,0:T(8,128)S(1)} %get-tuple-element.29), channel_id=1, source_target_pairs={{64,194},{66,196},{67,193},{68,198},{69,195},{70,200},{71,197},{72... | collective-permute-start | bytes 294920 | tf_op jit(solution)/shard_map/ppermute | solution.py:367
  106.0 6.5 %collective-permute-start.20 = (f32[3,2,16,128]{3,2,1,0:T(8,128)S(1)}, f32[3,2,16,128]{3,2,1,0:T(8,128)S(1)}, u32[]{:S(2)}, u32[]{:S(2)}) collective-permute-start(f32[3,2,16,128]{3,2,1,0:T(8,128)S(1)} %slice_select_fusion.3), channel_id=1, source_target_pairs={{64,192},{65,193},{66,194},{67,195},{68,196},{69,197},{70,198},{71... | collective-permute-start | bytes 147464 | tf_op jit(solution)/shard_map/ppermute | solution.py:367
  116.7 4.4 %collective-permute-start.22 = (f32[3,4,16,128]{3,2,1,0:T(8,128)S(1)}, f32[3,4,16,128]{3,2,1,0:T(8,128)S(1)}, u32[]{:S(2)}, u32[]{:S(2)}) collective-permute-start(f32[3,4,16,128]{3,2,1,0:T(8,128)S(1)} %get-tuple-element.35), channel_id=1, source_target_pairs={{192,324},{194,326},{196,328},{197,321},{198,330},{199,323},{200,3... | collective-permute-start | bytes 294920 | tf_op jit(solution)/shard_map/ppermute | solution.py:367
  117.4 3.8 %collective-permute-start.21 = (f32[3,4,16,128]{3,2,1,0:T(8,128)S(1)}, f32[3,4,16,128]{3,2,1,0:T(8,128)S(1)}, u32[]{:S(2)}, u32[]{:S(2)}) collective-permute-start(f32[3,4,16,128]{3,2,1,0:T(8,128)S(1)} %get-tuple-element.35), channel_id=1, source_target_pairs={{192,322},{194,324},{195,321},{196,326},{197,323},{198,328},{199,3... | collective-permute-start | bytes 294920 | tf_op jit(solution)/shard_map/ppermute | solution.py:367
  118.1 3.0 %collective-permute-start.23 = (f32[3,2,16,128]{3,2,1,0:T(8,128)S(1)}, f32[3,2,16,128]{3,2,1,0:T(8,128)S(1)}, u32[]{:S(2)}, u32[]{:S(2)}) collective-permute-start(f32[3,2,16,128]{3,2,1,0:T(8,128)S(1)} %slice_select_fusion.2), channel_id=1, source_target_pairs={{192,320},{193,321},{194,322},{195,323},{196,324},{197,325},{198,3... | collective-permute-start | bytes 147464 | tf_op jit(solution)/shard_map/ppermute | solution.py:367
  119.2 49.1 %collective-permute-start.17 = (f32[3,4,64,128]{3,2,1,0:T(8,128)S(1)}, f32[3,4,64,128]{3,2,1,0:T(8,128)S(1)}, u32[]{:S(2)}, u32[]{:S(2)}) collective-permute-start(f32[3,4,64,128]{3,2,1,0:T(8,128)S(1)} %fine_change.1), channel_id=1, source_target_pairs={{0,32},{1,33},{2,34},{3,35},{4,36},{5,37},{6,38},{7,39},{8,40},{9,... | collective-permute-start | bytes 1179656 | tf_op jit(solution)/shard_map/ppermute | solution.py:367
  125.2 2.1 %collective-permute-start.25 = (f32[3,4,16,128]{3,2,1,0:T(8,128)S(1)}, f32[3,4,16,128]{3,2,1,0:T(8,128)S(1)}, u32[]{:S(2)}, u32[]{:S(2)}) collective-permute-start(f32[3,4,16,128]{3,2,1,0:T(8,128)S(1)} %get-tuple-element.40), channel_id=1, source_target_pairs={{320,452},{322,454},{324,456},{325,449},{326,458},{327,451},{328,4... | collective-permute-start | bytes 294920 | tf_op jit(solution)/shard_map/ppermute | solution.py:367
  125.9 1.4 collective-permute-start.24
  126.5 0.7 collective-permute-start.26
  131.9 2.6 %collective-permute-start.27 = (f32[3,2,16,128]{3,2,1,0:T(8,128)S(1)}, f32[3,2,16,128]{3,2,1,0:T(8,128)S(1)}, u32[]{:S(2)}, u32[]{:S(2)}) collective-permute-start(f32[3,2,16,128]{3,2,1,0:T(8,128)S(1)} %get-tuple-element.46), channel_id=1, source_target_pairs={{0,32},{1,33},{2,34},{3,35},{4,36},{5,37},{6,38},{7,39},{8,40},{9,... | collective-permute-start | bytes 147464 | tf_op jit(solution)/shard_map/ppermute | solution.py:367
  132.5 2.0 %collective-permute-start.28 = (f32[3,2,16,128]{3,2,1,0:T(8,128)S(1)}, f32[3,2,16,128]{3,2,1,0:T(8,128)S(1)}, u32[]{:S(2)}, u32[]{:S(2)}) collective-permute-start(f32[3,2,16,128]{3,2,1,0:T(8,128)S(1)} %get-tuple-element.47), channel_id=1, source_target_pairs={{192,160},{193,161},{194,162},{195,163},{196,164},{197,165},{198,1... | collective-permute-start | bytes 147464 | tf_op jit(solution)/shard_map/ppermute | solution.py:367
  133.2 35.1 %collective-permute-start.29 = (f32[3,2,16,128]{3,2,1,0:T(8,128)S(1)}, f32[3,2,16,128]{3,2,1,0:T(8,128)S(1)}, u32[]{:S(2)}, u32[]{:S(2)}) collective-permute-start(f32[3,2,16,128]{3,2,1,0:T(8,128)S(1)} %get-tuple-element.48), channel_id=1, source_target_pairs={{192,128},{193,129},{194,130},{195,131},{196,132},{197,133},{198,1... | collective-permute-start | bytes 147464 | tf_op jit(solution)/shard_map/ppermute | solution.py:367

commit v4 on v3

--- a/solution.py
+++ b/solution.py
@@ -8,7 +8,8 @@
 from jax.sharding import PartitionSpec as P
 
 FSTEPS = 16
-HALO = 4
+HALO = 8
+OWN = 4
 ROUNDS = FSTEPS // HALO
 NY = 64
 NZ = 128
@@ -132,34 +133,43 @@
     return rows
 
 
-def fine_kernel(last, left_ref, mid_ref, right_ref, *rest):
+def fine_kernel(last, mid_ref, sibling_ref, near_ref, far_ref, beyond_ref, *rest):
     if last:
         oc_ref, out_ref, q_ref, a, b, sums = rest
     else:
         out_ref, a, b = rest
     group, slab = position()
+    core = slab & 1
     lane = lanes()
     left = lane == 0
     right = lane == 127
     zero = jnp.zeros((8, 128), f32)
+    width = OWN + 2 * HALO
     for c in range(3):
-        for i in range(3 * HALO):
+        for i in range(width):
             for buffer in (a, b):
                 buffer[c, i, 0:8, :] = zero
                 buffer[c, i, NY + 8 : NY + 16, :] = zero
-        for at, ref in ((0, left_ref), (HALO, mid_ref), (2 * HALO, right_ref)):
-            for i in range(HALO):
+        for ref, block0, block1 in ((far_ref, 0, 4), (near_ref, 1, 3), (sibling_ref, 3, 1), (beyond_ref, 4, 0)):
+            at = jnp.where(core == 0, block0, block1) * OWN
+            for i in range(OWN):
                 a[c, at + i, 8 : NY + 8, :] = ref[c, i]
-    has_left = jnp.where(slab > 0, f32(1.0), f32(0.0))
-    has_right = jnp.where(slab < SLABS - 1, f32(1.0), f32(0.0))
+        for i in range(OWN):
+            a[c, HALO + i, 8 : NY + 8, :] = mid_ref[c, i]
+    inside = [
+        jnp.where(slab > 1, f32(1.0), f32(0.0)),
+        jnp.where(slab > 0, f32(1.0), f32(0.0)),
+        None,
+        jnp.where(slab < SLABS - 1, f32(1.0), f32(0.0)),
+        jnp.where(slab < SLABS - 2, f32(1.0), f32(0.0)),
+    ]
     src, dst = a, b
     for step in range(1, HALO + 1):
-        for i in range(step, 3 * HALO - step):
-            factor = has_left if i < HALO else has_right if i >= 2 * HALO else None
-            one_plane(src, dst, i, NY, fine_rate, fine_advect, factor, left, right)
+        for i in range(step, width - step):
+            one_plane(src, dst, i, NY, fine_rate, fine_advect, inside[i // OWN], left, right)
         src, dst = dst, src
     for c in range(3):
-        for i in range(HALO):
+        for i in range(OWN):
             out_ref[c, i] = src[c, HALO + i, 8 : NY + 8, :]
     if last:
         rows = restricted(lambda c, p, start: src[c, HALO + p, pl.ds(8 + start, 32, stride=2), :])
@@ -174,31 +184,32 @@
                 q_ref[c, p] = ended[at : at + CY] - keep * oc_ref[c, p]
 
 
-def fine_round(left, mid, right, oc=None):
+def fine_round(fields, oc=None):
     last = oc is not None
-    shape = jax.ShapeDtypeStruct(mid.shape, f32)
-    buffer = pltpu.VMEM((3, 3 * HALO, NY + 16, NZ), f32)
+    shape = jax.ShapeDtypeStruct(fields[0].shape, f32)
+    buffer = pltpu.VMEM((3, OWN + 2 * HALO, NY + 16, NZ), f32)
     coarse = jax.ShapeDtypeStruct((3, 2, CY, NZ), f32)
     return pl.pallas_call(
         functools.partial(fine_kernel, last),
         out_shape=(shape, coarse) if last else shape,
-        in_specs=[VMEM] * (4 if last else 3),
+        in_specs=[VMEM] * (6 if last else 5),
         out_specs=(VMEM, VMEM) if last else VMEM,
         scratch_shapes=[buffer, buffer] + ([pltpu.VMEM((6 * CY, 256), f32)] if last else []),
         compiler_params=PARAMS,
-        cost_estimate=pl.CostEstimate(flops=40_000_000, bytes_accessed=2_000_000, transcendentals=0),
+        cost_estimate=pl.CostEstimate(flops=120_000_000, bytes_accessed=2_800_000, transcendentals=0),
         name="fine_last" if last else "fine_steps",
-    )(left, mid, right, *([oc] if last else []))
-
-
-def first_coarse_kernel(left_ref, mid_ref, right_ref, out_ref, a, b, sums):
+    )(*fields, *([oc] if last else []))
+
+
+def first_coarse_kernel(mid_ref, sibling_ref, near_ref, out_ref, a, b, sums):
     group, slab = position()
+    core = slab & 1
     for c in range(3):
-        for part, ref in enumerate((left_ref, mid_ref, right_ref)):
+        for ref, part in ((mid_ref, 1), (sibling_ref, jnp.where(core == 0, 2, 0)), (near_ref, jnp.where(core == 0, 0, 2))):
             rows = restricted(lambda c, p, start: ref[c, p, pl.ds(start, 32, stride=2), :])
             for p in range(2):
-                sums[pl.ds((c * 6 + part * 2 + p) * CY, CY), :] = rows(c, p)
-    averaged = dot(sums[...], pairs_to_one(0.125))
+                sums[c * 6 + part * 2 + p] = rows(c, p)
+    averaged = dot(sums[...].reshape(18 * CY, 256), pairs_to_one(0.125))
     for c in range(3):
         for i in range(6):
             at = (c * 6 + i) * CY
@@ -211,18 +222,18 @@
     coarse_step(reads(b), lambda c, i, j, value: into(c, i - 2, j, value), 2, 4, limits)
 
 
-def first_coarse(left, mid, right):
+def first_coarse(mid, sibling, near):
     buffer = pltpu.VMEM((3, 6, CY, NZ), f32)
     return pl.pallas_call(
         first_coarse_kernel,
         out_shape=jax.ShapeDtypeStruct((3, 2, CY, NZ), f32),
         in_specs=[VMEM, VMEM, VMEM],
         out_specs=VMEM,
-        scratch_shapes=[buffer, buffer, pltpu.VMEM((18 * CY, 256), f32)],
+        scratch_shapes=[buffer, buffer, pltpu.VMEM((18, CY, 256), f32)],
         compiler_params=PARAMS,
         cost_estimate=pl.CostEstimate(flops=4_000_000, bytes_accessed=1_300_000, transcendentals=0),
         name="first_coarse",
-    )(left, mid, right)
+    )(mid, sibling, near)
 
 
 def change_kernel(ends_ref, oc_ref, out_ref):
@@ -391,34 +402,37 @@
     initial = starts[0]
     slab = lax.axis_index("space")
     core = slab & 1
-    up = [(s, s + 1) for s in range(SLABS - 1)]
-    down = [(s + 1, s) for s in range(SLABS - 1)]
+    swap = [(s, s ^ 1) for s in range(SLABS)]
+    across = [(s, s + 1 if s % 2 else s - 1) for s in range(1, SLABS - 1)]
+    over = [(s, s + 2) for s in range(0, SLABS - 2, 2)] + [(s, s - 2) for s in range(3, SLABS, 2)]
     field = initial
     for turn in range(ROUNDS):
-        left = lax.ppermute(field, "space", up)
-        right = lax.ppermute(field, "space", down)
+        near = lax.ppermute(field, "space", across)
+        far = lax.ppermute(field, "space", over)
+        sibling = lax.ppermute(field, "space", swap)
+        beyond = lax.ppermute(near, "space", swap)
         if turn == 0:
-            oc = first_coarse(left, field, right)
+            oc = first_coarse(field, sibling, near)
         if turn < ROUNDS - 1:
-            field = fine_round(left, field, right)
+            field = fine_round((field, sibling, near, far, beyond))
         else:
-            ends, mine = fine_round(left, field, right, oc)
+            ends, mine = fine_round((field, sibling, near, far, beyond), oc)
     pair = both_cores(mine)
     whole = joined(pair[0], pair[1])
 
-    def near(value):
+    def nearest(value):
         return jnp.where(core == 0, value[:, 2:4], value[:, 0:2])
 
     s1 = handed_on(whole, [0], 2, outward(1))
     s0 = handed_on(mine, [0], 2, here)
-    d1 = handed_on(near(whole), [1], 1, outward(1))
+    d1 = handed_on(nearest(whole), [1], 1, outward(1))
     d0 = handed_on(mine, [1], 1, here)
     sources = [c for c in range(3, GROUPS - 2) if c % 4 != 2]
     l1 = handed_on(whole, sources, 0, outward(1))
-    l2 = handed_on(near(whole), sources[::3], 0, outward(2))
+    l2 = handed_on(nearest(whole), sources[::3], 0, outward(2))
     y3 = handed_on(joined(l1, l2, mine), sources[::3], 3, here)
     y2 = handed_on(joined(l1, mine), sources[1::3], 2, here)
-    y1 = handed_on(joined(near(l1), mine), sources[2::3], 1, here)
+    y1 = handed_on(joined(nearest(l1), mine), sources[2::3], 1, here)
     both = both_cores(joined(s1, s0, d1, d0))
     state, own, plus = sweep(2, 2, both[:, :, :6], both[:, :, 6:], whole, (oc, oc))
     minus2 = minus1 = oc

time: 170 us -> 161 us (0.947)
  the two profiles are of different devices: /device:TPU:102 before, /device:TPU:100 now
where the time goes in v4:
time: 161 us; the launch traced here: 160 us
  waiting for transfers between devices  72.6 us (45%)
  starting transfers between devices  47.5 us (30%)
  Pallas kernels  21.5 us (13%)
  blocking collectives  16.5 us (10%)
    ppermute x22, waiting for transfers between devices, handed_on(): return lax.ppermute(value, AXES, table)  46.4 us
    ppermute x2, waiting for transfers between devices, shards(): near = lax.ppermute(field, 'space', across)  22.3 us
    ppermute x22, starting transfers between devices, handed_on(): return lax.ppermute(value, AXES, table)  19.4 us
    all_gather x6, blocking collectives, both_cores(): lax.all_gather(value, 'space', axis=0, tiled=False, axis_index_groups=PAIRS)  16.5 us
    ppermute x2, starting transfers between devices, shards(): near = lax.ppermute(field, 'space', across)  16.2 us
    pallas_call x2, Pallas kernels, fine_round(): pl.pallas_call(functools.partial(fine_kernel, last), out_shape=(shape, co...  12.6 us
    pallas_call x4, Pallas kernels, sweep(): pl.pallas_call(functools.partial(sweep_kernel, target, depth), out_shape=...  6.67 us
    ppermute x2, starting transfers between devices, shards(): sibling = lax.ppermute(field, 'space', swap)  4.05 us
  transfers between devices with their start and end apart: 30, of which 7 were waited for; matrix products, arithmetic and copies ran while one was open for 0% of the time, Pallas kernels for 4%

profile of v4, /device:TPU:100, one launch (start us, length us, event | category | flops | bytes accessed | tf_op | source)
XLA Modules:
  0.0 159.9 jit_solution(14913180466349357308)
XLA Ops:
  0.0 9.4 %collective-permute-start.1 = (f32[3,4,64,128]{3,2,1,0:T(8,128)}, f32[3,4,64,128]{3,2,1,0:T(8,128)S(1)}, u32[]{:S(2)}, u32[]{:S(2)}) collective-permute-start(f32[3,4,64,128]{3,2,1,0:T(8,128)} %bitcast.10), channel_id=1, source_target_pairs={{1,2},{2,1},{3,4},{4,3},{5,6},{6,5},{7,8},{8,7},{9,10},{10,9},{11,... | collective-permute-start | bytes 1179656 | tf_op jit(solution)/shard_map/ppermute | solution.py:410
  9.4 1.9 %collective-permute-start.2 = (f32[3,4,64,128]{3,2,1,0:T(8,128)}, f32[3,4,64,128]{3,2,1,0:T(8,128)S(1)}, u32[]{:S(2)}, u32[]{:S(2)}) collective-permute-start(f32[3,4,64,128]{3,2,1,0:T(8,128)} %bitcast.11), channel_id=1, source_target_pairs={{0,2},{2,4},{4,6},{6,8},{8,10},{10,12},{12,14},{14,16},{16,18},{18... | collective-permute-start | bytes 1179656 | tf_op jit(solution)/shard_map/ppermute | solution.py:411
  11.4 2.0 %collective-permute-start = (f32[3,4,64,128]{3,2,1,0:T(8,128)}, f32[3,4,64,128]{3,2,1,0:T(8,128)S(1)}, u32[]{:S(2)}, u32[]{:S(2)}) collective-permute-start(f32[3,4,64,128]{3,2,1,0:T(8,128)} %bitcast.12), channel_id=1, source_target_pairs={{0,1},{1,0},{2,3},{3,2},{4,5},{5,4},{6,7},{7,6},{8,9},{9,8},{10,11... | collective-permute-start | bytes 1179656 | tf_op jit(solution)/shard_map/ppermute | solution.py:412
  13.4 10.7 %collective-permute-done.1.near_ref = f32[3,4,64,128]{3,2,1,0:T(8,128)S(1)} collective-permute-done((f32[3,4,64,128]{3,2,1,0:T(8,128)}, f32[3,4,64,128]{3,2,1,0:T(8,128)S(1)}, u32[]{:S(2)}, u32[]{:S(2)}) %collective-permute-start.1) | collective-permute-done | bytes 393248 | tf_op jit(solution)/shard_map/ppermute | solution.py:410
  24.1 1.9 %collective-permute-start.3 = (f32[3,4,64,128]{3,2,1,0:T(8,128)S(1)}, f32[3,4,64,128]{3,2,1,0:T(8,128)S(1)}, u32[]{:S(2)}, u32[]{:S(2)}) collective-permute-start(f32[3,4,64,128]{3,2,1,0:T(8,128)S(1)} %collective-permute-done.1.near_ref), channel_id=1, source_target_pairs={{0,1},{1,0},{2,3},{3,2},{4,5},{5,4},{6,7},{7,6},{8,9},{9,8},{10,11... | collective-permute-start | bytes 1179656 | tf_op jit(solution)/shard_map/ppermute | solution.py:413
  26.0 1.0 collective-permute-done.2.far_ref
  27.0 0.7 collective-permute-done.3.beyond_ref
  27.7 1.0 copy-done
  28.7 6.2 %fine_steps.1.mid_ref = f32[3,4,64,128]{3,2,1,0:T(8,128)S(1)} custom-call(f32[3,4,64,128]{3,2,1,0:T(8,128)S(1)} %bitcast.13, f32[3,4,64,128]{3,2,1,0:T(8,128)S(1)} %collective-permute-done.sibling_ref, f32[3,4,64,128]{3,2,1,0:T(8,128)S(1)} %collective-permute-done.1.near_ref, f32[3,4,64,128]{3,2,1,0:T(8,128)S(1)} %collective-permute-done.2.far_ref, ...), custom_call_target="tpu_custom_call" | custom-call | flops 120000000 | bytes 2800000 | tf_op jit(solution)/shard_map/fine_steps/pallas_call | solution.py:192
  34.9 6.8 %collective-permute-start.5 = (f32[3,4,64,128]{3,2,1,0:T(8,128)S(1)}, f32[3,4,64,128]{3,2,1,0:T(8,128)S(1)}, u32[]{:S(2)}, u32[]{:S(2)}) collective-permute-start(f32[3,4,64,128]{3,2,1,0:T(8,128)S(1)} %fine_steps.1.mid_ref), channel_id=1, source_target_pairs={{1,2},{2,1},{3,4},{4,3},{5,6},{6,5},{7,8},{8,7},{9,10},{10,9},{11,... | collective-permute-start | bytes 1179656 | tf_op jit(solution)/shard_map/ppermute | solution.py:410
  41.7 1.9 %collective-permute-start.6 = (f32[3,4,64,128]{3,2,1,0:T(8,128)S(1)}, f32[3,4,64,128]{3,2,1,0:T(8,128)S(1)}, u32[]{:S(2)}, u32[]{:S(2)}) collective-permute-start(f32[3,4,64,128]{3,2,1,0:T(8,128)S(1)} %fine_steps.1.mid_ref), channel_id=1, source_target_pairs={{0,2},{2,4},{4,6},{6,8},{8,10},{10,12},{12,14},{14,16},{16,18},{18... | collective-permute-start | bytes 1179656 | tf_op jit(solution)/shard_map/ppermute | solution.py:411
  43.6 2.0 %collective-permute-start.4 = (f32[3,4,64,128]{3,2,1,0:T(8,128)S(1)}, f32[3,4,64,128]{3,2,1,0:T(8,128)S(1)}, u32[]{:S(2)}, u32[]{:S(2)}) collective-permute-start(f32[3,4,64,128]{3,2,1,0:T(8,128)S(1)} %fine_steps.1.mid_ref), channel_id=1, source_target_pairs={{0,1},{1,0},{2,3},{3,2},{4,5},{5,4},{6,7},{7,6},{8,9},{9,8},{10,11... | collective-permute-start | bytes 1179656 | tf_op jit(solution)/shard_map/ppermute | solution.py:412
  45.6 11.6 %collective-permute-done.5.near_ref = f32[3,4,64,128]{3,2,1,0:T(8,128)S(1)} collective-permute-done((f32[3,4,64,128]{3,2,1,0:T(8,128)S(1)}, f32[3,4,64,128]{3,2,1,0:T(8,128)S(1)}, u32[]{:S(2)}, u32[]{:S(2)}) %collective-permute-start.5) | collective-permute-done | bytes 393248 | tf_op jit(solution)/shard_map/ppermute | solution.py:410
  57.2 2.1 %collective-permute-start.7 = (f32[3,4,64,128]{3,2,1,0:T(8,128)S(1)}, f32[3,4,64,128]{3,2,1,0:T(8,128)S(1)}, u32[]{:S(2)}, u32[]{:S(2)}) collective-permute-start(f32[3,4,64,128]{3,2,1,0:T(8,128)S(1)} %collective-permute-done.5.near_ref), channel_id=1, source_target_pairs={{0,1},{1,0},{2,3},{3,2},{4,5},{5,4},{6,7},{7,6},{8,9},{9,8},{10,11... | collective-permute-start | bytes 1179656 | tf_op jit(solution)/shard_map/ppermute | solution.py:413
  60.0 2.2 %collective-permute-done.6.far_ref = f32[3,4,64,128]{3,2,1,0:T(8,128)S(1)} collective-permute-done((f32[3,4,64,128]{3,2,1,0:T(8,128)S(1)}, f32[3,4,64,128]{3,2,1,0:T(8,128)S(1)}, u32[]{:S(2)}, u32[]{:S(2)}) %collective-permute-start.6) | collective-permute-done | bytes 393248 | tf_op jit(solution)/shard_map/ppermute | solution.py:411
  62.2 6.4 %fine_last.1 = (f32[3,4,64,128]{3,2,1,0:T(8,128)S(1)}, f32[3,2,16,128]{3,2,1,0:T(8,128)S(1)}) custom-call(f32[3,4,64,128]{3,2,1,0:T(8,128)S(1)} %fine_steps.1.mid_ref, f32[3,4,64,128]{3,2,1,0:T(8,128)S(1)} %collective-permute-done.4.sibling_ref, f32[3,4,64,128]{3,2,1,0:T(8,128)S(1)} %collective-permute-done.5.near_ref, ...), custom_call_target="tpu_custom_call" | custom-call | flops 120000000 | bytes 2800000 | tf_op jit(solution)/shard_map/fine_last/pallas_call | solution.py:192
  68.7 1.9 %all-gather = f32[6,2,16,128]{3,2,1,0:T(8,128)S(1)} all-gather(f32[3,2,16,128]{3,2,1,0:T(8,128)S(1)} %get-tuple-element.28), channel_id=2, replica_groups={{0,1},{2,3},{4,5},{6,7},{8,9},{10,11},{12,13},{14,15},{16,17},{18,19},{..., dimensions={0}, use_global_device_ids=true | all-gather | bytes 147456 | tf_op jit(solution)/shard_map/all_gather | solution.py:390
  73.9 1.9 %collective-permute-start.8 = (f32[3,4,16,128]{3,2,1,0:T(8,128)S(1)}, f32[3,4,16,128]{3,2,1,0:T(8,128)S(1)}, u32[]{:S(2)}, u32[]{:S(2)}) collective-permute-start(f32[3,4,16,128]{3,2,1,0:T(8,128)S(1)} %pad_maximum_fusion.7.refs_2_), channel_id=1, source_target_pairs={{96,98},{98,100},{99,97},{100,102},{101,99},{102,104},{103,101},{1... | collective-permute-start | bytes 294920 | tf_op jit(solution)/shard_map/ppermute | solution.py:378
  75.9 5.5 %all-gather.1 = f32[6,10,16,128]{3,2,1,0:T(8,128)S(1)} all-gather(f32[3,10,16,128]{3,2,1,0:T(8,128)S(1)} %pad_maximum_fusion.1), channel_id=3, replica_groups={{0,1},{2,3},{4,5},{6,7},{8,9},{10,11},{12,13},{14,15},{16,17},{18,19},{..., dimensions={0}, use_global_device_ids=true | all-gather | bytes 737280 | tf_op jit(solution)/shard_map/all_gather | solution.py:390
  81.4 2.0 %collective-permute-done.8 = f32[3,4,16,128]{3,2,1,0:T(8,128)S(1)} collective-permute-done((f32[3,4,16,128]{3,2,1,0:T(8,128)S(1)}, f32[3,4,16,128]{3,2,1,0:T(8,128)S(1)}, u32[]{:S(2)}, u32[]{:S(2)}) %collective-permute-start.8) | collective-permute-done | bytes 98336 | tf_op jit(solution)/shard_map/ppermute | solution.py:378
  84.2 1.3 collective-permute-start.15
  88.9 2.4 %all-gather.2 = f32[6,18,16,128]{3,2,1,0:T(8,128)S(1)} all-gather(f32[3,18,16,128]{3,2,1,0:T(8,128)S(1)} %pad_maximum_fusion), channel_id=4, replica_groups={{0,1},{2,3},{4,5},{6,7},{8,9},{10,11},{12,13},{14,15},{16,17},{18,19},{..., dimensions={0}, use_global_device_ids=true | all-gather | bytes 1327104 | tf_op jit(solution)/shard_map/all_gather | solution.py:390
  91.4 2.2 %all-gather.3 = f32[6,10,16,128]{3,2,1,0:T(8,128)S(1)} all-gather(f32[3,10,16,128]{3,2,1,0:T(8,128)S(1)} %pad_maximum_fusion.2), channel_id=5, replica_groups={{0,1},{2,3},{4,5},{6,7},{8,9},{10,11},{12,13},{14,15},{16,17},{18,19},{..., dimensions={0}, use_global_device_ids=true | all-gather | bytes 737280 | tf_op jit(solution)/shard_map/all_gather | solution.py:390
  93.6 1.8 %sweep_4.3 = (f32[3,4,16,128]{3,2,1,0:T(8,128)S(1)}, f32[3,2,16,128]{3,2,1,0:T(8,128)S(1)}, f32[3,2,16,128]{3,2,1,0:T(8,128)S(1)}, f32[3,2,16,128]{3,2,1,0:T(8,128)S(1)}, f32[3,2,16,128]{3,2,1,0:T(8,128)S(1)}) custom-call(f32[2,3,10,16,128]{4,3,2,1,0:T(8,128)S(1)} %bitcast.18, f32[2,3,18,16,128]{4,3,2,1,0:T(8,128)S(1)} %bitcast.7, ...), custom_call_target="tpu_custom_call" | custom-call | flops 4000000 | bytes 900000 | tf_op jit(solution)/shard_map/sweep_4/pallas_call | solution.py:326
  97.9 2.9 %collective-permute-start.17 = (f32[3,4,64,128]{3,2,1,0:T(8,128)S(1)}, f32[3,4,64,128]{3,2,1,0:T(8,128)S(1)}, u32[]{:S(2)}, u32[]{:S(2)}) collective-permute-start(f32[3,4,64,128]{3,2,1,0:T(8,128)S(1)} %fine_change.1), channel_id=1, source_target_pairs={{0,32},{1,33},{2,34},{3,35},{4,36},{5,37},{6,38},{7,39},{8,40},{9,... | collective-permute-start | bytes 1179656 | tf_op jit(solution)/shard_map/ppermute | solution.py:378
  100.9 2.4 %all-gather.4 = f32[6,10,16,128]{3,2,1,0:T(8,128)S(1)} all-gather(f32[3,10,16,128]{3,2,1,0:T(8,128)S(1)} %pad_maximum_fusion.3), channel_id=6, replica_groups={{0,1},{2,3},{4,5},{6,7},{8,9},{10,11},{12,13},{14,15},{16,17},{18,19},{..., dimensions={0}, use_global_device_ids=true | all-gather | bytes 737280 | tf_op jit(solution)/shard_map/all_gather | solution.py:390
  103.3 1.8 %sweep_4.4 = (f32[3,4,16,128]{3,2,1,0:T(8,128)S(1)}, f32[3,2,16,128]{3,2,1,0:T(8,128)S(1)}, f32[3,2,16,128]{3,2,1,0:T(8,128)S(1)}, f32[3,2,16,128]{3,2,1,0:T(8,128)S(1)}, f32[3,2,16,128]{3,2,1,0:T(8,128)S(1)}) custom-call(f32[2,3,10,16,128]{4,3,2,1,0:T(8,128)S(1)} %bitcast.17, f32[2,3,18,16,128]{4,3,2,1,0:T(8,128)S(1)} %bitcast.8, ...), custom_call_target="tpu_custom_call" | custom-call | flops 4000000 | bytes 900000 | tf_op jit(solution)/shard_map/sweep_4/pallas_call | solution.py:326
  107.2 2.2 %all-gather.5 = f32[6,10,16,128]{3,2,1,0:T(8,128)S(1)} all-gather(f32[3,10,16,128]{3,2,1,0:T(8,128)S(1)} %pad_maximum_fusion.4), channel_id=7, replica_groups={{0,1},{2,3},{4,5},{6,7},{8,9},{10,11},{12,13},{14,15},{16,17},{18,19},{..., dimensions={0}, use_global_device_ids=true | all-gather | bytes 737280 | tf_op jit(solution)/shard_map/all_gather | solution.py:390
  109.3 2.4 %sweep_4.5 = (f32[3,4,16,128]{3,2,1,0:T(8,128)}, f32[3,2,16,128]{3,2,1,0:T(8,128)S(1)}, f32[3,2,16,128]{3,2,1,0:T(8,128)S(1)}, f32[3,2,16,128]{3,2,1,0:T(8,128)S(1)}, f32[3,2,16,128]{3,2,1,0:T(8,128)S(1)}) custom-call(f32[2,3,10,16,128]{4,3,2,1,0:T(8,128)S(1)} %bitcast.16, f32[2,3,18,16,128]{4,3,2,1,0:T(8,128)S(1)} %bitcast.9, ...), custom_call_target="tpu_custom_call" | custom-call | flops 4000000 | bytes 900000 | tf_op jit(solution)/shard_map/sweep_4/pallas_call | solution.py:326
  113.1 1.3 collective-permute-start.29
  114.4 44.3 %collective-permute-done.29.c_ref = f32[3,2,16,128]{3,2,1,0:T(8,128)S(1)} collective-permute-done((f32[3,2,16,128]{3,2,1,0:T(8,128)S(1)}, f32[3,2,16,128]{3,2,1,0:T(8,128)S(1)}, u32[]{:S(2)}, u32[]{:S(2)}) %collective-permute-start.29) | collective-permute-done | bytes 49184 | tf_op jit(solution)/shard_map/ppermute | solution.py:378
  158.7 1.2 final.1
  (63 shorter events, 14.0 us)
Async XLA Ops:
  0.0 24.1 %collective-permute-start.1 = (f32[3,4,64,128]{3,2,1,0:T(8,128)}, f32[3,4,64,128]{3,2,1,0:T(8,128)S(1)}, u32[]{:S(2)}, u32[]{:S(2)}) collective-permute-start(f32[3,4,64,128]{3,2,1,0:T(8,128)} %bitcast.10), channel_id=1, source_target_pairs={{1,2},{2,1},{3,4},{4,3},{5,6},{6,5},{7,8},{8,7},{9,10},{10,9},{11,... | collective-permute-start | bytes 1179656 | tf_op jit(solution)/shard_map/ppermute | solution.py:410
  9.4 17.5 %collective-permute-start.2 = (f32[3,4,64,128]{3,2,1,0:T(8,128)}, f32[3,4,64,128]{3,2,1,0:T(8,128)S(1)}, u32[]{:S(2)}, u32[]{:S(2)}) collective-permute-start(f32[3,4,64,128]{3,2,1,0:T(8,128)} %bitcast.11), channel_id=1, source_target_pairs={{0,2},{2,4},{4,6},{6,8},{8,10},{10,12},{12,14},{14,16},{16,18},{18... | collective-permute-start | bytes 1179656 | tf_op jit(solution)/shard_map/ppermute | solution.py:411
  11.4 15.6 %collective-permute-start = (f32[3,4,64,128]{3,2,1,0:T(8,128)}, f32[3,4,64,128]{3,2,1,0:T(8,128)S(1)}, u32[]{:S(2)}, u32[]{:S(2)}) collective-permute-start(f32[3,4,64,128]{3,2,1,0:T(8,128)} %bitcast.12), channel_id=1, source_target_pairs={{0,1},{1,0},{2,3},{3,2},{4,5},{5,4},{6,7},{7,6},{8,9},{9,8},{10,11... | collective-permute-start | bytes 1179656 | tf_op jit(solution)/shard_map/ppermute | solution.py:412
  24.1 3.6 %collective-permute-start.3 = (f32[3,4,64,128]{3,2,1,0:T(8,128)S(1)}, f32[3,4,64,128]{3,2,1,0:T(8,128)S(1)}, u32[]{:S(2)}, u32[]{:S(2)}) collective-permute-start(f32[3,4,64,128]{3,2,1,0:T(8,128)S(1)} %collective-permute-done.1.near_ref), channel_id=1, source_target_pairs={{0,1},{1,0},{2,3},{3,2},{4,5},{5,4},{6,7},{7,6},{8,9},{9,8},{10,11... | collective-permute-start | bytes 1179656 | tf_op jit(solution)/shard_map/ppermute | solution.py:413
  27.7 1.0 copy-start
  28.7 30.7 %copy-start.1 = (f32[1,3,4,64,128]{4,3,2,1,0:T(8,128)S(1)}, f32[1,3,4,64,128]{4,3,2,1,0:T(8,128)}, u32[]{:S(2)}) copy-start(f32[1,3,4,64,128]{4,3,2,1,0:T(8,128)} %param.1) | copy-start | bytes 1179652
  34.9 22.4 %collective-permute-start.5 = (f32[3,4,64,128]{3,2,1,0:T(8,128)S(1)}, f32[3,4,64,128]{3,2,1,0:T(8,128)S(1)}, u32[]{:S(2)}, u32[]{:S(2)}) collective-permute-start(f32[3,4,64,128]{3,2,1,0:T(8,128)S(1)} %fine_steps.1.mid_ref), channel_id=1, source_target_pairs={{1,2},{2,1},{3,4},{4,3},{5,6},{6,5},{7,8},{8,7},{9,10},{10,9},{11,... | collective-permute-start | bytes 1179656 | tf_op jit(solution)/shard_map/ppermute | solution.py:410
  41.7 20.6 %collective-permute-start.6 = (f32[3,4,64,128]{3,2,1,0:T(8,128)S(1)}, f32[3,4,64,128]{3,2,1,0:T(8,128)S(1)}, u32[]{:S(2)}, u32[]{:S(2)}) collective-permute-start(f32[3,4,64,128]{3,2,1,0:T(8,128)S(1)} %fine_steps.1.mid_ref), channel_id=1, source_target_pairs={{0,2},{2,4},{4,6},{6,8},{8,10},{10,12},{12,14},{14,16},{16,18},{18... | collective-permute-start | bytes 1179656 | tf_op jit(solution)/shard_map/ppermute | solution.py:411
  43.6 18.6 %collective-permute-start.4 = (f32[3,4,64,128]{3,2,1,0:T(8,128)S(1)}, f32[3,4,64,128]{3,2,1,0:T(8,128)S(1)}, u32[]{:S(2)}, u32[]{:S(2)}) collective-permute-start(f32[3,4,64,128]{3,2,1,0:T(8,128)S(1)} %fine_steps.1.mid_ref), channel_id=1, source_target_pairs={{0,1},{1,0},{2,3},{3,2},{4,5},{5,4},{6,7},{7,6},{8,9},{9,8},{10,11... | collective-permute-start | bytes 1179656 | tf_op jit(solution)/shard_map/ppermute | solution.py:412
  57.2 5.0 %collective-permute-start.7 = (f32[3,4,64,128]{3,2,1,0:T(8,128)S(1)}, f32[3,4,64,128]{3,2,1,0:T(8,128)S(1)}, u32[]{:S(2)}, u32[]{:S(2)}) collective-permute-start(f32[3,4,64,128]{3,2,1,0:T(8,128)S(1)} %collective-permute-done.5.near_ref), channel_id=1, source_target_pairs={{0,1},{1,0},{2,3},{3,2},{4,5},{5,4},{6,7},{7,6},{8,9},{9,8},{10,11... | collective-permute-start | bytes 1179656 | tf_op jit(solution)/shard_map/ppermute | solution.py:413
  70.6 5.3 %collective-permute-start.11 = (f32[3,4,16,128]{3,2,1,0:T(8,128)S(1)}, f32[3,4,16,128]{3,2,1,0:T(8,128)S(1)}, u32[]{:S(2)}, u32[]{:S(2)}) collective-permute-start(f32[3,4,16,128]{3,2,1,0:T(8,128)S(1)} %pad_maximum_fusion.7.refs_2_), channel_id=1, source_target_pairs={{0,66},{2,68},{3,65},{4,70},{5,67},{6,72},{7,69},{8,74},{9,71},{10... | collective-permute-start | bytes 294920 | tf_op jit(solution)/shard_map/ppermute | solution.py:378
  71.2 2.7 %collective-permute-start.14 = (f32[3,2,16,128]{3,2,1,0:T(8,128)S(1)}, f32[3,2,16,128]{3,2,1,0:T(8,128)S(1)}, u32[]{:S(2)}, u32[]{:S(2)}) collective-permute-start(f32[3,2,16,128]{3,2,1,0:T(8,128)S(1)} %get-tuple-element.28), channel_id=1, source_target_pairs={{32,64},{33,65},{34,66},{35,67},{36,68},{37,69},{38,70},{39,71},{4... | collective-permute-start | bytes 147464 | tf_op jit(solution)/shard_map/ppermute | solution.py:378
  71.9 4.0 %collective-permute-start.12 = (f32[3,2,16,128]{3,2,1,0:T(8,128)S(1)}, f32[3,2,16,128]{3,2,1,0:T(8,128)S(1)}, u32[]{:S(2)}, u32[]{:S(2)}) collective-permute-start(f32[3,2,16,128]{3,2,1,0:T(8,128)S(1)} %get-tuple-element.28), channel_id=1, source_target_pairs={{0,64},{1,65},{2,66},{3,67},{4,68},{5,69},{6,70},{7,71},{8,72},{9,... | collective-permute-start | bytes 147464 | tf_op jit(solution)/shard_map/ppermute | solution.py:378
  72.6 3.3 %collective-permute-start.13 = (f32[3,2,16,128]{3,2,1,0:T(8,128)S(1)}, f32[3,2,16,128]{3,2,1,0:T(8,128)S(1)}, u32[]{:S(2)}, u32[]{:S(2)}) collective-permute-start(f32[3,2,16,128]{3,2,1,0:T(8,128)S(1)} %get-tuple-element.49), channel_id=1, source_target_pairs={{32,66},{34,68},{35,65},{36,70},{37,67},{38,72},{39,69},{40,74},{4... | collective-permute-start | bytes 147464 | tf_op jit(solution)/shard_map/ppermute | solution.py:378
  73.3 12.2 %collective-permute-start.9 = (f32[3,2,16,128]{3,2,1,0:T(8,128)S(1)}, f32[3,2,16,128]{3,2,1,0:T(8,128)S(1)}, u32[]{:S(2)}, u32[]{:S(2)}) collective-permute-start(f32[3,2,16,128]{3,2,1,0:T(8,128)S(1)} %get-tuple-element.49), channel_id=1, source_target_pairs={{96,100},{98,102},{100,104},{101,97},{102,106},{103,99},{104,108},... | collective-permute-start | bytes 147464 | tf_op jit(solution)/shard_map/ppermute | solution.py:378
  73.9 9.5 %collective-permute-start.8 = (f32[3,4,16,128]{3,2,1,0:T(8,128)S(1)}, f32[3,4,16,128]{3,2,1,0:T(8,128)S(1)}, u32[]{:S(2)}, u32[]{:S(2)}) collective-permute-start(f32[3,4,16,128]{3,2,1,0:T(8,128)S(1)} %pad_maximum_fusion.7.refs_2_), channel_id=1, source_target_pairs={{96,98},{98,100},{99,97},{100,102},{101,99},{102,104},{103,101},{1... | collective-permute-start | bytes 294920 | tf_op jit(solution)/shard_map/ppermute | solution.py:378
  83.5 5.4 %collective-permute-start.16 = (f32[3,4,16,128]{3,2,1,0:T(8,128)S(1)}, f32[3,4,16,128]{3,2,1,0:T(8,128)S(1)}, u32[]{:S(2)}, u32[]{:S(2)}) collective-permute-start(f32[3,4,16,128]{3,2,1,0:T(8,128)S(1)} %pad_maximum_fusion.8), channel_id=1, source_target_pairs={{160,192},{161,193},{162,194},{163,195},{164,196},{165,197},{166,1... | collective-permute-start | bytes 294920 | tf_op jit(solution)/shard_map/ppermute | solution.py:378
  84.2 4.7 %collective-permute-start.15 = (f32[3,6,16,128]{3,2,1,0:T(8,128)S(1)}, f32[3,6,16,128]{3,2,1,0:T(8,128)S(1)}, u32[]{:S(2)}, u32[]{:S(2)}) collective-permute-start(f32[3,6,16,128]{3,2,1,0:T(8,128)S(1)} %pad_maximum_fusion.6), channel_id=1, source_target_pairs={{128,192},{129,193},{130,194},{131,195},{132,196},{133,197},{134,1... | collective-permute-start | bytes 442376 | tf_op jit(solution)/shard_map/ppermute | solution.py:378
  85.5 2.7 %collective-permute-start.10 = (f32[3,8,16,128]{3,2,1,0:T(8,128)S(1)}, f32[3,8,16,128]{3,2,1,0:T(8,128)S(1)}, u32[]{:S(2)}, u32[]{:S(2)}) collective-permute-start(f32[3,8,16,128]{3,2,1,0:T(8,128)S(1)} %pad_maximum_fusion.5), channel_id=1, source_target_pairs={{96,192},{97,193},{98,194},{99,195},{100,196},{101,197},{102,198},... | collective-permute-start | bytes 589832 | tf_op jit(solution)/shard_map/ppermute | solution.py:378
  86.9 4.5 %collective-permute-start.19 = (f32[3,4,16,128]{3,2,1,0:T(8,128)S(1)}, f32[3,4,16,128]{3,2,1,0:T(8,128)S(1)}, u32[]{:S(2)}, u32[]{:S(2)}) collective-permute-start(f32[3,4,16,128]{3,2,1,0:T(8,128)S(1)} %get-tuple-element.29), channel_id=1, source_target_pairs={{64,196},{66,198},{68,200},{69,193},{70,202},{71,195},{72,204},{73... | collective-permute-start | bytes 294920 | tf_op jit(solution)/shard_map/ppermute | solution.py:378
  87.5 3.9 %collective-permute-start.18 = (f32[3,4,16,128]{3,2,1,0:T(8,128)S(1)}, f32[3,4,16,128]{3,2,1,0:T(8,128)S(1)}, u32[]{:S(2)}, u32[]{:S(2)}) collective-permute-start(f32[3,4,16,128]{3,2,1,0:T(8,128)S(1)} %get-tuple-element.29), channel_id=1, source_target_pairs={{64,194},{66,196},{67,193},{68,198},{69,195},{70,200},{71,197},{72... | collective-permute-start | bytes 294920 | tf_op jit(solution)/shard_map/ppermute | solution.py:378
  88.2 3.2 %collective-permute-start.20 = (f32[3,2,16,128]{3,2,1,0:T(8,128)S(1)}, f32[3,2,16,128]{3,2,1,0:T(8,128)S(1)}, u32[]{:S(2)}, u32[]{:S(2)}) collective-permute-start(f32[3,2,16,128]{3,2,1,0:T(8,128)S(1)} %slice_select_fusion.3), channel_id=1, source_target_pairs={{64,192},{65,193},{66,194},{67,195},{68,196},{69,197},{70,198},{71... | collective-permute-start | bytes 147464 | tf_op jit(solution)/shard_map/ppermute | solution.py:378
  95.4 5.4 %collective-permute-start.22 = (f32[3,4,16,128]{3,2,1,0:T(8,128)S(1)}, f32[3,4,16,128]{3,2,1,0:T(8,128)S(1)}, u32[]{:S(2)}, u32[]{:S(2)}) collective-permute-start(f32[3,4,16,128]{3,2,1,0:T(8,128)S(1)} %get-tuple-element.35), channel_id=1, source_target_pairs={{192,324},{194,326},{196,328},{197,321},{198,330},{199,323},{200,3... | collective-permute-start | bytes 294920 | tf_op jit(solution)/shard_map/ppermute | solution.py:378
  96.1 4.8 %collective-permute-start.21 = (f32[3,4,16,128]{3,2,1,0:T(8,128)S(1)}, f32[3,4,16,128]{3,2,1,0:T(8,128)S(1)}, u32[]{:S(2)}, u32[]{:S(2)}) collective-permute-start(f32[3,4,16,128]{3,2,1,0:T(8,128)S(1)} %get-tuple-element.35), channel_id=1, source_target_pairs={{192,322},{194,324},{195,321},{196,326},{197,323},{198,328},{199,3... | collective-permute-start | bytes 294920 | tf_op jit(solution)/shard_map/ppermute | solution.py:378
  96.8 4.1 %collective-permute-start.23 = (f32[3,2,16,128]{3,2,1,0:T(8,128)S(1)}, f32[3,2,16,128]{3,2,1,0:T(8,128)S(1)}, u32[]{:S(2)}, u32[]{:S(2)}) collective-permute-start(f32[3,2,16,128]{3,2,1,0:T(8,128)S(1)} %slice_select_fusion.2), channel_id=1, source_target_pairs={{192,320},{193,321},{194,322},{195,323},{196,324},{197,325},{198,3... | collective-permute-start | bytes 147464 | tf_op jit(solution)/shard_map/ppermute | solution.py:378
  97.9 60.9 %collective-permute-start.17 = (f32[3,4,64,128]{3,2,1,0:T(8,128)S(1)}, f32[3,4,64,128]{3,2,1,0:T(8,128)S(1)}, u32[]{:S(2)}, u32[]{:S(2)}) collective-permute-start(f32[3,4,64,128]{3,2,1,0:T(8,128)S(1)} %fine_change.1), channel_id=1, source_target_pairs={{0,32},{1,33},{2,34},{3,35},{4,36},{5,37},{6,38},{7,39},{8,40},{9,... | collective-permute-start | bytes 1179656 | tf_op jit(solution)/shard_map/ppermute | solution.py:378
  105.1 2.1 %collective-permute-start.25 = (f32[3,4,16,128]{3,2,1,0:T(8,128)S(1)}, f32[3,4,16,128]{3,2,1,0:T(8,128)S(1)}, u32[]{:S(2)}, u32[]{:S(2)}) collective-permute-start(f32[3,4,16,128]{3,2,1,0:T(8,128)S(1)} %get-tuple-element.40), channel_id=1, source_target_pairs={{320,452},{322,454},{324,456},{325,449},{326,458},{327,451},{328,4... | collective-permute-start | bytes 294920 | tf_op jit(solution)/shard_map/ppermute | solution.py:378
  105.8 1.4 collective-permute-start.24
  106.4 0.7 collective-permute-start.26
  111.8 2.6 %collective-permute-start.27 = (f32[3,2,16,128]{3,2,1,0:T(8,128)S(1)}, f32[3,2,16,128]{3,2,1,0:T(8,128)S(1)}, u32[]{:S(2)}, u32[]{:S(2)}) collective-permute-start(f32[3,2,16,128]{3,2,1,0:T(8,128)S(1)} %get-tuple-element.46), channel_id=1, source_target_pairs={{0,32},{1,33},{2,34},{3,35},{4,36},{5,37},{6,38},{7,39},{8,40},{9,... | collective-permute-start | bytes 147464 | tf_op jit(solution)/shard_map/ppermute | solution.py:378
  112.4 2.0 %collective-permute-start.28 = (f32[3,2,16,128]{3,2,1,0:T(8,128)S(1)}, f32[3,2,16,128]{3,2,1,0:T(8,128)S(1)}, u32[]{:S(2)}, u32[]{:S(2)}) collective-permute-start(f32[3,2,16,128]{3,2,1,0:T(8,128)S(1)} %get-tuple-element.47), channel_id=1, source_target_pairs={{192,160},{193,161},{194,162},{195,163},{196,164},{197,165},{198,1... | collective-permute-start | bytes 147464 | tf_op jit(solution)/shard_map/ppermute | solution.py:378
  113.1 45.6 %collective-permute-start.29 = (f32[3,2,16,128]{3,2,1,0:T(8,128)S(1)}, f32[3,2,16,128]{3,2,1,0:T(8,128)S(1)}, u32[]{:S(2)}, u32[]{:S(2)}) collective-permute-start(f32[3,2,16,128]{3,2,1,0:T(8,128)S(1)} %get-tuple-element.48), channel_id=1, source_target_pairs={{192,128},{193,129},{194,130},{195,131},{196,132},{197,133},{198,1... | collective-permute-start | bytes 147464 | tf_op jit(solution)/shard_map/ppermute | solution.py:378

commit v5 on v4

--- a/solution.py
+++ b/solution.py
@@ -275,8 +275,8 @@
 
 
 def sweep_kernel(target, depth, *refs):
-    got_ref, before_ref, own_ref, *kept = refs[: 3 + depth]
-    state_ref, *results = refs[3 + depth : 4 + 2 * depth]
+    got_ref, before_ref, *kept = refs[: 2 + depth]
+    state_ref, half_ref, *results = refs[2 + depth : 4 + 2 * depth]
     a, b = refs[4 + 2 * depth :]
     group, slab = position()
     core = slab & 1
@@ -306,33 +306,33 @@
             for i in range(2):
                 value = jnp.where(core == 0, a[c, reach + i], a[c, reach + 2 + i])
                 results[turn][c, i] = jnp.where(mine, value, kept[turn][c, i])
-        if turn == depth - 1:
+        count = reach - edge
+        for core_at, at, place in halves(count):
             for c in range(3):
-                for i in range(4):
-                    state_ref[c, i] = a[c, reach + i] + own_ref[c, i]
-        else:
-            count = reach - edge
-            for core_at, at, place in halves(count):
-                for c in range(3):
-                    i = place + edge + 2
-                    a[c, i] = a[c, i] + before_ref[core_at, c, at_before + at]
-            at_before += count
-
-
-def sweep(target, depth, got, before, own, kept):
+                i = place + edge + 2
+                a[c, i] = a[c, i] + before_ref[core_at, c, at_before + at]
+        at_before += count
+    for c in range(3):
+        for i in range(4):
+            state_ref[c, i] = a[c, reach + i]
+        for i in range(2):
+            half_ref[c, i] = jnp.where(core == 0, a[c, reach + i], a[c, reach + 2 + i])
+
+
+def sweep(target, depth, got, before, kept):
     buffer = pltpu.VMEM((3, 4 * depth + 4, CY, NZ), f32)
     two = jax.ShapeDtypeStruct((3, 2, CY, NZ), f32)
     four = jax.ShapeDtypeStruct((3, 4, CY, NZ), f32)
     return pl.pallas_call(
         functools.partial(sweep_kernel, target, depth),
-        out_shape=(four,) + (two,) * depth,
-        in_specs=[VMEM] * (3 + depth),
-        out_specs=(VMEM,) * (1 + depth),
+        out_shape=(four, two) + (two,) * depth,
+        in_specs=[VMEM] * (2 + depth),
+        out_specs=(VMEM,) * (2 + depth),
         scratch_shapes=[buffer, buffer],
         compiler_params=PARAMS,
         cost_estimate=pl.CostEstimate(flops=4_000_000, bytes_accessed=900_000, transcendentals=0),
         name="sweep_%d" % depth,
-    )(got, before, own, *kept)
+    )(got, before, *kept)
 
 
 def final_kernel(start_ref, previous_ref, own_ref, a_ref, b_ref, c_ref, out_ref):
@@ -345,7 +345,7 @@
     @pl.when(group != 0)
     def _():
         expand = one_to_pairs()
-        chain = (group & 3) == 2
+        chain = (group == 2) | ((group & 3) == 0)
         for c in range(3):
             for p in range(2):
                 others = a_ref[c, p] + b_ref[c, p] + c_ref[c, p]
@@ -369,12 +369,16 @@
     )(*arrays)
 
 
-def handed_on(value, groups, by, place):
+def legs(groups, by, place):
     table = []
     for c in groups:
         for s in range(SLABS):
             if 0 <= place(s) < SLABS and 0 <= c + by < GROUPS:
                 table.append((c * SLABS + s, (c + by) * SLABS + place(s)))
+    return table
+
+
+def moved(value, table):
     return lax.ppermute(value, AXES, table)
 
 
@@ -423,36 +427,35 @@
     def nearest(value):
         return jnp.where(core == 0, value[:, 2:4], value[:, 0:2])
 
-    s1 = handed_on(whole, [0], 2, outward(1))
-    s0 = handed_on(mine, [0], 2, here)
-    d1 = handed_on(nearest(whole), [1], 1, outward(1))
-    d0 = handed_on(mine, [1], 1, here)
     sources = [c for c in range(3, GROUPS - 2) if c % 4 != 2]
-    l1 = handed_on(whole, sources, 0, outward(1))
-    l2 = handed_on(nearest(whole), sources[::3], 0, outward(2))
-    y3 = handed_on(joined(l1, l2, mine), sources[::3], 3, here)
-    y2 = handed_on(joined(l1, mine), sources[1::3], 2, here)
-    y1 = handed_on(joined(nearest(l1), mine), sources[2::3], 1, here)
-    both = both_cores(joined(s1, s0, d1, d0))
-    state, own, plus = sweep(2, 2, both[:, :, :6], both[:, :, 6:], whole, (oc, oc))
-    minus2 = minus1 = oc
+    wide = moved(whole, legs([0], 2, outward(1)) + legs(sources, 0, outward(1)))
+    thin = moved(nearest(whole), legs([1], 1, outward(1)) + legs([3, 7, 11], 0, outward(2)))
+    inner = moved(mine, legs([0], 2, here) + legs([6, 10, 14], -2, here))
+    inner1 = moved(mine, legs([1], 1, here))
+    to_next = joined(wide, thin, mine)
+    to_last = joined(nearest(wide), mine)
+    y3 = moved(to_next, legs([3, 7, 11], 1, here))
+    y1 = moved(to_last, legs([5, 9, 13], -1, here))
+    wide, to_next, to_last = lax.optimization_barrier((wide, to_next, to_last))
+    both = both_cores(joined(wide, inner, thin, inner1, mine))
+    state, half, own, plus1 = sweep(2, 2, both[:, :, :6], both[:, :, 6:], (oc, oc))
+    plus2 = plus3 = oc
     before = None
-    for target in (6, 10, 14):
-        half = jnp.where(core == 0, state[:, :2], state[:, 2:])
-        s2 = handed_on(state, [target - 4], 4, outward(2))
-        s1 = handed_on(state, [target - 4], 4, outward(1))
-        s0 = handed_on(half, [target - 4], 4, here)
+    for target, by in ((4, 2), (8, 4), (12, 4)):
+        s2 = moved(state, legs([target - by], by, outward(2)))
+        s1 = moved(state, legs([target - by], by, outward(1)))
+        s0 = moved(half, legs([target - by], by, here))
         if before is None:
-            before = both_cores(joined(after(y3, state), y2, y1))
+            before = both_cores(joined(after(y3, state), wide, mine, y1, inner))
             change = after(fine_change(ends, oc), before)
-            previous = handed_on(change, range(GROUPS), 1, here)
+            previous = moved(change, legs(range(GROUPS), 1, here))
             s1 = after(s1, before)
         both = both_cores(joined(s1, s2, s0))
-        state, minus2, minus1, own, plus = sweep(target, 4, both, before, whole, (minus2, minus1, own, plus))
-    plus = handed_on(plus, [0, 2, 6, 10, 14], 1, here)
-    minus1 = handed_on(minus1, [6, 10, 14], -1, here)
-    minus2 = handed_on(minus2, [6, 10, 14], -2, here)
-    return final(initial, previous, own, plus, minus1, minus2)[None]
+        state, half, own, plus1, plus2, plus3 = sweep(target, 4, both, before, (own, plus1, plus2, plus3))
+    plus3 = moved(plus3, legs([4, 8, 12], 3, here))
+    plus2 = moved(plus2, legs([4, 8, 12], 2, here))
+    plus1 = moved(plus1, legs([0, 2, 4, 8, 12], 1, here))
+    return final(initial, previous, own, plus1, plus2, plus3)[None]
 
 
 def solution(mesh):

time: 161 us -> 153 us (0.950)
  the two profiles are of different devices: /device:TPU:100 before, /device:TPU:124 now
where the time goes in v5:
time: 153 us; the launch traced here: 152 us
  waiting for transfers between devices  73.4 us (48%)
  starting transfers between devices  42 us (27%)
  Pallas kernels  21.6 us (14%)
  blocking collectives  13.3 us (9%)
    ppermute x19, waiting for transfers between devices, moved(): return lax.ppermute(value, AXES, table)  47.2 us
    ppermute x2, waiting for transfers between devices, shards(): near = lax.ppermute(field, 'space', across)  22.3 us
    ppermute x2, starting transfers between devices, shards(): near = lax.ppermute(field, 'space', across)  16.2 us
    ppermute x19, starting transfers between devices, moved(): return lax.ppermute(value, AXES, table)  13.9 us
    all_gather x6, blocking collectives, both_cores(): lax.all_gather(value, 'space', axis=0, tiled=False, axis_index_groups=PAIRS)  13.3 us
    pallas_call x2, Pallas kernels, fine_round(): pl.pallas_call(functools.partial(fine_kernel, last), out_shape=(shape, co...  12.6 us
    pallas_call x4, Pallas kernels, sweep(): pl.pallas_call(functools.partial(sweep_kernel, target, depth), out_shape=...  6.69 us
    ppermute x2, starting transfers between devices, shards(): sibling = lax.ppermute(field, 'space', swap)  4.05 us
  transfers between devices with their start and end apart: 27, of which 6 were waited for; matrix products, arithmetic and copies ran while one was open for 0% of the time, Pallas kernels for 4%

profile of v5, /device:TPU:124, one launch (start us, length us, event | category | flops | bytes accessed | tf_op | source)
XLA Modules:
  0.0 152.1 jit_solution(7247964858822106523)
XLA Ops:
  0.0 9.4 %collective-permute-start.1 = (f32[3,4,64,128]{3,2,1,0:T(8,128)}, f32[3,4,64,128]{3,2,1,0:T(8,128)S(1)}, u32[]{:S(2)}, u32[]{:S(2)}) collective-permute-start(f32[3,4,64,128]{3,2,1,0:T(8,128)} %bitcast.10), channel_id=1, source_target_pairs={{1,2},{2,1},{3,4},{4,3},{5,6},{6,5},{7,8},{8,7},{9,10},{10,9},{11,... | collective-permute-start | bytes 1179656 | tf_op jit(solution)/shard_map/ppermute | solution.py:414
  9.4 1.9 %collective-permute-start.2 = (f32[3,4,64,128]{3,2,1,0:T(8,128)}, f32[3,4,64,128]{3,2,1,0:T(8,128)S(1)}, u32[]{:S(2)}, u32[]{:S(2)}) collective-permute-start(f32[3,4,64,128]{3,2,1,0:T(8,128)} %bitcast.11), channel_id=1, source_target_pairs={{0,2},{2,4},{4,6},{6,8},{8,10},{10,12},{12,14},{14,16},{16,18},{18... | collective-permute-start | bytes 1179656 | tf_op jit(solution)/shard_map/ppermute | solution.py:415
  11.4 2.0 %collective-permute-start = (f32[3,4,64,128]{3,2,1,0:T(8,128)}, f32[3,4,64,128]{3,2,1,0:T(8,128)S(1)}, u32[]{:S(2)}, u32[]{:S(2)}) collective-permute-start(f32[3,4,64,128]{3,2,1,0:T(8,128)} %bitcast.12), channel_id=1, source_target_pairs={{0,1},{1,0},{2,3},{3,2},{4,5},{5,4},{6,7},{7,6},{8,9},{9,8},{10,11... | collective-permute-start | bytes 1179656 | tf_op jit(solution)/shard_map/ppermute | solution.py:416
  13.4 10.7 %collective-permute-done.1.near_ref = f32[3,4,64,128]{3,2,1,0:T(8,128)S(1)} collective-permute-done((f32[3,4,64,128]{3,2,1,0:T(8,128)}, f32[3,4,64,128]{3,2,1,0:T(8,128)S(1)}, u32[]{:S(2)}, u32[]{:S(2)}) %collective-permute-start.1) | collective-permute-done | bytes 393248 | tf_op jit(solution)/shard_map/ppermute | solution.py:414
  24.1 1.9 %collective-permute-start.3 = (f32[3,4,64,128]{3,2,1,0:T(8,128)S(1)}, f32[3,4,64,128]{3,2,1,0:T(8,128)S(1)}, u32[]{:S(2)}, u32[]{:S(2)}) collective-permute-start(f32[3,4,64,128]{3,2,1,0:T(8,128)S(1)} %collective-permute-done.1.near_ref), channel_id=1, source_target_pairs={{0,1},{1,0},{2,3},{3,2},{4,5},{5,4},{6,7},{7,6},{8,9},{9,8},{10,11... | collective-permute-start | bytes 1179656 | tf_op jit(solution)/shard_map/ppermute | solution.py:417
  26.0 1.0 collective-permute-done.2.far_ref
  27.0 0.7 collective-permute-done.3.beyond_ref
  27.7 1.0 copy-done
  28.7 6.2 %fine_steps.1.mid_ref = f32[3,4,64,128]{3,2,1,0:T(8,128)S(1)} custom-call(f32[3,4,64,128]{3,2,1,0:T(8,128)S(1)} %bitcast.13, f32[3,4,64,128]{3,2,1,0:T(8,128)S(1)} %collective-permute-done.sibling_ref, f32[3,4,64,128]{3,2,1,0:T(8,128)S(1)} %collective-permute-done.1.near_ref, f32[3,4,64,128]{3,2,1,0:T(8,128)S(1)} %collective-permute-done.2.far_ref, ...), custom_call_target="tpu_custom_call" | custom-call | flops 120000000 | bytes 2800000 | tf_op jit(solution)/shard_map/fine_steps/pallas_call | solution.py:192
  34.9 6.8 %collective-permute-start.5 = (f32[3,4,64,128]{3,2,1,0:T(8,128)S(1)}, f32[3,4,64,128]{3,2,1,0:T(8,128)S(1)}, u32[]{:S(2)}, u32[]{:S(2)}) collective-permute-start(f32[3,4,64,128]{3,2,1,0:T(8,128)S(1)} %fine_steps.1.mid_ref), channel_id=1, source_target_pairs={{1,2},{2,1},{3,4},{4,3},{5,6},{6,5},{7,8},{8,7},{9,10},{10,9},{11,... | collective-permute-start | bytes 1179656 | tf_op jit(solution)/shard_map/ppermute | solution.py:414
  41.7 1.9 %collective-permute-start.6 = (f32[3,4,64,128]{3,2,1,0:T(8,128)S(1)}, f32[3,4,64,128]{3,2,1,0:T(8,128)S(1)}, u32[]{:S(2)}, u32[]{:S(2)}) collective-permute-start(f32[3,4,64,128]{3,2,1,0:T(8,128)S(1)} %fine_steps.1.mid_ref), channel_id=1, source_target_pairs={{0,2},{2,4},{4,6},{6,8},{8,10},{10,12},{12,14},{14,16},{16,18},{18... | collective-permute-start | bytes 1179656 | tf_op jit(solution)/shard_map/ppermute | solution.py:415
  43.6 2.0 %collective-permute-start.4 = (f32[3,4,64,128]{3,2,1,0:T(8,128)S(1)}, f32[3,4,64,128]{3,2,1,0:T(8,128)S(1)}, u32[]{:S(2)}, u32[]{:S(2)}) collective-permute-start(f32[3,4,64,128]{3,2,1,0:T(8,128)S(1)} %fine_steps.1.mid_ref), channel_id=1, source_target_pairs={{0,1},{1,0},{2,3},{3,2},{4,5},{5,4},{6,7},{7,6},{8,9},{9,8},{10,11... | collective-permute-start | bytes 1179656 | tf_op jit(solution)/shard_map/ppermute | solution.py:416
  45.6 11.6 %collective-permute-done.5.near_ref = f32[3,4,64,128]{3,2,1,0:T(8,128)S(1)} collective-permute-done((f32[3,4,64,128]{3,2,1,0:T(8,128)S(1)}, f32[3,4,64,128]{3,2,1,0:T(8,128)S(1)}, u32[]{:S(2)}, u32[]{:S(2)}) %collective-permute-start.5) | collective-permute-done | bytes 393248 | tf_op jit(solution)/shard_map/ppermute | solution.py:414
  57.2 2.1 %collective-permute-start.7 = (f32[3,4,64,128]{3,2,1,0:T(8,128)S(1)}, f32[3,4,64,128]{3,2,1,0:T(8,128)S(1)}, u32[]{:S(2)}, u32[]{:S(2)}) collective-permute-start(f32[3,4,64,128]{3,2,1,0:T(8,128)S(1)} %collective-permute-done.5.near_ref), channel_id=1, source_target_pairs={{0,1},{1,0},{2,3},{3,2},{4,5},{5,4},{6,7},{7,6},{8,9},{9,8},{10,11... | collective-permute-start | bytes 1179656 | tf_op jit(solution)/shard_map/ppermute | solution.py:417
  60.0 2.2 %collective-permute-done.6.far_ref = f32[3,4,64,128]{3,2,1,0:T(8,128)S(1)} collective-permute-done((f32[3,4,64,128]{3,2,1,0:T(8,128)S(1)}, f32[3,4,64,128]{3,2,1,0:T(8,128)S(1)}, u32[]{:S(2)}, u32[]{:S(2)}) %collective-permute-start.6) | collective-permute-done | bytes 393248 | tf_op jit(solution)/shard_map/ppermute | solution.py:415
  62.2 6.4 %fine_last.1 = (f32[3,4,64,128]{3,2,1,0:T(8,128)S(1)}, f32[3,2,16,128]{3,2,1,0:T(8,128)S(1)}) custom-call(f32[3,4,64,128]{3,2,1,0:T(8,128)S(1)} %fine_steps.1.mid_ref, f32[3,4,64,128]{3,2,1,0:T(8,128)S(1)} %collective-permute-done.4.sibling_ref, f32[3,4,64,128]{3,2,1,0:T(8,128)S(1)} %collective-permute-done.5.near_ref, ...), custom_call_target="tpu_custom_call" | custom-call | flops 120000000 | bytes 2800000 | tf_op jit(solution)/shard_map/fine_last/pallas_call | solution.py:192
  68.7 1.9 %all-gather = f32[6,2,16,128]{3,2,1,0:T(8,128)S(1)} all-gather(f32[3,2,16,128]{3,2,1,0:T(8,128)S(1)} %get-tuple-element.32), channel_id=2, replica_groups={{0,1},{2,3},{4,5},{6,7},{8,9},{10,11},{12,13},{14,15},{16,17},{18,19},{..., dimensions={0}, use_global_device_ids=true | all-gather | bytes 147456 | tf_op jit(solution)/shard_map/all_gather | solution.py:394
  70.6 0.7 collective-permute-start.8
  74.0 0.7 collective-permute-start.10
  74.8 2.2 %all-gather.1 = f32[6,12,16,128]{3,2,1,0:T(8,128)S(1)} all-gather(f32[3,12,16,128]{3,2,1,0:T(8,128)S(1)} %constant_dynamic-update-slice_fusion.3), channel_id=3, replica_groups={{0,1},{2,3},{4,5},{6,7},{8,9},{10,11},{12,13},{14,15},{16,17},{18,19},{..., dimensions={0}, use_global_device_ids=true | all-gather | bytes 884736 | tf_op jit(solution)/shard_map/all_gather | solution.py:394
  77.7 0.7 collective-permute-start.16
  79.8 2.5 %all-gather.2 = f32[6,20,16,128]{3,2,1,0:T(8,128)S(1)} all-gather(f32[3,20,16,128]{3,2,1,0:T(8,128)S(1)} %constant_dynamic-update-slice_fusion.8), channel_id=4, replica_groups={{0,1},{2,3},{4,5},{6,7},{8,9},{10,11},{12,13},{14,15},{16,17},{18,19},{..., dimensions={0}, use_global_device_ids=true | all-gather | bytes 1474560 | tf_op jit(solution)/shard_map/all_gather | solution.py:394
  82.4 2.2 %all-gather.3 = f32[6,10,16,128]{3,2,1,0:T(8,128)S(1)} all-gather(f32[3,10,16,128]{3,2,1,0:T(8,128)S(1)} %pad_maximum_fusion), channel_id=5, replica_groups={{0,1},{2,3},{4,5},{6,7},{8,9},{10,11},{12,13},{14,15},{16,17},{18,19},{..., dimensions={0}, use_global_device_ids=true | all-gather | bytes 737280 | tf_op jit(solution)/shard_map/all_gather | solution.py:394
  84.6 1.8 %sweep_4.3 = (f32[3,4,16,128]{3,2,1,0:T(8,128)S(1)}, f32[3,2,16,128]{3,2,1,0:T(8,128)S(1)}, f32[3,2,16,128]{3,2,1,0:T(8,128)S(1)}, f32[3,2,16,128]{3,2,1,0:T(8,1...) custom-call(f32[2,3,10,16,128]{4,3,2,1,0:T(8,128)S(1)} %bitcast.18, ...), custom_call_target="tpu_custom_call" | custom-call | flops 4000000 | bytes 900000 | tf_op jit(solution)/shard_map/sweep_4/pallas_call | solution.py:326
  88.8 1.3 collective-permute-start.14
  90.2 2.4 %all-gather.4 = f32[6,10,16,128]{3,2,1,0:T(8,128)S(1)} all-gather(f32[3,10,16,128]{3,2,1,0:T(8,128)S(1)} %pad_maximum_fusion.1), channel_id=6, replica_groups={{0,1},{2,3},{4,5},{6,7},{8,9},{10,11},{12,13},{14,15},{16,17},{18,19},{..., dimensions={0}, use_global_device_ids=true | all-gather | bytes 737280 | tf_op jit(solution)/shard_map/all_gather | solution.py:394
  92.6 1.8 %sweep_4.4 = (f32[3,4,16,128]{3,2,1,0:T(8,128)S(1)}, f32[3,2,16,128]{3,2,1,0:T(8,128)S(1)}, f32[3,2,16,128]{3,2,1,0:T(8,128)S(1)}, f32[3,2,16,128]{3,2,1,0:T(8,1...) custom-call(f32[2,3,10,16,128]{4,3,2,1,0:T(8,128)S(1)} %bitcast.17, ...), custom_call_target="tpu_custom_call" | custom-call | flops 4000000 | bytes 900000 | tf_op jit(solution)/shard_map/sweep_4/pallas_call | solution.py:326
  96.5 2.2 %all-gather.5 = f32[6,10,16,128]{3,2,1,0:T(8,128)S(1)} all-gather(f32[3,10,16,128]{3,2,1,0:T(8,128)S(1)} %pad_maximum_fusion.2), channel_id=7, replica_groups={{0,1},{2,3},{4,5},{6,7},{8,9},{10,11},{12,13},{14,15},{16,17},{18,19},{..., dimensions={0}, use_global_device_ids=true | all-gather | bytes 737280 | tf_op jit(solution)/shard_map/all_gather | solution.py:394
  98.6 2.5 %sweep_4.5 = (f32[3,4,16,128]{3,2,1,0:T(8,128)}, f32[3,2,16,128]{3,2,1,0:T(8,128)}, f32[3,2,16,128]{3,2,1,0:T(8,128)S(1)}, f32[3,2,16,128]{3,2,1,0:T(8,128)S(1)}...) custom-call(f32[2,3,10,16,128]{4,3,2,1,0:T(8,128)S(1)} %bitcast.16, f32[2,3,20,16,128]{4,3,2,1,0:T(8,128)S(1)} %bitcast.9, ...), custom_call_target="tpu_custom_call" | custom-call | flops 4000000 | bytes 900000 | tf_op jit(solution)/shard_map/sweep_4/pallas_call | solution.py:326
  102.4 1.3 collective-permute-start.26
  103.7 47.1 %collective-permute-done.26.c_ref = f32[3,2,16,128]{3,2,1,0:T(8,128)S(1)} collective-permute-done((f32[3,2,16,128]{3,2,1,0:T(8,128)S(1)}, f32[3,2,16,128]{3,2,1,0:T(8,128)S(1)}, u32[]{:S(2)}, u32[]{:S(2)}) %collective-permute-start.26) | collective-permute-done | bytes 49184 | tf_op jit(solution)/shard_map/ppermute | solution.py:382
  150.9 1.2 final.1
  (62 shorter events, 11.3 us)
Async XLA Ops:
  0.0 24.1 %collective-permute-start.1 = (f32[3,4,64,128]{3,2,1,0:T(8,128)}, f32[3,4,64,128]{3,2,1,0:T(8,128)S(1)}, u32[]{:S(2)}, u32[]{:S(2)}) collective-permute-start(f32[3,4,64,128]{3,2,1,0:T(8,128)} %bitcast.10), channel_id=1, source_target_pairs={{1,2},{2,1},{3,4},{4,3},{5,6},{6,5},{7,8},{8,7},{9,10},{10,9},{11,... | collective-permute-start | bytes 1179656 | tf_op jit(solution)/shard_map/ppermute | solution.py:414
  9.4 17.5 %collective-permute-start.2 = (f32[3,4,64,128]{3,2,1,0:T(8,128)}, f32[3,4,64,128]{3,2,1,0:T(8,128)S(1)}, u32[]{:S(2)}, u32[]{:S(2)}) collective-permute-start(f32[3,4,64,128]{3,2,1,0:T(8,128)} %bitcast.11), channel_id=1, source_target_pairs={{0,2},{2,4},{4,6},{6,8},{8,10},{10,12},{12,14},{14,16},{16,18},{18... | collective-permute-start | bytes 1179656 | tf_op jit(solution)/shard_map/ppermute | solution.py:415
  11.4 15.6 %collective-permute-start = (f32[3,4,64,128]{3,2,1,0:T(8,128)}, f32[3,4,64,128]{3,2,1,0:T(8,128)S(1)}, u32[]{:S(2)}, u32[]{:S(2)}) collective-permute-start(f32[3,4,64,128]{3,2,1,0:T(8,128)} %bitcast.12), channel_id=1, source_target_pairs={{0,1},{1,0},{2,3},{3,2},{4,5},{5,4},{6,7},{7,6},{8,9},{9,8},{10,11... | collective-permute-start | bytes 1179656 | tf_op jit(solution)/shard_map/ppermute | solution.py:416
  24.1 3.6 %collective-permute-start.3 = (f32[3,4,64,128]{3,2,1,0:T(8,128)S(1)}, f32[3,4,64,128]{3,2,1,0:T(8,128)S(1)}, u32[]{:S(2)}, u32[]{:S(2)}) collective-permute-start(f32[3,4,64,128]{3,2,1,0:T(8,128)S(1)} %collective-permute-done.1.near_ref), channel_id=1, source_target_pairs={{0,1},{1,0},{2,3},{3,2},{4,5},{5,4},{6,7},{7,6},{8,9},{9,8},{10,11... | collective-permute-start | bytes 1179656 | tf_op jit(solution)/shard_map/ppermute | solution.py:417
  27.7 1.0 copy-start
  28.7 30.7 %copy-start.1 = (f32[1,3,4,64,128]{4,3,2,1,0:T(8,128)S(1)}, f32[1,3,4,64,128]{4,3,2,1,0:T(8,128)}, u32[]{:S(2)}) copy-start(f32[1,3,4,64,128]{4,3,2,1,0:T(8,128)} %param.1) | copy-start | bytes 1179652
  34.9 22.4 %collective-permute-start.5 = (f32[3,4,64,128]{3,2,1,0:T(8,128)S(1)}, f32[3,4,64,128]{3,2,1,0:T(8,128)S(1)}, u32[]{:S(2)}, u32[]{:S(2)}) collective-permute-start(f32[3,4,64,128]{3,2,1,0:T(8,128)S(1)} %fine_steps.1.mid_ref), channel_id=1, source_target_pairs={{1,2},{2,1},{3,4},{4,3},{5,6},{6,5},{7,8},{8,7},{9,10},{10,9},{11,... | collective-permute-start | bytes 1179656 | tf_op jit(solution)/shard_map/ppermute | solution.py:414
  41.7 20.6 %collective-permute-start.6 = (f32[3,4,64,128]{3,2,1,0:T(8,128)S(1)}, f32[3,4,64,128]{3,2,1,0:T(8,128)S(1)}, u32[]{:S(2)}, u32[]{:S(2)}) collective-permute-start(f32[3,4,64,128]{3,2,1,0:T(8,128)S(1)} %fine_steps.1.mid_ref), channel_id=1, source_target_pairs={{0,2},{2,4},{4,6},{6,8},{8,10},{10,12},{12,14},{14,16},{16,18},{18... | collective-permute-start | bytes 1179656 | tf_op jit(solution)/shard_map/ppermute | solution.py:415
  43.6 18.6 %collective-permute-start.4 = (f32[3,4,64,128]{3,2,1,0:T(8,128)S(1)}, f32[3,4,64,128]{3,2,1,0:T(8,128)S(1)}, u32[]{:S(2)}, u32[]{:S(2)}) collective-permute-start(f32[3,4,64,128]{3,2,1,0:T(8,128)S(1)} %fine_steps.1.mid_ref), channel_id=1, source_target_pairs={{0,1},{1,0},{2,3},{3,2},{4,5},{5,4},{6,7},{7,6},{8,9},{9,8},{10,11... | collective-permute-start | bytes 1179656 | tf_op jit(solution)/shard_map/ppermute | solution.py:416
  57.2 5.0 %collective-permute-start.7 = (f32[3,4,64,128]{3,2,1,0:T(8,128)S(1)}, f32[3,4,64,128]{3,2,1,0:T(8,128)S(1)}, u32[]{:S(2)}, u32[]{:S(2)}) collective-permute-start(f32[3,4,64,128]{3,2,1,0:T(8,128)S(1)} %collective-permute-done.5.near_ref), channel_id=1, source_target_pairs={{0,1},{1,0},{2,3},{3,2},{4,5},{5,4},{6,7},{7,6},{8,9},{9,8},{10,11... | collective-permute-start | bytes 1179656 | tf_op jit(solution)/shard_map/ppermute | solution.py:417
  70.6 2.7 %collective-permute-start.8 = (f32[3,4,16,128]{3,2,1,0:T(8,128)S(1)}, f32[3,4,16,128]{3,2,1,0:T(8,128)S(1)}, u32[]{:S(2)}, u32[]{:S(2)}) collective-permute-start(f32[3,4,16,128]{3,2,1,0:T(8,128)S(1)} %pad_maximum_fusion.3), channel_id=1, source_target_pairs={{0,66},{2,68},{3,65},{4,70},{5,67},{6,72},{7,69},{8,74},{9,71},{10... | collective-permute-start | bytes 294920 | tf_op jit(solution)/shard_map/ppermute | solution.py:382
  71.2 3.5 %collective-permute-start.12 = (f32[3,2,16,128]{3,2,1,0:T(8,128)S(1)}, f32[3,2,16,128]{3,2,1,0:T(8,128)S(1)}, u32[]{:S(2)}, u32[]{:S(2)}) collective-permute-start(f32[3,2,16,128]{3,2,1,0:T(8,128)S(1)} %get-tuple-element.32), channel_id=1, source_target_pairs={{32,64},{33,65},{34,66},{35,67},{36,68},{37,69},{38,70},{39,71},{4... | collective-permute-start | bytes 147464 | tf_op jit(solution)/shard_map/ppermute | solution.py:382
  71.9 2.8 %collective-permute-start.11 = (f32[3,2,16,128]{3,2,1,0:T(8,128)S(1)}, f32[3,2,16,128]{3,2,1,0:T(8,128)S(1)}, u32[]{:S(2)}, u32[]{:S(2)}) collective-permute-start(f32[3,2,16,128]{3,2,1,0:T(8,128)S(1)} %get-tuple-element.32), channel_id=1, source_target_pairs={{0,64},{1,65},{2,66},{3,67},{4,68},{5,69},{6,70},{7,71},{8,72},{9,... | collective-permute-start | bytes 147464 | tf_op jit(solution)/shard_map/ppermute | solution.py:382
  72.6 1.4 collective-permute-start.9
  73.3 6.5 %collective-permute-start.13 = (f32[3,4,16,128]{3,2,1,0:T(8,128)S(1)}, f32[3,4,16,128]{3,2,1,0:T(8,128)S(1)}, u32[]{:S(2)}, u32[]{:S(2)}) collective-permute-start(f32[3,4,16,128]{3,2,1,0:T(8,128)S(1)} %pad_maximum_fusion.4), channel_id=1, source_target_pairs={{160,128},{161,129},{162,130},{163,131},{164,132},{165,133},{166,1... | collective-permute-start | bytes 294920 | tf_op jit(solution)/shard_map/ppermute | solution.py:382
  74.0 5.7 %collective-permute-start.10 = (f32[3,8,16,128]{3,2,1,0:T(8,128)S(1)}, f32[3,8,16,128]{3,2,1,0:T(8,128)S(1)}, u32[]{:S(2)}, u32[]{:S(2)}) collective-permute-start(f32[3,8,16,128]{3,2,1,0:T(8,128)S(1)} %constant_dynamic-update-slice_fusion), channel_id=1, source_target_pairs={{96,128},{97,129},{98,130},{99,131},{100,132},{101,133},{102,134},... | collective-permute-start | bytes 589832 | tf_op jit(solution)/shard_map/ppermute | solution.py:382
  77.7 4.6 %collective-permute-start.16 = (f32[3,4,16,128]{3,2,1,0:T(8,128)S(1)}, f32[3,4,16,128]{3,2,1,0:T(8,128)S(1)}, u32[]{:S(2)}, u32[]{:S(2)}) collective-permute-start(f32[3,4,16,128]{3,2,1,0:T(8,128)S(1)} %get-tuple-element.34), channel_id=1, source_target_pairs={{64,132},{66,134},{68,136},{69,129},{70,138},{71,131},{72,140},{73... | collective-permute-start | bytes 294920 | tf_op jit(solution)/shard_map/ppermute | solution.py:382
  78.4 4.0 %collective-permute-start.15 = (f32[3,4,16,128]{3,2,1,0:T(8,128)S(1)}, f32[3,4,16,128]{3,2,1,0:T(8,128)S(1)}, u32[]{:S(2)}, u32[]{:S(2)}) collective-permute-start(f32[3,4,16,128]{3,2,1,0:T(8,128)S(1)} %get-tuple-element.34), channel_id=1, source_target_pairs={{64,130},{66,132},{67,129},{68,134},{69,131},{70,136},{71,133},{72... | collective-permute-start | bytes 294920 | tf_op jit(solution)/shard_map/ppermute | solution.py:382
  79.1 3.3 %collective-permute-start.17 = (f32[3,2,16,128]{3,2,1,0:T(8,128)S(1)}, f32[3,2,16,128]{3,2,1,0:T(8,128)S(1)}, u32[]{:S(2)}, u32[]{:S(2)}) collective-permute-start(f32[3,2,16,128]{3,2,1,0:T(8,128)S(1)} %get-tuple-element.38), channel_id=1, source_target_pairs={{64,128},{65,129},{66,130},{67,131},{68,132},{69,133},{70,134},{71... | collective-permute-start | bytes 147464 | tf_op jit(solution)/shard_map/ppermute | solution.py:382
  86.4 3.8 %collective-permute-start.19 = (f32[3,4,16,128]{3,2,1,0:T(8,128)S(1)}, f32[3,4,16,128]{3,2,1,0:T(8,128)S(1)}, u32[]{:S(2)}, u32[]{:S(2)}) collective-permute-start(f32[3,4,16,128]{3,2,1,0:T(8,128)S(1)} %get-tuple-element.41), channel_id=1, source_target_pairs={{128,260},{130,262},{132,264},{133,257},{134,266},{135,259},{136,2... | collective-permute-start | bytes 294920 | tf_op jit(solution)/shard_map/ppermute | solution.py:382
  87.0 3.1 %collective-permute-start.18 = (f32[3,4,16,128]{3,2,1,0:T(8,128)S(1)}, f32[3,4,16,128]{3,2,1,0:T(8,128)S(1)}, u32[]{:S(2)}, u32[]{:S(2)}) collective-permute-start(f32[3,4,16,128]{3,2,1,0:T(8,128)S(1)} %get-tuple-element.41), channel_id=1, source_target_pairs={{128,258},{130,260},{131,257},{132,262},{133,259},{134,264},{135,2... | collective-permute-start | bytes 294920 | tf_op jit(solution)/shard_map/ppermute | solution.py:382
  87.7 2.4 %collective-permute-start.20 = (f32[3,2,16,128]{3,2,1,0:T(8,128)S(1)}, f32[3,2,16,128]{3,2,1,0:T(8,128)S(1)}, u32[]{:S(2)}, u32[]{:S(2)}) collective-permute-start(f32[3,2,16,128]{3,2,1,0:T(8,128)S(1)} %get-tuple-element.42), channel_id=1, source_target_pairs={{128,256},{129,257},{130,258},{131,259},{132,260},{133,261},{134,2... | collective-permute-start | bytes 147464 | tf_op jit(solution)/shard_map/ppermute | solution.py:382
  88.8 62.0 %collective-permute-start.14 = (f32[3,4,64,128]{3,2,1,0:T(8,128)S(1)}, f32[3,4,64,128]{3,2,1,0:T(8,128)S(1)}, u32[]{:S(2)}, u32[]{:S(2)}) collective-permute-start(f32[3,4,64,128]{3,2,1,0:T(8,128)S(1)} %fine_change.1), channel_id=1, source_target_pairs={{0,32},{1,33},{2,34},{3,35},{4,36},{5,37},{6,38},{7,39},{8,40},{9,... | collective-permute-start | bytes 1179656 | tf_op jit(solution)/shard_map/ppermute | solution.py:382
  94.4 2.0 %collective-permute-start.22 = (f32[3,4,16,128]{3,2,1,0:T(8,128)S(1)}, f32[3,4,16,128]{3,2,1,0:T(8,128)S(1)}, u32[]{:S(2)}, u32[]{:S(2)}) collective-permute-start(f32[3,4,16,128]{3,2,1,0:T(8,128)S(1)} %get-tuple-element.47), channel_id=1, source_target_pairs={{256,388},{258,390},{260,392},{261,385},{262,394},{263,387},{264,3... | collective-permute-start | bytes 294920 | tf_op jit(solution)/shard_map/ppermute | solution.py:382
  95.1 1.4 collective-permute-start.21
  95.7 0.7 collective-permute-start.23
  101.1 2.6 %collective-permute-start.24 = (f32[3,2,16,128]{3,2,1,0:T(8,128)S(1)}, f32[3,2,16,128]{3,2,1,0:T(8,128)S(1)}, u32[]{:S(2)}, u32[]{:S(2)}) collective-permute-start(f32[3,2,16,128]{3,2,1,0:T(8,128)S(1)} %get-tuple-element.54), channel_id=1, source_target_pairs={{0,32},{1,33},{2,34},{3,35},{4,36},{5,37},{6,38},{7,39},{8,40},{9,... | collective-permute-start | bytes 147464 | tf_op jit(solution)/shard_map/ppermute | solution.py:382
  101.7 2.0 %collective-permute-start.25 = (f32[3,2,16,128]{3,2,1,0:T(8,128)S(1)}, f32[3,2,16,128]{3,2,1,0:T(8,128)S(1)}, u32[]{:S(2)}, u32[]{:S(2)}) collective-permute-start(f32[3,2,16,128]{3,2,1,0:T(8,128)S(1)} %get-tuple-element.55), channel_id=1, source_target_pairs={{128,192},{129,193},{130,194},{131,195},{132,196},{133,197},{134,1... | collective-permute-start | bytes 147464 | tf_op jit(solution)/shard_map/ppermute | solution.py:382
  102.4 48.5 %collective-permute-start.26 = (f32[3,2,16,128]{3,2,1,0:T(8,128)S(1)}, f32[3,2,16,128]{3,2,1,0:T(8,128)S(1)}, u32[]{:S(2)}, u32[]{:S(2)}) collective-permute-start(f32[3,2,16,128]{3,2,1,0:T(8,128)S(1)} %get-tuple-element.56), channel_id=1, source_target_pairs={{128,224},{129,225},{130,226},{131,227},{132,228},{133,229},{134,2... | collective-permute-start | bytes 147464 | tf_op jit(solution)/shard_map/ppermute | solution.py:382

commit v6 on v5

--- a/solution.py
+++ b/solution.py
@@ -335,7 +335,7 @@
     )(got, before, *kept)
 
 
-def final_kernel(start_ref, previous_ref, own_ref, a_ref, b_ref, c_ref, out_ref):
+def final_kernel(start_ref, low_ref, high_ref, own_ref, a_ref, b_ref, c_ref, out_ref):
     group, slab = position()
 
     @pl.when(group == 0)
@@ -354,7 +354,7 @@
                 for i in (2 * p, 2 * p + 1):
                     for start in (0, 1):
                         at = pl.ds(start, 32, stride=2)
-                        out_ref[c, i, at, :] = previous_ref[c, i, at, :] + tall
+                        out_ref[c, i, at, :] = (low_ref[c, i, at, :] + high_ref[c, i, at, :]) + tall
 
 
 def final(*arrays):
@@ -440,22 +440,23 @@
     both = both_cores(joined(wide, inner, thin, inner1, mine))
     state, half, own, plus1 = sweep(2, 2, both[:, :, :6], both[:, :, 6:], (oc, oc))
     plus2 = plus3 = oc
-    before = None
     for target, by in ((4, 2), (8, 4), (12, 4)):
         s2 = moved(state, legs([target - by], by, outward(2)))
         s1 = moved(state, legs([target - by], by, outward(1)))
         s0 = moved(half, legs([target - by], by, here))
-        if before is None:
+        if target == 4:
             before = both_cores(joined(after(y3, state), wide, mine, y1, inner))
             change = after(fine_change(ends, oc), before)
-            previous = moved(change, legs(range(GROUPS), 1, here))
+            high = moved(change, legs(range(GROUPS // 2, GROUPS), 1, here))
             s1 = after(s1, before)
         both = both_cores(joined(s1, s2, s0))
+        if target == 12:
+            low = moved(after(change, both), legs(range(GROUPS // 2), 1, here))
         state, half, own, plus1, plus2, plus3 = sweep(target, 4, both, before, (own, plus1, plus2, plus3))
     plus3 = moved(plus3, legs([4, 8, 12], 3, here))
     plus2 = moved(plus2, legs([4, 8, 12], 2, here))
     plus1 = moved(plus1, legs([0, 2, 4, 8, 12], 1, here))
-    return final(initial, previous, own, plus1, plus2, plus3)[None]
+    return final(initial, low, high, own, plus1, plus2, plus3)[None]
 
 
 def solution(mesh):

time: 153 us -> 154 us (level)
  the two profiles are of different devices: /device:TPU:124 before, /device:TPU:68 now
where the time goes in v6:
time: 154 us
  waiting for transfers between devices  64.1 us (42%)
  starting transfers between devices  51.4 us (33%)
  Pallas kernels  21.6 us (14%)
  blocking collectives  14.9 us (10%)
    ppermute x20, waiting for transfers between devices, moved(): return lax.ppermute(value, AXES, table)  37.9 us
    ppermute x20, starting transfers between devices, moved(): return lax.ppermute(value, AXES, table)  23.3 us
    ppermute x2, waiting for transfers between devices, shards(): near = lax.ppermute(field, 'space', across)  22.3 us
    ppermute x2, starting transfers between devices, shards(): near = lax.ppermute(field, 'space', across)  16.2 us
    all_gather x6, blocking collectives, both_cores(): lax.all_gather(value, 'space', axis=0, tiled=False, axis_index_groups=PAIRS)  14.9 us
    pallas_call x2, Pallas kernels, fine_round(): pl.pallas_call(functools.partial(fine_kernel, last), out_shape=(shape, co...  12.6 us
    pallas_call x4, Pallas kernels, sweep(): pl.pallas_call(functools.partial(sweep_kernel, target, depth), out_shape=...  6.69 us
    ppermute x2, starting transfers between devices, shards(): sibling = lax.ppermute(field, 'space', swap)  4.05 us
  transfers between devices with their start and end apart: 28, of which 13 were waited for; matrix products, arithmetic and copies ran while one was open for 0% of the time, Pallas kernels for 3%

profile of v6, /device:TPU:68, one launch (start us, length us, event | category | flops | bytes accessed | tf_op | source)
XLA Modules:
  0.0 153.7 jit_solution(17991593199725192737)
XLA Ops:
  0.0 9.4 %collective-permute-start.1 = (f32[3,4,64,128]{3,2,1,0:T(8,128)}, f32[3,4,64,128]{3,2,1,0:T(8,128)S(1)}, u32[]{:S(2)}, u32[]{:S(2)}) collective-permute-start(f32[3,4,64,128]{3,2,1,0:T(8,128)} %bitcast.10), channel_id=1, source_target_pairs={{1,2},{2,1},{3,4},{4,3},{5,6},{6,5},{7,8},{8,7},{9,10},{10,9},{11,... | collective-permute-start | bytes 1179656 | tf_op jit(solution)/shard_map/ppermute | solution.py:414
  9.4 1.9 %collective-permute-start.2 = (f32[3,4,64,128]{3,2,1,0:T(8,128)}, f32[3,4,64,128]{3,2,1,0:T(8,128)S(1)}, u32[]{:S(2)}, u32[]{:S(2)}) collective-permute-start(f32[3,4,64,128]{3,2,1,0:T(8,128)} %bitcast.11), channel_id=1, source_target_pairs={{0,2},{2,4},{4,6},{6,8},{8,10},{10,12},{12,14},{14,16},{16,18},{18... | collective-permute-start | bytes 1179656 | tf_op jit(solution)/shard_map/ppermute | solution.py:415
  11.4 2.0 %collective-permute-start = (f32[3,4,64,128]{3,2,1,0:T(8,128)}, f32[3,4,64,128]{3,2,1,0:T(8,128)S(1)}, u32[]{:S(2)}, u32[]{:S(2)}) collective-permute-start(f32[3,4,64,128]{3,2,1,0:T(8,128)} %bitcast.12), channel_id=1, source_target_pairs={{0,1},{1,0},{2,3},{3,2},{4,5},{5,4},{6,7},{7,6},{8,9},{9,8},{10,11... | collective-permute-start | bytes 1179656 | tf_op jit(solution)/shard_map/ppermute | solution.py:416
  13.4 10.7 %collective-permute-done.1.near_ref = f32[3,4,64,128]{3,2,1,0:T(8,128)S(1)} collective-permute-done((f32[3,4,64,128]{3,2,1,0:T(8,128)}, f32[3,4,64,128]{3,2,1,0:T(8,128)S(1)}, u32[]{:S(2)}, u32[]{:S(2)}) %collective-permute-start.1) | collective-permute-done | bytes 393248 | tf_op jit(solution)/shard_map/ppermute | solution.py:414
  24.1 1.9 %collective-permute-start.3 = (f32[3,4,64,128]{3,2,1,0:T(8,128)S(1)}, f32[3,4,64,128]{3,2,1,0:T(8,128)S(1)}, u32[]{:S(2)}, u32[]{:S(2)}) collective-permute-start(f32[3,4,64,128]{3,2,1,0:T(8,128)S(1)} %collective-permute-done.1.near_ref), channel_id=1, source_target_pairs={{0,1},{1,0},{2,3},{3,2},{4,5},{5,4},{6,7},{7,6},{8,9},{9,8},{10,11... | collective-permute-start | bytes 1179656 | tf_op jit(solution)/shard_map/ppermute | solution.py:417
  28.7 6.2 %fine_steps.1.mid_ref = f32[3,4,64,128]{3,2,1,0:T(8,128)S(1)} custom-call(f32[3,4,64,128]{3,2,1,0:T(8,128)S(1)} %bitcast.13, f32[3,4,64,128]{3,2,1,0:T(8,128)S(1)} %collective-permute-done.sibling_ref, f32[3,4,64,128]{3,2,1,0:T(8,128)S(1)} %collective-permute-done.1.near_ref, f32[3,4,64,128]{3,2,1,0:T(8,128)S(1)} %collective-permute-done.2.far_ref, ...), custom_call_target="tpu_custom_call" | custom-call | flops 120000000 | bytes 2800000 | tf_op jit(solution)/shard_map/fine_steps/pallas_call | solution.py:192
  34.9 6.8 %collective-permute-start.5 = (f32[3,4,64,128]{3,2,1,0:T(8,128)S(1)}, f32[3,4,64,128]{3,2,1,0:T(8,128)S(1)}, u32[]{:S(2)}, u32[]{:S(2)}) collective-permute-start(f32[3,4,64,128]{3,2,1,0:T(8,128)S(1)} %fine_steps.1.mid_ref), channel_id=1, source_target_pairs={{1,2},{2,1},{3,4},{4,3},{5,6},{6,5},{7,8},{8,7},{9,10},{10,9},{11,... | collective-permute-start | bytes 1179656 | tf_op jit(solution)/shard_map/ppermute | solution.py:414
  41.7 1.9 %collective-permute-start.6 = (f32[3,4,64,128]{3,2,1,0:T(8,128)S(1)}, f32[3,4,64,128]{3,2,1,0:T(8,128)S(1)}, u32[]{:S(2)}, u32[]{:S(2)}) collective-permute-start(f32[3,4,64,128]{3,2,1,0:T(8,128)S(1)} %fine_steps.1.mid_ref), channel_id=1, source_target_pairs={{0,2},{2,4},{4,6},{6,8},{8,10},{10,12},{12,14},{14,16},{16,18},{18... | collective-permute-start | bytes 1179656 | tf_op jit(solution)/shard_map/ppermute | solution.py:415
  43.6 2.0 %collective-permute-start.4 = (f32[3,4,64,128]{3,2,1,0:T(8,128)S(1)}, f32[3,4,64,128]{3,2,1,0:T(8,128)S(1)}, u32[]{:S(2)}, u32[]{:S(2)}) collective-permute-start(f32[3,4,64,128]{3,2,1,0:T(8,128)S(1)} %fine_steps.1.mid_ref), channel_id=1, source_target_pairs={{0,1},{1,0},{2,3},{3,2},{4,5},{5,4},{6,7},{7,6},{8,9},{9,8},{10,11... | collective-permute-start | bytes 1179656 | tf_op jit(solution)/shard_map/ppermute | solution.py:416
  45.6 11.6 %collective-permute-done.5.near_ref = f32[3,4,64,128]{3,2,1,0:T(8,128)S(1)} collective-permute-done((f32[3,4,64,128]{3,2,1,0:T(8,128)S(1)}, f32[3,4,64,128]{3,2,1,0:T(8,128)S(1)}, u32[]{:S(2)}, u32[]{:S(2)}) %collective-permute-start.5) | collective-permute-done | bytes 393248 | tf_op jit(solution)/shard_map/ppermute | solution.py:414
  57.2 2.1 %collective-permute-start.7 = (f32[3,4,64,128]{3,2,1,0:T(8,128)S(1)}, f32[3,4,64,128]{3,2,1,0:T(8,128)S(1)}, u32[]{:S(2)}, u32[]{:S(2)}) collective-permute-start(f32[3,4,64,128]{3,2,1,0:T(8,128)S(1)} %collective-permute-done.5.near_ref), channel_id=1, source_target_pairs={{0,1},{1,0},{2,3},{3,2},{4,5},{5,4},{6,7},{7,6},{8,9},{9,8},{10,11... | collective-permute-start | bytes 1179656 | tf_op jit(solution)/shard_map/ppermute | solution.py:417
  60.0 2.2 %collective-permute-done.6.far_ref = f32[3,4,64,128]{3,2,1,0:T(8,128)S(1)} collective-permute-done((f32[3,4,64,128]{3,2,1,0:T(8,128)S(1)}, f32[3,4,64,128]{3,2,1,0:T(8,128)S(1)}, u32[]{:S(2)}, u32[]{:S(2)}) %collective-permute-start.6) | collective-permute-done | bytes 393248 | tf_op jit(solution)/shard_map/ppermute | solution.py:415
  62.2 6.4 %fine_last.1 = (f32[3,4,64,128]{3,2,1,0:T(8,128)S(1)}, f32[3,2,16,128]{3,2,1,0:T(8,128)S(1)}) custom-call(f32[3,4,64,128]{3,2,1,0:T(8,128)S(1)} %fine_steps.1.mid_ref, f32[3,4,64,128]{3,2,1,0:T(8,128)S(1)} %collective-permute-done.4.sibling_ref, f32[3,4,64,128]{3,2,1,0:T(8,128)S(1)} %collective-permute-done.5.near_ref, ...), custom_call_target="tpu_custom_call" | custom-call | flops 120000000 | bytes 2800000 | tf_op jit(solution)/shard_map/fine_last/pallas_call | solution.py:192
  68.7 1.9 %all-gather = f32[6,2,16,128]{3,2,1,0:T(8,128)S(1)} all-gather(f32[3,2,16,128]{3,2,1,0:T(8,128)S(1)} %get-tuple-element.33), channel_id=2, replica_groups={{0,1},{2,3},{4,5},{6,7},{8,9},{10,11},{12,13},{14,15},{16,17},{18,19},{..., dimensions={0}, use_global_device_ids=true | all-gather | bytes 147456 | tf_op jit(solution)/shard_map/all_gather | solution.py:394
  70.6 1.9 %collective-permute-start.8 = (f32[3,4,16,128]{3,2,1,0:T(8,128)S(1)}, f32[3,4,16,128]{3,2,1,0:T(8,128)S(1)}, u32[]{:S(2)}, u32[]{:S(2)}) collective-permute-start(f32[3,4,16,128]{3,2,1,0:T(8,128)S(1)} %pad_maximum_fusion.3), channel_id=1, source_target_pairs={{0,66},{2,68},{3,65},{4,70},{5,67},{6,72},{7,69},{8,74},{9,71},{10... | collective-permute-start | bytes 294920 | tf_op jit(solution)/shard_map/ppermute | solution.py:382
  75.1 4.9 %collective-permute-done.8 = f32[3,4,16,128]{3,2,1,0:T(8,128)S(1)} collective-permute-done((f32[3,4,16,128]{3,2,1,0:T(8,128)S(1)}, f32[3,4,16,128]{3,2,1,0:T(8,128)S(1)}, u32[]{:S(2)}, u32[]{:S(2)}) %collective-permute-start.8) | collective-permute-done | bytes 98336 | tf_op jit(solution)/shard_map/ppermute | solution.py:382
  82.9 2.2 %all-gather.1 = f32[6,12,16,128]{3,2,1,0:T(8,128)S(1)} all-gather(f32[3,12,16,128]{3,2,1,0:T(8,128)S(1)} %constant_dynamic-update-slice_fusion.3), channel_id=3, replica_groups={{0,1},{2,3},{4,5},{6,7},{8,9},{10,11},{12,13},{14,15},{16,17},{18,19},{..., dimensions={0}, use_global_device_ids=true | all-gather | bytes 884736 | tf_op jit(solution)/shard_map/all_gather | solution.py:394
  87.8 7.6 %collective-permute-done.10 = f32[3,8,16,128]{3,2,1,0:T(8,128)S(1)} collective-permute-done((f32[3,8,16,128]{3,2,1,0:T(8,128)S(1)}, f32[3,8,16,128]{3,2,1,0:T(8,128)S(1)}, u32[]{:S(2)}, u32[]{:S(2)}) %collective-permute-start.10) | collective-permute-done | bytes 196640 | tf_op jit(solution)/shard_map/ppermute | solution.py:382
  95.5 4.1 %all-gather.2 = f32[6,20,16,128]{3,2,1,0:T(8,128)S(1)} all-gather(f32[3,20,16,128]{3,2,1,0:T(8,128)S(1)} %constant_dynamic-update-slice_fusion.8), channel_id=4, replica_groups={{0,1},{2,3},{4,5},{6,7},{8,9},{10,11},{12,13},{14,15},{16,17},{18,19},{..., dimensions={0}, use_global_device_ids=true | all-gather | bytes 1474560 | tf_op jit(solution)/shard_map/all_gather | solution.py:394
  99.6 2.2 %all-gather.3 = f32[6,10,16,128]{3,2,1,0:T(8,128)S(1)} all-gather(f32[3,10,16,128]{3,2,1,0:T(8,128)S(1)} %pad_maximum_fusion), channel_id=5, replica_groups={{0,1},{2,3},{4,5},{6,7},{8,9},{10,11},{12,13},{14,15},{16,17},{18,19},{..., dimensions={0}, use_global_device_ids=true | all-gather | bytes 737280 | tf_op jit(solution)/shard_map/all_gather | solution.py:394
  101.8 1.8 %sweep_4.3 = (f32[3,4,16,128]{3,2,1,0:T(8,128)S(1)}, f32[3,2,16,128]{3,2,1,0:T(8,128)S(1)}, f32[3,2,16,128]{3,2,1,0:T(8,128)S(1)}, f32[3,2,16,128]{3,2,1,0:T(8,1...) custom-call(f32[2,3,10,16,128]{4,3,2,1,0:T(8,128)S(1)} %bitcast.18, ...), custom_call_target="tpu_custom_call" | custom-call | flops 4000000 | bytes 900000 | tf_op jit(solution)/shard_map/sweep_4/pallas_call | solution.py:326
  107.5 14.9 %collective-permute-done.19 = f32[3,2,16,128]{3,2,1,0:T(8,128)S(1)} collective-permute-done((f32[3,2,16,128]{3,2,1,0:T(8,128)S(1)}, f32[3,2,16,128]{3,2,1,0:T(8,128)S(1)}, u32[]{:S(2)}, u32[]{:S(2)}) %collective-permute-start.19) | collective-permute-done | bytes 49184 | tf_op jit(solution)/shard_map/ppermute | solution.py:382
  123.5 2.4 %all-gather.4 = f32[6,10,16,128]{3,2,1,0:T(8,128)S(1)} all-gather(f32[3,10,16,128]{3,2,1,0:T(8,128)S(1)} %pad_maximum_fusion.1), channel_id=6, replica_groups={{0,1},{2,3},{4,5},{6,7},{8,9},{10,11},{12,13},{14,15},{16,17},{18,19},{..., dimensions={0}, use_global_device_ids=true | all-gather | bytes 737280 | tf_op jit(solution)/shard_map/all_gather | solution.py:394
  125.8 1.8 %sweep_4.4 = (f32[3,4,16,128]{3,2,1,0:T(8,128)S(1)}, f32[3,2,16,128]{3,2,1,0:T(8,128)S(1)}, f32[3,2,16,128]{3,2,1,0:T(8,128)S(1)}, f32[3,2,16,128]{3,2,1,0:T(8,1...) custom-call(f32[2,3,10,16,128]{4,3,2,1,0:T(8,128)S(1)} %bitcast.17, ...), custom_call_target="tpu_custom_call" | custom-call | flops 4000000 | bytes 900000 | tf_op jit(solution)/shard_map/sweep_4/pallas_call | solution.py:326
  127.7 1.3 collective-permute-start.21
  129.0 1.3 collective-permute-start.20
  132.0 1.3 collective-permute-start.24
  133.3 1.9 %collective-permute-done.22 = f32[3,2,16,128]{3,2,1,0:T(8,128)S(1)} collective-permute-done((f32[3,2,16,128]{3,2,1,0:T(8,128)S(1)}, f32[3,2,16,128]{3,2,1,0:T(8,128)S(1)}, u32[]{:S(2)}, u32[]{:S(2)}) %collective-permute-start.22) | collective-permute-done | bytes 49184 | tf_op jit(solution)/shard_map/ppermute | solution.py:382
  135.2 2.2 %all-gather.5 = f32[6,10,16,128]{3,2,1,0:T(8,128)S(1)} all-gather(f32[3,10,16,128]{3,2,1,0:T(8,128)S(1)} %pad_maximum_fusion.2), channel_id=7, replica_groups={{0,1},{2,3},{4,5},{6,7},{8,9},{10,11},{12,13},{14,15},{16,17},{18,19},{..., dimensions={0}, use_global_device_ids=true | all-gather | bytes 737280 | tf_op jit(solution)/shard_map/all_gather | solution.py:394
  138.7 2.5 %sweep_4.5 = (f32[3,4,16,128]{3,2,1,0:T(8,128)}, f32[3,2,16,128]{3,2,1,0:T(8,128)}, f32[3,2,16,128]{3,2,1,0:T(8,128)S(1)}, f32[3,2,16,128]{3,2,1,0:T(8,128)S(1)}...) custom-call(f32[2,3,10,16,128]{4,3,2,1,0:T(8,128)S(1)} %bitcast.16, f32[2,3,20,16,128]{4,3,2,1,0:T(8,128)S(1)} %bitcast.9, ...), custom_call_target="tpu_custom_call" | custom-call | flops 4000000 | bytes 900000 | tf_op jit(solution)/shard_map/sweep_4/pallas_call | solution.py:326
  145.5 1.3 collective-permute-done.27.c_ref
  146.8 5.8 %collective-permute-done.23.low_ref = f32[3,4,64,128]{3,2,1,0:T(8,128)S(1)} collective-permute-done((f32[3,4,64,128]{3,2,1,0:T(8,128)S(1)}, f32[3,4,64,128]{3,2,1,0:T(8,128)S(1)}, u32[]{:S(2)}, u32[]{:S(2)}) %collective-permute-start.23) | collective-permute-done | bytes 393248 | tf_op jit(solution)/shard_map/ppermute | solution.py:382
  (64 shorter events, 24.9 us)
Async XLA Ops:
  0.0 24.1 %collective-permute-start.1 = (f32[3,4,64,128]{3,2,1,0:T(8,128)}, f32[3,4,64,128]{3,2,1,0:T(8,128)S(1)}, u32[]{:S(2)}, u32[]{:S(2)}) collective-permute-start(f32[3,4,64,128]{3,2,1,0:T(8,128)} %bitcast.10), channel_id=1, source_target_pairs={{1,2},{2,1},{3,4},{4,3},{5,6},{6,5},{7,8},{8,7},{9,10},{10,9},{11,... | collective-permute-start | bytes 1179656 | tf_op jit(solution)/shard_map/ppermute | solution.py:414
  9.4 17.5 %collective-permute-start.2 = (f32[3,4,64,128]{3,2,1,0:T(8,128)}, f32[3,4,64,128]{3,2,1,0:T(8,128)S(1)}, u32[]{:S(2)}, u32[]{:S(2)}) collective-permute-start(f32[3,4,64,128]{3,2,1,0:T(8,128)} %bitcast.11), channel_id=1, source_target_pairs={{0,2},{2,4},{4,6},{6,8},{8,10},{10,12},{12,14},{14,16},{16,18},{18... | collective-permute-start | bytes 1179656 | tf_op jit(solution)/shard_map/ppermute | solution.py:415
  11.4 15.6 %collective-permute-start = (f32[3,4,64,128]{3,2,1,0:T(8,128)}, f32[3,4,64,128]{3,2,1,0:T(8,128)S(1)}, u32[]{:S(2)}, u32[]{:S(2)}) collective-permute-start(f32[3,4,64,128]{3,2,1,0:T(8,128)} %bitcast.12), channel_id=1, source_target_pairs={{0,1},{1,0},{2,3},{3,2},{4,5},{5,4},{6,7},{7,6},{8,9},{9,8},{10,11... | collective-permute-start | bytes 1179656 | tf_op jit(solution)/shard_map/ppermute | solution.py:416
  24.1 3.6 %collective-permute-start.3 = (f32[3,4,64,128]{3,2,1,0:T(8,128)S(1)}, f32[3,4,64,128]{3,2,1,0:T(8,128)S(1)}, u32[]{:S(2)}, u32[]{:S(2)}) collective-permute-start(f32[3,4,64,128]{3,2,1,0:T(8,128)S(1)} %collective-permute-done.1.near_ref), channel_id=1, source_target_pairs={{0,1},{1,0},{2,3},{3,2},{4,5},{5,4},{6,7},{7,6},{8,9},{9,8},{10,11... | collective-permute-start | bytes 1179656 | tf_op jit(solution)/shard_map/ppermute | solution.py:417
  27.7 1.0 copy-start
  28.7 30.7 %copy-start.1 = (f32[1,3,4,64,128]{4,3,2,1,0:T(8,128)S(1)}, f32[1,3,4,64,128]{4,3,2,1,0:T(8,128)}, u32[]{:S(2)}) copy-start(f32[1,3,4,64,128]{4,3,2,1,0:T(8,128)} %param.1) | copy-start | bytes 1179652
  34.9 22.4 %collective-permute-start.5 = (f32[3,4,64,128]{3,2,1,0:T(8,128)S(1)}, f32[3,4,64,128]{3,2,1,0:T(8,128)S(1)}, u32[]{:S(2)}, u32[]{:S(2)}) collective-permute-start(f32[3,4,64,128]{3,2,1,0:T(8,128)S(1)} %fine_steps.1.mid_ref), channel_id=1, source_target_pairs={{1,2},{2,1},{3,4},{4,3},{5,6},{6,5},{7,8},{8,7},{9,10},{10,9},{11,... | collective-permute-start | bytes 1179656 | tf_op jit(solution)/shard_map/ppermute | solution.py:414
  41.7 20.6 %collective-permute-start.6 = (f32[3,4,64,128]{3,2,1,0:T(8,128)S(1)}, f32[3,4,64,128]{3,2,1,0:T(8,128)S(1)}, u32[]{:S(2)}, u32[]{:S(2)}) collective-permute-start(f32[3,4,64,128]{3,2,1,0:T(8,128)S(1)} %fine_steps.1.mid_ref), channel_id=1, source_target_pairs={{0,2},{2,4},{4,6},{6,8},{8,10},{10,12},{12,14},{14,16},{16,18},{18... | collective-permute-start | bytes 1179656 | tf_op jit(solution)/shard_map/ppermute | solution.py:415
  43.6 18.6 %collective-permute-start.4 = (f32[3,4,64,128]{3,2,1,0:T(8,128)S(1)}, f32[3,4,64,128]{3,2,1,0:T(8,128)S(1)}, u32[]{:S(2)}, u32[]{:S(2)}) collective-permute-start(f32[3,4,64,128]{3,2,1,0:T(8,128)S(1)} %fine_steps.1.mid_ref), channel_id=1, source_target_pairs={{0,1},{1,0},{2,3},{3,2},{4,5},{5,4},{6,7},{7,6},{8,9},{9,8},{10,11... | collective-permute-start | bytes 1179656 | tf_op jit(solution)/shard_map/ppermute | solution.py:416
  57.2 5.0 %collective-permute-start.7 = (f32[3,4,64,128]{3,2,1,0:T(8,128)S(1)}, f32[3,4,64,128]{3,2,1,0:T(8,128)S(1)}, u32[]{:S(2)}, u32[]{:S(2)}) collective-permute-start(f32[3,4,64,128]{3,2,1,0:T(8,128)S(1)} %collective-permute-done.5.near_ref), channel_id=1, source_target_pairs={{0,1},{1,0},{2,3},{3,2},{4,5},{5,4},{6,7},{7,6},{8,9},{9,8},{10,11... | collective-permute-start | bytes 1179656 | tf_op jit(solution)/shard_map/ppermute | solution.py:417
  70.6 9.5 %collective-permute-start.8 = (f32[3,4,16,128]{3,2,1,0:T(8,128)S(1)}, f32[3,4,16,128]{3,2,1,0:T(8,128)S(1)}, u32[]{:S(2)}, u32[]{:S(2)}) collective-permute-start(f32[3,4,16,128]{3,2,1,0:T(8,128)S(1)} %pad_maximum_fusion.3), channel_id=1, source_target_pairs={{0,66},{2,68},{3,65},{4,70},{5,67},{6,72},{7,69},{8,74},{9,71},{10... | collective-permute-start | bytes 294920 | tf_op jit(solution)/shard_map/ppermute | solution.py:382
  72.5 10.3 %collective-permute-start.12 = (f32[3,2,16,128]{3,2,1,0:T(8,128)S(1)}, f32[3,2,16,128]{3,2,1,0:T(8,128)S(1)}, u32[]{:S(2)}, u32[]{:S(2)}) collective-permute-start(f32[3,2,16,128]{3,2,1,0:T(8,128)S(1)} %get-tuple-element.33), channel_id=1, source_target_pairs={{32,64},{33,65},{34,66},{35,67},{36,68},{37,69},{38,70},{39,71},{4... | collective-permute-start | bytes 147464 | tf_op jit(solution)/shard_map/ppermute | solution.py:382
  73.2 9.6 %collective-permute-start.11 = (f32[3,2,16,128]{3,2,1,0:T(8,128)S(1)}, f32[3,2,16,128]{3,2,1,0:T(8,128)S(1)}, u32[]{:S(2)}, u32[]{:S(2)}) collective-permute-start(f32[3,2,16,128]{3,2,1,0:T(8,128)S(1)} %get-tuple-element.33), channel_id=1, source_target_pairs={{0,64},{1,65},{2,66},{3,67},{4,68},{5,69},{6,70},{7,71},{8,72},{9,... | collective-permute-start | bytes 147464 | tf_op jit(solution)/shard_map/ppermute | solution.py:382
  74.5 7.0 %collective-permute-start.9 = (f32[3,2,16,128]{3,2,1,0:T(8,128)S(1)}, f32[3,2,16,128]{3,2,1,0:T(8,128)S(1)}, u32[]{:S(2)}, u32[]{:S(2)}) collective-permute-start(f32[3,2,16,128]{3,2,1,0:T(8,128)S(1)} %get-tuple-element.61), channel_id=1, source_target_pairs={{32,66},{34,68},{35,65},{36,70},{37,67},{38,72},{39,69},{40,74},{4... | collective-permute-start | bytes 147464 | tf_op jit(solution)/shard_map/ppermute | solution.py:382
  80.1 15.3 %collective-permute-start.13 = (f32[3,4,16,128]{3,2,1,0:T(8,128)S(1)}, f32[3,4,16,128]{3,2,1,0:T(8,128)S(1)}, u32[]{:S(2)}, u32[]{:S(2)}) collective-permute-start(f32[3,4,16,128]{3,2,1,0:T(8,128)S(1)} %pad_maximum_fusion.4), channel_id=1, source_target_pairs={{160,128},{161,129},{162,130},{163,131},{164,132},{165,133},{166,1... | collective-permute-start | bytes 294920 | tf_op jit(solution)/shard_map/ppermute | solution.py:382
  81.5 13.9 %collective-permute-start.10 = (f32[3,8,16,128]{3,2,1,0:T(8,128)S(1)}, f32[3,8,16,128]{3,2,1,0:T(8,128)S(1)}, u32[]{:S(2)}, u32[]{:S(2)}) collective-permute-start(f32[3,8,16,128]{3,2,1,0:T(8,128)S(1)} %constant_dynamic-update-slice_fusion), channel_id=1, source_target_pairs={{96,128},{97,129},{98,130},{99,131},{100,132},{101,133},{102,134},... | collective-permute-start | bytes 589832 | tf_op jit(solution)/shard_map/ppermute | solution.py:382
  85.8 13.8 %collective-permute-start.15 = (f32[3,4,16,128]{3,2,1,0:T(8,128)S(1)}, f32[3,4,16,128]{3,2,1,0:T(8,128)S(1)}, u32[]{:S(2)}, u32[]{:S(2)}) collective-permute-start(f32[3,4,16,128]{3,2,1,0:T(8,128)S(1)} %get-tuple-element.35), channel_id=1, source_target_pairs={{64,132},{66,134},{68,136},{69,129},{70,138},{71,131},{72,140},{73... | collective-permute-start | bytes 294920 | tf_op jit(solution)/shard_map/ppermute | solution.py:382
  86.5 13.1 %collective-permute-start.14 = (f32[3,4,16,128]{3,2,1,0:T(8,128)S(1)}, f32[3,4,16,128]{3,2,1,0:T(8,128)S(1)}, u32[]{:S(2)}, u32[]{:S(2)}) collective-permute-start(f32[3,4,16,128]{3,2,1,0:T(8,128)S(1)} %get-tuple-element.35), channel_id=1, source_target_pairs={{64,130},{66,132},{67,129},{68,134},{69,131},{70,136},{71,133},{72... | collective-permute-start | bytes 294920 | tf_op jit(solution)/shard_map/ppermute | solution.py:382
  87.1 12.5 %collective-permute-start.16 = (f32[3,2,16,128]{3,2,1,0:T(8,128)S(1)}, f32[3,2,16,128]{3,2,1,0:T(8,128)S(1)}, u32[]{:S(2)}, u32[]{:S(2)}) collective-permute-start(f32[3,2,16,128]{3,2,1,0:T(8,128)S(1)} %get-tuple-element.39), channel_id=1, source_target_pairs={{64,128},{65,129},{66,130},{67,131},{68,132},{69,133},{70,134},{71... | collective-permute-start | bytes 147464 | tf_op jit(solution)/shard_map/ppermute | solution.py:382
  103.6 19.9 %collective-permute-start.18 = (f32[3,4,16,128]{3,2,1,0:T(8,128)S(1)}, f32[3,4,16,128]{3,2,1,0:T(8,128)S(1)}, u32[]{:S(2)}, u32[]{:S(2)}) collective-permute-start(f32[3,4,16,128]{3,2,1,0:T(8,128)S(1)} %get-tuple-element.42), channel_id=1, source_target_pairs={{128,260},{130,262},{132,264},{133,257},{134,266},{135,259},{136,2... | collective-permute-start | bytes 294920 | tf_op jit(solution)/shard_map/ppermute | solution.py:382
  104.9 18.6 %collective-permute-start.17 = (f32[3,4,16,128]{3,2,1,0:T(8,128)S(1)}, f32[3,4,16,128]{3,2,1,0:T(8,128)S(1)}, u32[]{:S(2)}, u32[]{:S(2)}) collective-permute-start(f32[3,4,16,128]{3,2,1,0:T(8,128)S(1)} %get-tuple-element.42), channel_id=1, source_target_pairs={{128,258},{130,260},{131,257},{132,262},{133,259},{134,264},{135,2... | collective-permute-start | bytes 294920 | tf_op jit(solution)/shard_map/ppermute | solution.py:382
  106.2 16.2 %collective-permute-start.19 = (f32[3,2,16,128]{3,2,1,0:T(8,128)S(1)}, f32[3,2,16,128]{3,2,1,0:T(8,128)S(1)}, u32[]{:S(2)}, u32[]{:S(2)}) collective-permute-start(f32[3,2,16,128]{3,2,1,0:T(8,128)S(1)} %get-tuple-element.43), channel_id=1, source_target_pairs={{128,256},{129,257},{130,258},{131,259},{132,260},{133,261},{134,2... | collective-permute-start | bytes 147464 | tf_op jit(solution)/shard_map/ppermute | solution.py:382
  127.7 7.6 %collective-permute-start.21 = (f32[3,4,16,128]{3,2,1,0:T(8,128)S(1)}, f32[3,4,16,128]{3,2,1,0:T(8,128)S(1)}, u32[]{:S(2)}, u32[]{:S(2)}) collective-permute-start(f32[3,4,16,128]{3,2,1,0:T(8,128)S(1)} %get-tuple-element.48), channel_id=1, source_target_pairs={{256,388},{258,390},{260,392},{261,385},{262,394},{263,387},{264,3... | collective-permute-start | bytes 294920 | tf_op jit(solution)/shard_map/ppermute | solution.py:382
  129.0 6.3 %collective-permute-start.20 = (f32[3,4,16,128]{3,2,1,0:T(8,128)S(1)}, f32[3,4,16,128]{3,2,1,0:T(8,128)S(1)}, u32[]{:S(2)}, u32[]{:S(2)}) collective-permute-start(f32[3,4,16,128]{3,2,1,0:T(8,128)S(1)} %get-tuple-element.48), channel_id=1, source_target_pairs={{256,386},{258,388},{259,385},{260,390},{261,387},{262,392},{263,3... | collective-permute-start | bytes 294920 | tf_op jit(solution)/shard_map/ppermute | solution.py:382
  130.3 5.0 %collective-permute-start.22 = (f32[3,2,16,128]{3,2,1,0:T(8,128)S(1)}, f32[3,2,16,128]{3,2,1,0:T(8,128)S(1)}, u32[]{:S(2)}, u32[]{:S(2)}) collective-permute-start(f32[3,2,16,128]{3,2,1,0:T(8,128)S(1)} %get-tuple-element.49), channel_id=1, source_target_pairs={{256,384},{257,385},{258,386},{259,387},{260,388},{261,389},{262,3... | collective-permute-start | bytes 147464 | tf_op jit(solution)/shard_map/ppermute | solution.py:382
  132.0 14.8 %collective-permute-start.24 = (f32[3,4,64,128]{3,2,1,0:T(8,128)S(1)}, f32[3,4,64,128]{3,2,1,0:T(8,128)S(1)}, u32[]{:S(2)}, u32[]{:S(2)}) collective-permute-start(f32[3,4,64,128]{3,2,1,0:T(8,128)S(1)} %fine_change.1), channel_id=1, source_target_pairs={{256,288},{257,289},{258,290},{259,291},{260,292},{261,293},{262,2... | collective-permute-start | bytes 1179656 | tf_op jit(solution)/shard_map/ppermute | solution.py:382
  137.4 15.1 %collective-permute-start.23 = (f32[3,4,64,128]{3,2,1,0:T(8,128)S(1)}, f32[3,4,64,128]{3,2,1,0:T(8,128)S(1)}, u32[]{:S(2)}, u32[]{:S(2)}) collective-permute-start(f32[3,4,64,128]{3,2,1,0:T(8,128)S(1)} %fine_change.1), channel_id=1, source_target_pairs={{0,32},{1,33},{2,34},{3,35},{4,36},{5,37},{6,38},{7,39},{8,40},{9,... | collective-permute-start | bytes 1179656 | tf_op jit(solution)/shard_map/ppermute | solution.py:382
  141.1 3.9 %collective-permute-start.25 = (f32[3,2,16,128]{3,2,1,0:T(8,128)S(1)}, f32[3,2,16,128]{3,2,1,0:T(8,128)S(1)}, u32[]{:S(2)}, u32[]{:S(2)}) collective-permute-start(f32[3,2,16,128]{3,2,1,0:T(8,128)S(1)} %get-tuple-element.56), channel_id=1, source_target_pairs={{0,32},{1,33},{2,34},{3,35},{4,36},{5,37},{6,38},{7,39},{8,40},{9,... | collective-permute-start | bytes 147464 | tf_op jit(solution)/shard_map/ppermute | solution.py:382
  142.4 3.0 %collective-permute-start.26 = (f32[3,2,16,128]{3,2,1,0:T(8,128)S(1)}, f32[3,2,16,128]{3,2,1,0:T(8,128)S(1)}, u32[]{:S(2)}, u32[]{:S(2)}) collective-permute-start(f32[3,2,16,128]{3,2,1,0:T(8,128)S(1)} %get-tuple-element.57), channel_id=1, source_target_pairs={{128,192},{129,193},{130,194},{131,195},{132,196},{133,197},{134,1... | collective-permute-start | bytes 147464 | tf_op jit(solution)/shard_map/ppermute | solution.py:382
  143.7 3.0 %collective-permute-start.27 = (f32[3,2,16,128]{3,2,1,0:T(8,128)S(1)}, f32[3,2,16,128]{3,2,1,0:T(8,128)S(1)}, u32[]{:S(2)}, u32[]{:S(2)}) collective-permute-start(f32[3,2,16,128]{3,2,1,0:T(8,128)S(1)} %get-tuple-element.58), channel_id=1, source_target_pairs={{128,224},{129,225},{130,226},{131,227},{132,228},{133,229},{134,2... | collective-permute-start | bytes 147464 | tf_op jit(solution)/shard_map/ppermute | solution.py:382
